TPU v7x, 32 devices: a whole 2x2x4 slice. The times are simulated.
32 devices in a mesh: dp: 2 (over y), expert: 16 (over z, x, core).
Axes of the slice: x: 2, y: 2, z: 4, core: 2. Of those that a mesh axis runs over, the one named last changes fastest.
Arguments:
- tokens: bfloat16 [4096, 2048], P(('dp', 'expert')), may hold values from -6 to 6
- lengths: int32 [64, 4], P(('dp', 'expert')), may hold values from 1 to 32, 64 in all within a row
- routes: int32 [4096, 6], P(('dp', 'expert')), may hold values from 0 to 15, all different within a row; in each aligned block of 64 rows (0 to 63, 64 to 127, ...) at most 32 rows name the same one
- gates: float32 [4096, 6], P(('dp', 'expert')), may hold values from 0.25 to 1
- norm_in: bfloat16 [2048], P(('dp', 'expert')), may hold values from 0.25 to 1.75
- latent_gain: bfloat16 [512], P(('dp', 'expert')), may hold values from 0.25 to 1.75
- norm_mid: bfloat16 [2048], P(('dp', 'expert')), may hold values from 0.25 to 1.75
- w_query: bfloat16 [2048, 3072], P(('dp', 'expert')), may hold values from -0.125 to 0.125
- w_latent: bfloat16 [2048, 576], P(('dp', 'expert')), may hold values from -0.125 to 0.125
- w_expand: bfloat16 [512, 4096], P(('dp', 'expert')), may hold values from -0.25 to 0.25
- w_output: bfloat16 [2048, 2048], P(None, ('dp', 'expert')), may hold values from -0.375 to 0.375
- shared_gate: bfloat16 [2048, 2816], P(('dp', 'expert')), may hold values from -0.125 to 0.125
- shared_up: bfloat16 [2048, 2816], P(('dp', 'expert')), may hold values from -0.125 to 0.125
- shared_down: bfloat16 [2816, 2048], P(None, ('dp', 'expert')), may hold values from -0.109375 to 0.109375
- expert_gate: bfloat16 [16, 2048, 1408], P('expert', 'dp'), may hold values from -0.125 to 0.125
- expert_up: bfloat16 [16, 2048, 1408], P('expert', 'dp'), may hold values from -0.125 to 0.125
- expert_down: bfloat16 [16, 1408, 2048], P('expert', None, 'dp'), may hold values from -0.15625 to 0.15625
- cotangent: float32 [4096, 2048], P(('dp', 'expert')), may hold values from -6 to 6
Outputs:
- out: bfloat16 [4096, 2048], P(('dp', 'expert'))
- d_tokens: float32 [4096, 2048], P(('dp', 'expert'))
- d_norm_in: float32 [2048], P(('dp', 'expert'))
- d_latent_gain: float32 [512], P(('dp', 'expert'))
- d_norm_mid: float32 [2048], P(('dp', 'expert'))
- d_w_query: float32 [2048, 3072], P(('dp', 'expert'))
- d_w_latent: float32 [2048, 576], P(('dp', 'expert'))
- d_w_expand: float32 [512, 4096], P(('dp', 'expert'))
- d_w_output: float32 [2048, 2048], P(None, ('dp', 'expert'))
- d_shared_gate: float32 [2048, 2816], P(('dp', 'expert'))
- d_shared_up: float32 [2048, 2816], P(('dp', 'expert'))
- d_shared_down: float32 [2816, 2048], P(None, ('dp', 'expert'))
- d_expert_gate: float32 [16, 2048, 1408], P('expert', 'dp')
- d_expert_up: float32 [16, 2048, 1408], P('expert', 'dp')
- d_expert_down: float32 [16, 1408, 2048], P('expert', None, 'dp')
Inputs may be any that keep to these rules, and one draw needn't show every extreme that they name: `routes`: each row names 6 different experts; in each aligned block of 64 rows (one micro-batch of one device) no expert is named by more than 32 rows, a bound that some block reaches. `lengths`: each row sums to 64; its longest sequence has exactly 32 tokens.
All inputs are finite; a program needn't handle non-finite values.
Results may differ from a plain program's by a relative error of at most 0.019.
Values may be sent and summed in bfloat16 or wider, within the bound.
No kernel may reach another device: no remote copies, remote signals or barrier semaphores. Data moves between devices by JAX's collectives and lax.ppermute only.
A program may use at most 448 MiB of HBM per device.

v0:
```python
import jax
import jax.numpy as jnp
from jax import lax
from jax.sharding import PartitionSpec as P

HEADS = 16
HD = 128
RD = 64
VD = 128
LAT = 512
TOP = 6


EPS = 1e-06


def matmul(left, right):
    return jnp.dot(left, right, preferred_element_type=jnp.float32)


def mat_trans(left, right):
    return lax.dot_general(
        left, right, (((1,), (1,)), ((), ())), preferred_element_type=jnp.float32
    )


def contract(left, right):
    return lax.dot_general(
        left, right, (((0,), (0,)), ((), ())), preferred_element_type=jnp.float32
    )


def rms_scale(values):
    return lax.rsqrt(jnp.mean(values * values, axis=-1, keepdims=True) + EPS)


def rms_back(incoming, values, scale, gain):
    scaled = incoming * gain
    inner = jnp.mean(scaled * values, axis=-1, keepdims=True)
    grad_in = scale * (scaled - values * scale * scale * inner)
    grad_gain = jnp.sum(incoming * values * scale, axis=0)
    return (grad_in, grad_gain)


def swish_parts(gate_pre):
    sigma = jax.nn.sigmoid(gate_pre)
    return (gate_pre * sigma, sigma * (1.0 + gate_pre * (1.0 - sigma)))


def layout(lengths, rows):
    ends = jnp.cumsum(lengths, axis=-1)
    place = jnp.arange(rows, dtype=jnp.int32)
    passed = (place[None, :, None] >= ends[:, None, :]).astype(jnp.int32)
    doc = jnp.sum(passed, axis=-1)
    start = jnp.sum(passed * lengths[:, None, :], axis=-1)
    return ((place[None, :] - start).astype(jnp.float32), doc)


def angles(position, size):
    freq = jnp.power(10000.0, -2.0 * jnp.arange(size // 2, dtype=jnp.float32) / size)
    theta = position[..., None] * freq
    return (jnp.cos(theta), jnp.sin(theta))


def rotate(values, cosine, sine):
    half = values.shape[-1] // 2
    first, second = (values[..., :half], values[..., half:])
    return jnp.concatenate(
        [first * cosine - second * sine, second * cosine + first * sine], axis=-1
    )


def unrotate(values, cosine, sine):
    half = values.shape[-1] // 2
    first, second = (values[..., :half], values[..., half:])
    return jnp.concatenate(
        [first * cosine + second * sine, second * cosine - first * sine], axis=-1
    )


def local(
    tokens,
    lengths,
    routes,
    gates,
    norm_in,
    latent_gain,
    norm_mid,
    w_query,
    w_latent,
    w_expand,
    w_output,
    shared_gate,
    shared_up,
    shared_down,
    expert_gate,
    expert_up,
    expert_down,
    cotangent,
):
    micro = lengths.shape[0]
    rows = tokens.shape[0] // micro
    width = tokens.shape[1]
    flat_rows = micro * rows
    experts = lax.axis_size("expert")
    cap = rows * TOP * 4 // (3 * experts)
    score_scale = (HD + RD) ** (-0.5)
    dense = (
        lax.all_gather(w_query, ("dp", "expert"), axis=0, tiled=True),
        lax.all_gather(w_latent, ("dp", "expert"), axis=0, tiled=True),
        lax.all_gather(w_expand, ("dp", "expert"), axis=0, tiled=True),
        lax.all_gather(w_output, ("dp", "expert"), axis=1, tiled=True),
        lax.all_gather(norm_in, ("dp", "expert"), axis=0, tiled=True),
        lax.all_gather(latent_gain, ("dp", "expert"), axis=0, tiled=True),
        lax.all_gather(norm_mid, ("dp", "expert"), axis=0, tiled=True),
        lax.all_gather(shared_gate, ("dp", "expert"), axis=0, tiled=True),
        lax.all_gather(shared_up, ("dp", "expert"), axis=0, tiled=True),
        lax.all_gather(shared_down, ("dp", "expert"), axis=1, tiled=True),
    )
    q_w, lat_w, exp_w, out_w = (dense[0], dense[1], dense[2], dense[3])
    gain_in = dense[4].astype(jnp.float32)
    gain_lat = dense[5].astype(jnp.float32)
    gain_mid = dense[6].astype(jnp.float32)
    held = (
        lax.all_gather(expert_gate, "dp", axis=1, tiled=True),
        lax.all_gather(expert_up, "dp", axis=1, tiled=True),
        lax.all_gather(expert_down, "dp", axis=2, tiled=True),
    )
    eg_w, eu_w, ed_w = (held[0][0], held[1][0], held[2][0])
    position, doc = layout(lengths, rows)
    place = jnp.arange(rows, dtype=jnp.int32)
    same_seq = (doc[:, :, None] == doc[:, None, :]) & (place[None, None, :] <= place[None, :, None])
    cosine, sine = angles(position, RD)
    cos_heads = cosine[:, :, None, :]
    sin_heads = sine[:, :, None, :]
    xf = tokens.astype(jnp.float32)
    scale_in = rms_scale(xf)
    normed = (xf * scale_in * gain_in).astype(jnp.bfloat16)
    query = matmul(normed, q_w).reshape(micro, rows, HEADS, HD + RD)
    latent = matmul(normed, lat_w)
    lat_part = latent[:, :LAT]
    scale_lat = rms_scale(lat_part)
    compressed = (lat_part * scale_lat * gain_lat).astype(jnp.bfloat16)
    expanded = matmul(compressed, exp_w).reshape(micro, rows, HEADS, HD + VD)
    q_all = jnp.concatenate(
        [query[..., :HD], rotate(query[..., HD:], cos_heads, sin_heads)], axis=-1
    ).astype(jnp.bfloat16)
    key_rot = rotate(latent[:, LAT:].reshape(micro, rows, RD), cosine, sine)
    k_all = jnp.concatenate(
        [expanded[..., :HD], jnp.broadcast_to(key_rot[:, :, None, :], (micro, rows, HEADS, RD))],
        axis=-1,
    ).astype(jnp.bfloat16)
    values = expanded[..., HD:].astype(jnp.bfloat16)
    scores = (
        jnp.einsum("mqhd,mkhd->mhqk", q_all, k_all, preferred_element_type=jnp.float32)
        * score_scale
    )
    scores = jnp.where(same_seq[:, None], scores, -1e30)
    expo = jnp.exp(scores - jnp.max(scores, axis=-1, keepdims=True))
    probs = expo / jnp.sum(expo, axis=-1, keepdims=True)
    prob_low = probs.astype(jnp.bfloat16)
    attended = jnp.einsum("mhqk,mkhd->mqhd", prob_low, values, preferred_element_type=jnp.float32)
    attended = attended.astype(jnp.bfloat16).reshape(flat_rows, HEADS * VD)
    mid = xf + matmul(attended, out_w)
    scale_mid = rms_scale(mid)
    normed_mid = (mid * scale_mid * gain_mid).astype(jnp.bfloat16)
    sg_w, su_w, sd_w = (dense[7], dense[8], dense[9])
    s_gate = matmul(normed_mid, sg_w)
    s_up = matmul(normed_mid, su_w)
    s_swish, s_slope = swish_parts(s_gate)
    s_act = (s_swish * s_up).astype(jnp.bfloat16)
    shared_out = matmul(s_act, sd_w)
    route_flat = routes.reshape(micro, rows * TOP)
    hot = (route_flat[:, :, None] == jnp.arange(experts, dtype=jnp.int32)[None, None, :]).astype(
        jnp.int32
    )
    slot = jnp.sum(hot * (jnp.cumsum(hot, axis=1) - 1), axis=2)
    target = route_flat * cap + slot
    dispatch = (
        jnp.arange(experts * cap, dtype=jnp.int32)[None, :, None] == target[:, None, :]
    ).astype(jnp.bfloat16)
    by_token = jnp.sum(dispatch.reshape(micro, experts * cap, rows, TOP), axis=3)
    mid_blocks = normed_mid.reshape(micro, rows, width)
    outgoing = jnp.einsum("mjt,mtd->mjd", by_token, mid_blocks, preferred_element_type=jnp.float32)
    outgoing = outgoing.astype(jnp.bfloat16).reshape(micro, experts, cap, width)
    arrived = lax.all_to_all(outgoing, "expert", split_axis=1, concat_axis=1, tiled=True)
    expert_rows = arrived.reshape(micro * experts * cap, width)
    e_gate = matmul(expert_rows, eg_w)
    e_up = matmul(expert_rows, eu_w)
    e_swish, e_slope = swish_parts(e_gate)
    e_act = (e_swish * e_up).astype(jnp.bfloat16)
    e_out = matmul(e_act, ed_w).astype(jnp.bfloat16).reshape(micro, experts, cap, width)
    returned = lax.all_to_all(e_out, "expert", split_axis=1, concat_axis=1, tiled=True).reshape(
        micro, experts * cap, width
    )
    picked = returned[jnp.arange(micro, dtype=jnp.int32)[:, None], target].reshape(
        micro, rows, TOP, width
    )
    gate_four = gates.reshape(micro, rows, TOP, 1)
    routed = jnp.sum(gate_four * picked.astype(jnp.float32), axis=2).reshape(flat_rows, width)
    out = (mid + shared_out + routed).astype(jnp.bfloat16)
    grad_low = cotangent.astype(jnp.bfloat16)
    d_sd = contract(s_act, grad_low)
    d_s_act = mat_trans(grad_low, sd_w)
    d_sg_pre = (d_s_act * s_up * s_slope).astype(jnp.bfloat16)
    d_su_pre = (d_s_act * s_swish).astype(jnp.bfloat16)
    d_sg = contract(normed_mid, d_sg_pre)
    d_su = contract(normed_mid, d_su_pre)
    d_mid_normed = mat_trans(d_sg_pre, sg_w) + mat_trans(d_su_pre, su_w)
    grad_route = (gate_four * cotangent.reshape(micro, rows, 1, width)).astype(jnp.bfloat16)
    grad_route = grad_route.reshape(micro, rows * TOP, width)
    to_slots = jnp.einsum("mjr,mrd->mjd", dispatch, grad_route, preferred_element_type=jnp.float32)
    to_slots = to_slots.astype(jnp.bfloat16).reshape(micro, experts, cap, width)
    grad_arrived = lax.all_to_all(
        to_slots, "expert", split_axis=1, concat_axis=1, tiled=True
    ).reshape(micro * experts * cap, width)
    d_e_act = mat_trans(grad_arrived, ed_w)
    d_ed = contract(e_act, grad_arrived)
    d_eg_pre = (d_e_act * e_up * e_slope).astype(jnp.bfloat16)
    d_eu_pre = (d_e_act * e_swish).astype(jnp.bfloat16)
    d_eg = contract(expert_rows, d_eg_pre)
    d_eu = contract(expert_rows, d_eu_pre)
    d_rows = (mat_trans(d_eg_pre, eg_w) + mat_trans(d_eu_pre, eu_w)).astype(jnp.bfloat16)
    d_rows = d_rows.reshape(micro, experts, cap, width)
    d_returned = lax.all_to_all(d_rows, "expert", split_axis=1, concat_axis=1, tiled=True).reshape(
        micro, experts * cap, width
    )
    d_routed = jnp.einsum("mjt,mjd->mtd", by_token, d_returned, preferred_element_type=jnp.float32)
    d_mid_normed = d_mid_normed + d_routed.reshape(flat_rows, width)
    d_mid_in, d_gain_mid = rms_back(d_mid_normed, mid, scale_mid, gain_mid)
    d_mid = cotangent + d_mid_in
    grad_attn = d_mid.astype(jnp.bfloat16)
    d_wo = contract(attended, grad_attn)
    d_att = mat_trans(grad_attn, out_w).astype(jnp.bfloat16).reshape(micro, rows, HEADS, VD)
    d_prob = jnp.einsum("mqhd,mkhd->mhqk", d_att, values, preferred_element_type=jnp.float32)
    d_values = jnp.einsum("mhqk,mqhd->mkhd", prob_low, d_att, preferred_element_type=jnp.float32)
    d_scores = (probs * (d_prob - jnp.sum(probs * d_prob, axis=-1, keepdims=True))).astype(
        jnp.bfloat16
    )
    d_q = (
        jnp.einsum("mhqk,mkhd->mqhd", d_scores, k_all, preferred_element_type=jnp.float32)
        * score_scale
    )
    d_k = (
        jnp.einsum("mhqk,mqhd->mkhd", d_scores, q_all, preferred_element_type=jnp.float32)
        * score_scale
    )
    d_query = jnp.concatenate(
        [d_q[..., :HD], unrotate(d_q[..., HD:], cos_heads, sin_heads)], axis=-1
    )
    d_query = d_query.astype(jnp.bfloat16).reshape(flat_rows, HEADS * (HD + RD))
    d_key_rot = unrotate(jnp.sum(d_k[..., HD:], axis=2), cosine, sine).reshape(flat_rows, RD)
    d_expanded = jnp.concatenate([d_k[..., :HD], d_values], axis=-1)
    d_expanded = d_expanded.astype(jnp.bfloat16).reshape(flat_rows, HEADS * (HD + VD))
    d_wkvb = contract(compressed, d_expanded)
    d_compressed = mat_trans(d_expanded, exp_w)
    d_lat_part, d_gain_lat = rms_back(d_compressed, lat_part, scale_lat, gain_lat)
    d_latent = jnp.concatenate([d_lat_part, d_key_rot], axis=-1).astype(jnp.bfloat16)
    d_wq = contract(normed, d_query)
    d_wkva = contract(normed, d_latent)
    d_normed = mat_trans(d_query, q_w) + mat_trans(d_latent, lat_w)
    d_in, d_gain_in = rms_back(d_normed, xf, scale_in, gain_in)
    d_tokens = d_mid + d_in
    summed = (
        lax.psum_scatter(d_wq, ("dp", "expert"), scatter_dimension=0, tiled=True),
        lax.psum_scatter(d_wkva, ("dp", "expert"), scatter_dimension=0, tiled=True),
        lax.psum_scatter(d_wkvb, ("dp", "expert"), scatter_dimension=0, tiled=True),
        lax.psum_scatter(d_wo, ("dp", "expert"), scatter_dimension=1, tiled=True),
        lax.psum_scatter(d_gain_in, ("dp", "expert"), scatter_dimension=0, tiled=True),
        lax.psum_scatter(d_gain_lat, ("dp", "expert"), scatter_dimension=0, tiled=True),
        lax.psum_scatter(d_gain_mid, ("dp", "expert"), scatter_dimension=0, tiled=True),
        lax.psum_scatter(d_sg, ("dp", "expert"), scatter_dimension=0, tiled=True),
        lax.psum_scatter(d_su, ("dp", "expert"), scatter_dimension=0, tiled=True),
        lax.psum_scatter(d_sd, ("dp", "expert"), scatter_dimension=1, tiled=True),
    )
    expert_sums = (
        lax.psum_scatter(d_eg.astype(jnp.bfloat16), "dp", scatter_dimension=0, tiled=True).astype(
            jnp.float32
        ),
        lax.psum_scatter(d_eu.astype(jnp.bfloat16), "dp", scatter_dimension=0, tiled=True).astype(
            jnp.float32
        ),
        lax.psum_scatter(d_ed.astype(jnp.bfloat16), "dp", scatter_dimension=1, tiled=True).astype(
            jnp.float32
        ),
    )
    grad_sg, grad_su, grad_sd = (summed[7], summed[8], summed[9])
    return (
        out,
        d_tokens,
        summed[4],
        summed[5],
        summed[6],
        summed[0],
        summed[1],
        summed[2],
        summed[3],
        grad_sg,
        grad_su,
        grad_sd,
        expert_sums[0][None],
        expert_sums[1][None],
        expert_sums[2][None],
    )


def solution(mesh):
    return jax.shard_map(
        local,
        mesh=mesh,
        in_specs=(
            P(("dp", "expert"), None),
            P(("dp", "expert"), None),
            P(("dp", "expert"), None),
            P(("dp", "expert"), None),
            P(("dp", "expert")),
            P(("dp", "expert")),
            P(("dp", "expert")),
            P(("dp", "expert"), None),
            P(("dp", "expert"), None),
            P(("dp", "expert"), None),
            P(None, ("dp", "expert")),
            P(("dp", "expert"), None),
            P(("dp", "expert"), None),
            P(None, ("dp", "expert")),
            P("expert", "dp", None),
            P("expert", "dp", None),
            P("expert", None, "dp"),
            P(("dp", "expert"), None),
        ),
        out_specs=(
            P(("dp", "expert"), None),
            P(("dp", "expert"), None),
            P(("dp", "expert")),
            P(("dp", "expert")),
            P(("dp", "expert")),
            P(("dp", "expert"), None),
            P(("dp", "expert"), None),
            P(("dp", "expert"), None),
            P(None, ("dp", "expert")),
            P(("dp", "expert"), None),
            P(("dp", "expert"), None),
            P(None, ("dp", "expert")),
            P("expert", "dp", None),
            P("expert", "dp", None),
            P("expert", None, "dp"),
        ),
        check_vma=False,
    )
```

profile of v0, /device:TPU:0, one launch (start us, length us, event | category | flops | bytes accessed | tf_op | source)
XLA Modules:
  0.0 2635.3 jit_solution(10506896324074197632)
XLA Ops:
  34.2 126.1 %all-reduce.7 = (bf16[2048]{0:T(1024)(128)(2,1)S(1)}, bf16[512]{0:T(512)(128)(2,1)S(1)}, bf16[2048]{0:T(1024)(128)(2,1)S(1)}) all-reduce(bf16[2048]{0:T(1024)(128)(2,1)S(1)} %dynamic-update-slice, bf16[512]{0:T(512)(128)(2,1)S(1)} %dynamic-update-slice.1, ...), channel_id=1, replica_groups=mesh['dp'=2,'expert'=16] {'dp','expert'}, use_global_device_ids=true, to_apply=%add | all-reduce | flops 4608 | bytes 18432
  165.3 17.5 all-gather.13.cloned.1.call-done
  187.3 93.0 %all-gather.15.cloned.1.call-done = bf16[2048,3072]{1,0:T(8,128)(2,1)} async-done(((bf16[64,3072]{1,0:T(8,128)(2,1)}), bf16[2048,3072]{1,0:T(8,128)(2,1)}) %all-gather.15.cloned.1.call-update) | async-done | bytes 12582928 | tf_op jit(solution)/shard_map/all_gather | solution.py:109
  296.8 62.0 %all-gather.17.cloned.1.call-done = bf16[2048,2048]{0,1:T(8,128)(2,1)} async-done(((bf16[2048,64]{0,1:T(8,128)(2,1)}), bf16[2048,2048]{0,1:T(8,128)(2,1)}) %all-gather.17.cloned.1.call-update) | async-done | bytes 8388624 | tf_op jit(solution)/shard_map/all_gather | solution.py:112
  378.5 54.7 %all-gather.29.cloned.1.call-done = bf16[1,1408,2048]{2,1,0:T(8,128)(2,1)} async-done(((bf16[1,1408,1024]{2,1,0:T(8,128)(2,1)}), bf16[1,1408,2048]{2,1,0:T(8,128)(2,1)}) %all-gather.29.cloned.1.call-update) | async-done | bytes 5767184 | tf_op jit(solution)/shard_map/all_gather | solution.py:127
  433.3 11.9 fusion.2
  455.9 53.2 %all-gather.27.cloned.1.call-done = bf16[1,2048,1408]{2,1,0:T(8,128)(2,1)} async-done(((bf16[1,1024,1408]{2,1,0:T(8,128)(2,1)}), bf16[1,2048,1408]{2,1,0:T(8,128)(2,1)}) %all-gather.27.cloned.1.call-update) | async-done | bytes 5767184 | tf_op jit(solution)/shard_map/all_gather | solution.py:126
  509.2 11.7 fusion.8
  520.9 64.4 %all-gather.25.cloned.1.call-done = bf16[1,2048,1408]{2,1,0:T(8,128)(2,1)} async-done(((bf16[1,1024,1408]{2,1,0:T(8,128)(2,1)}), bf16[1,2048,1408]{2,1,0:T(8,128)(2,1)}) %all-gather.25.cloned.1.call-update) | async-done | bytes 5767184 | tf_op jit(solution)/shard_map/all_gather | solution.py:125
  585.2 16.6 multiply_convert_fusion.1
  661.2 48.5 %all-gather.19.cloned.1.call-done = bf16[2048,2816]{1,0:T(8,128)(2,1)} async-done(((bf16[64,2816]{1,0:T(8,128)(2,1)}), bf16[2048,2816]{1,0:T(8,128)(2,1)}) %all-gather.19.cloned.1.call-update) | async-done | bytes 11534352 | tf_op jit(solution)/shard_map/all_gather | solution.py:116
  716.8 112.8 %all-gather.21.cloned.1.call-done = bf16[2048,2816]{1,0:T(8,128)(2,1)} async-done(((bf16[64,2816]{1,0:T(8,128)(2,1)}), bf16[2048,2816]{1,0:T(8,128)(2,1)}) %all-gather.21.cloned.1.call-update) | async-done | bytes 11534352 | tf_op jit(solution)/shard_map/all_gather | solution.py:117
  836.7 85.2 %all-gather.23.cloned.1.call-done = bf16[2816,2048]{0,1:T(8,128)(2,1)} async-done(((bf16[2816,64]{0,1:T(8,128)(2,1)}), bf16[2816,2048]{0,1:T(8,128)(2,1)}) %all-gather.23.cloned.1.call-update) | async-done | bytes 11534352 | tf_op jit(solution)/shard_map/all_gather | solution.py:118
  999.6 12.4 fusion.57
  1029.4 11.8 fusion.93
  1070.1 102.3 %all-reduce.6 = (f32[2048]{0:T(1024)S(1)}, f32[512]{0:T(512)S(1)}, f32[2048]{0:T(1024)S(1)}) all-reduce(f32[2048]{0:T(1024)S(1)} %get-tuple-element.17, f32[512]{0:T(512)S(1)} %get-tuple-element.19, f32[2048]{0:T(1024)S(1)} %get-tuple-element.15), channel_id=2, replica_groups=mesh['dp'=2,'expert'=16] {'dp','expert'}, use_global_device_ids=true, to_apply=%region_19.20.clone | all-reduce | flops 4608 | bytes 36864
  1178.4 14.6 gather_fusion
  1231.9 57.0 %reduce-scatter.13.cloned.1.call-done = f32[64,576]{1,0:T(8,128)} async-done(((f32[2048,576]{1,0:T(8,128)}), f32[64,576]{1,0:T(8,128)}) %reduce-scatter.13.cloned.1.call-update) | async-done | bytes 147472 | tf_op jit(solution)/shard_map/reduce_scatter | solution.py:266
  1288.9 147.7 %reduce-scatter.15.cloned.1.call-done = f32[16,4096]{1,0:T(8,128)} async-done(((f32[512,4096]{1,0:T(8,128)}), f32[16,4096]{1,0:T(8,128)}) %reduce-scatter.15.cloned.1.call-update) | async-done | bytes 262160 | tf_op jit(solution)/shard_map/reduce_scatter | solution.py:267
  1436.6 246.5 %reduce-scatter.19.cloned.1.call-done = f32[64,2816]{1,0:T(8,128)} async-done(((f32[2048,2816]{1,0:T(8,128)}), f32[64,2816]{1,0:T(8,128)}) %reduce-scatter.19.cloned.1.call-update) | async-done | bytes 720912 | tf_op jit(solution)/shard_map/reduce_scatter | solution.py:272
  1683.1 251.5 %reduce-scatter.21.cloned.1.call-done = f32[64,2816]{1,0:T(8,128)} async-done(((f32[2048,2816]{1,0:T(8,128)}), f32[64,2816]{1,0:T(8,128)}) %reduce-scatter.21.cloned.1.call-update) | async-done | bytes 720912 | tf_op jit(solution)/shard_map/reduce_scatter | solution.py:273
  1934.6 251.5 %reduce-scatter.23.cloned.1.call-done = f32[2816,64]{0,1:T(8,128)} async-done(((f32[2816,2048]{0,1:T(8,128)}), f32[2816,64]{0,1:T(8,128)}) %reduce-scatter.23.cloned.1.call-update) | async-done | bytes 720912 | tf_op jit(solution)/shard_map/reduce_scatter | solution.py:274
  2186.0 185.6 %reduce-scatter.17.cloned.1.call-done = f32[2048,64]{0,1:T(8,128)} async-done(((f32[2048,2048]{0,1:T(8,128)}), f32[2048,64]{0,1:T(8,128)}) %reduce-scatter.17.cloned.1.call-update) | async-done | bytes 524304 | tf_op jit(solution)/shard_map/reduce_scatter | solution.py:268
  2371.6 256.7 %reduce-scatter.11.cloned.1.call-done = f32[64,3072]{1,0:T(8,128)} async-done(((f32[2048,3072]{1,0:T(8,128)}), f32[64,3072]{1,0:T(8,128)}) %reduce-scatter.11.cloned.1.call-update) | async-done | bytes 786448 | tf_op jit(solution)/shard_map/reduce_scatter | solution.py:265
  (321 shorter events, 324.3 us)
Async XLA Ops:
  7.2 154.6 %all-gather.11.cloned.1.call-start = ((), (), s32[]{:S(2)}) async-start(), calls=%async_computation.14 | async-start | bytes 2703360 | tf_op jit(solution)/shard_map/all_gather | solution.py:110
  7.9 175.0 %all-gather.13.cloned.1.call-start = ((), (), s32[]{:S(2)}) async-start(), calls=%async_computation.15 | async-start | bytes 4325376 | tf_op jit(solution)/shard_map/all_gather | solution.py:111
  8.7 271.7 %all-gather.15.cloned.1.call-start = ((), (), s32[]{:S(2)}) async-start(), calls=%async_computation.16 | async-start | bytes 12976128 | tf_op jit(solution)/shard_map/all_gather | solution.py:109
  9.4 349.4 %all-gather.17.cloned.1.call-start = ((), (), s32[]{:S(2)}) async-start(), calls=%async_computation.17 | async-start | bytes 8650752 | tf_op jit(solution)/shard_map/all_gather | solution.py:112
  10.0 423.3 %all-gather.29.cloned.1.call-start = ((), (), s32[]{:S(2)}) async-start(), calls=%async_computation.23 | async-start | bytes 8650752 | tf_op jit(solution)/shard_map/all_gather | solution.py:127
  10.6 498.6 %all-gather.27.cloned.1.call-start = ((), (), s32[]{:S(2)}) async-start(), calls=%async_computation.22 | async-start | bytes 8650752 | tf_op jit(solution)/shard_map/all_gather | solution.py:126
  11.2 574.1 %all-gather.25.cloned.1.call-start = ((), (), s32[]{:S(2)}) async-start(), calls=%async_computation.21 | async-start | bytes 8650752 | tf_op jit(solution)/shard_map/all_gather | solution.py:125
  11.9 697.8 %all-gather.19.cloned.1.call-start = ((), (), s32[]{:S(2)}) async-start(), calls=%async_computation.18 | async-start | bytes 11894784 | tf_op jit(solution)/shard_map/all_gather | solution.py:116
  12.7 816.9 %all-gather.21.cloned.1.call-start = ((), (), s32[]{:S(2)}) async-start(), calls=%async_computation.19 | async-start | bytes 11894784 | tf_op jit(solution)/shard_map/all_gather | solution.py:117
  25.1 344.0 %all-to-all-start.2 = ((bf16[2,16,32,2048]{3,2,0,1:T(8,128)(2,1)}), bf16[2,16,32,2048]{3,2,0,1:T(8,128)(2,1)}, u32[]{:S(2)}, u32[]{:S(2)}) async-start(bf16[2,16,32,2048]{3,2,0,1:T(8,128)(2,1)} %copy.178), calls=%async_computation.2 | async-start | bytes 8388608 | tf_op jit(solution)/shard_map/all_to_all | solution.py:214
  32.6 889.2 %all-gather.23.cloned.1.call-start = ((), (), s32[]{:S(2)}) async-start(), calls=%async_computation.20 | async-start | bytes 11894784 | tf_op jit(solution)/shard_map/all_gather | solution.py:118
  369.1 82.2 %all-to-all-start = ((bf16[2,16,32,2048]{3,2,0,1:T(8,128)(2,1)}), bf16[2,16,32,2048]{3,2,0,1:T(8,128)(2,1)}, u32[]{:S(2)}, u32[]{:S(2)}) async-start(bf16[2,16,32,2048]{3,2,0,1:T(8,128)(2,1)} %copy.169), calls=%async_computation | async-start | bytes 8388608 | tf_op jit(solution)/shard_map/all_to_all | solution.py:186
  373.6 843.7 %reduce-scatter.27.cloned.1.call-start = ((), (), s32[]{:S(2)}) async-start(), calls=%async_computation.32 | async-start | bytes 8650752 | tf_op jit(solution)/shard_map/reduce_scatter | solution.py:280
  612.0 610.0 %reduce-scatter.25.cloned.1.call-start = ((), (), s32[]{:S(2)}) async-start(), calls=%async_computation.31 | async-start | bytes 8650752 | tf_op jit(solution)/shard_map/reduce_scatter | solution.py:277
  644.5 294.7 %all-to-all-start.3 = ((bf16[2,16,32,2048]{3,2,0,1:T(8,128)(2,1)}), bf16[2,16,32,2048]{3,2,0,1:T(8,128)(2,1)}, u32[]{:S(2)}, u32[]{:S(2)}) async-start(bf16[2,16,32,2048]{3,2,0,1:T(8,128)(2,1)} %copy.180), calls=%async_computation.3 | async-start | bytes 8388608 | tf_op jit(solution)/shard_map/all_to_all | solution.py:225
  650.1 576.7 %reduce-scatter.29.cloned.1.call-start = ((), (), s32[]{:S(2)}) async-start(), calls=%async_computation.33 | async-start | bytes 8650752 | tf_op jit(solution)/shard_map/reduce_scatter | solution.py:283
  660.7 628.2 %reduce-scatter.13.cloned.1.call-start = ((), (), s32[]{:S(2)}) async-start(), calls=%async_computation.25 | async-start | bytes 5406720 | tf_op jit(solution)/shard_map/reduce_scatter | solution.py:266
  972.2 464.4 %reduce-scatter.15.cloned.1.call-start = ((), (), s32[]{:S(2)}) async-start(), calls=%async_computation.26 | async-start | bytes 8650752 | tf_op jit(solution)/shard_map/reduce_scatter | solution.py:267
  978.2 704.9 %reduce-scatter.19.cloned.1.call-start = ((), (), s32[]{:S(2)}) async-start(), calls=%async_computation.28 | async-start | bytes 23789568 | tf_op jit(solution)/shard_map/reduce_scatter | solution.py:272
  988.9 945.6 %reduce-scatter.21.cloned.1.call-start = ((), (), s32[]{:S(2)}) async-start(), calls=%async_computation.29 | async-start | bytes 23789568 | tf_op jit(solution)/shard_map/reduce_scatter | solution.py:273
  999.6 1186.5 %reduce-scatter.23.cloned.1.call-start = ((), (), s32[]{:S(2)}) async-start(), calls=%async_computation.30 | async-start | bytes 23789568 | tf_op jit(solution)/shard_map/reduce_scatter | solution.py:274
  1012.0 1359.6 %reduce-scatter.17.cloned.1.call-start = ((), (), s32[]{:S(2)}) async-start(), calls=%async_computation.27 | async-start | bytes 17301504 | tf_op jit(solution)/shard_map/reduce_scatter | solution.py:268
  1021.3 1607.0 %reduce-scatter.11.cloned.1.call-start = ((), (), s32[]{:S(2)}) async-start(), calls=%async_computation.24 | async-start | bytes 25952256 | tf_op jit(solution)/shard_map/reduce_scatter | solution.py:265
  1053.2 120.4 %all-to-all-start.1 = ((bf16[2,16,32,2048]{3,2,0,1:T(8,128)(2,1)}), bf16[2,16,32,2048]{3,2,0,1:T(8,128)(2,1)}, u32[]{:S(2)}, u32[]{:S(2)}) async-start(bf16[2,16,32,2048]{3,2,0,1:T(8,128)(2,1)} %copy.171), calls=%async_computation.1 | async-start | bytes 8388608 | tf_op jit(solution)/shard_map/all_to_all | solution.py:193
  (67 other events, 1681.2 us)
Sparse Core Ops, SparseCore 0:
  10.9 98.6 all-gather.10
  112.5 70.3 all-gather.12
  185.8 94.5 all-gather.14
  283.0 75.7 all-gather.16
  360.2 73.0 all-gather.28
  434.7 74.4 all-gather.26
  510.7 74.4 all-gather.24
  588.1 121.6 all-gather.18
  712.6 116.9 all-gather.20
  832.3 89.5 all-gather.22
  924.7 69.7 reduce-scatter.26
  997.4 71.3 reduce-scatter.24
  1071.0 71.7 reduce-scatter.28
  1145.7 143.1 reduce-scatter.12
  1291.7 144.8 reduce-scatter.14
  1439.5 243.5 reduce-scatter.18
  1685.9 248.6 reduce-scatter.20
  1937.4 248.5 reduce-scatter.22
  2189.0 182.5 reduce-scatter.16
  2379.6 248.6 reduce-scatter.10
where the time goes:
time: 2640 us
  waiting for transfers between devices  2000 us (76%)
  matrix products  260 us (10%)
  blocking collectives  228 us (9%)
  local copies, waits for them, and re-layouts  72.6 us (3%)
  other arithmetic  34 us (1%)
    reduce_scatter x1, waiting for transfers between devices, local(): lax.psum_scatter(d_wq, ('dp', 'expert'), scatter_dimension=0, tiled=True)  257 us
    reduce_scatter x1, waiting for transfers between devices, local(): lax.psum_scatter(d_su, ('dp', 'expert'), scatter_dimension=0, tiled=True)  251 us
    reduce_scatter x1, waiting for transfers between devices, local(): lax.psum_scatter(d_sd, ('dp', 'expert'), scatter_dimension=1, tiled=True)  251 us
    reduce_scatter x1, waiting for transfers between devices, local(): lax.psum_scatter(d_sg, ('dp', 'expert'), scatter_dimension=0, tiled=True)  246 us
    unnamed x2, blocking collectives  228 us
    reduce_scatter x1, waiting for transfers between devices, local(): lax.psum_scatter(d_wo, ('dp', 'expert'), scatter_dimension=1, tiled=True)  186 us
    reduce_scatter x1, waiting for transfers between devices, local(): lax.psum_scatter(d_wkvb, ('dp', 'expert'), scatter_dimension=0, tiled=True)  148 us
    all_gather x1, waiting for transfers between devices, local(): lax.all_gather(shared_up, ('dp', 'expert'), axis=0, tiled=True)  113 us
  transfers between devices with their start and end apart: 24, of which 17 were waited for; matrix products, arithmetic and copies ran while one was open for 14% of the time, Pallas kernels for 0%

commit v1 on v0

v1 whole, which is shorter than its diff:
```python
import functools

import jax
import jax.numpy as jnp
from jax import lax
from jax.experimental import pallas as pl
from jax.experimental.pallas import tpu as pltpu
from jax.sharding import PartitionSpec as P

HEADS = 16
HD = 128
RD = 64
VD = 128
LAT = 512
TOP = 6
EPS = 1e-06
CHUNK = 256
SCALE = (HD + RD) ** (-0.5)
BF = jnp.bfloat16
F32 = jnp.float32
VMEM_LIMIT = 56 * 1024 * 1024


def matmul(left, right):
    return jnp.dot(left, right, preferred_element_type=F32)


def mat_trans(left, right):
    return lax.dot_general(left, right, (((1,), (1,)), ((), ())), preferred_element_type=F32)


def contract(left, right):
    return lax.dot_general(left, right, (((0,), (0,)), ((), ())), preferred_element_type=F32)


def rms_scale(values):
    return lax.rsqrt(jnp.mean(values * values, axis=-1, keepdims=True) + EPS)


def rms_back(incoming, values, scale, gain):
    scaled = incoming * gain
    inner = jnp.mean(scaled * values, axis=-1, keepdims=True)
    grad_in = scale * (scaled - values * scale * scale * inner)
    grad_gain = jnp.sum(incoming * values * scale, axis=0)
    return (grad_in, grad_gain)


def layout(lengths, rows):
    ends = jnp.cumsum(lengths, axis=-1)
    place = jnp.arange(rows, dtype=jnp.int32)
    passed = (place[None, :, None] >= ends[:, None, :]).astype(jnp.int32)
    doc = jnp.sum(passed, axis=-1)
    start = jnp.sum(passed * lengths[:, None, :], axis=-1)
    return ((place[None, :] - start).astype(F32), doc)


def move(value, to):
    return lax.ppermute(value, "expert", [(i, to(i)) for i in range(16)])


def z_up(value):
    return move(value, lambda i: (i + 4) % 16)


def z_down(value):
    return move(value, lambda i: (i + 12) % 16)


def z_two(value):
    return move(value, lambda i: (i + 8) % 16)


def x_swap(value):
    return move(value, lambda i: i ^ 2)


def core_swap(value):
    return move(value, lambda i: i ^ 1)


def gather_rows(own):
    pieces = [own]
    for _ in range(3):
        pieces.append(z_up(pieces[-1]))
    near = jnp.concatenate(pieces, axis=0)
    far = jnp.concatenate([x_swap(piece) for piece in pieces], axis=0)
    return jnp.concatenate([near, far, core_swap(near), core_swap(far)], axis=0)


def scatter_rows(partial):
    quarter = partial.shape[0] // 4
    rows = quarter // 4
    far = core_swap(partial[3 * quarter :])
    near = core_swap(partial[2 * quarter : 3 * quarter])
    far = (far.astype(F32) + partial[quarter : 2 * quarter].astype(F32)).astype(BF)
    near = near.astype(F32) + partial[:quarter].astype(F32)
    total = None
    for step in (3, 2, 1, 0):
        part = slice(step * rows, (step + 1) * rows)
        term = near[part] + x_swap(far[part]).astype(F32)
        if total is not None:
            term = term + z_down(total.astype(BF)).astype(F32)
        total = term
    return total


def exchange(blocks, place):
    z, x, core = place
    rest = blocks.shape[1:]
    view = blocks.reshape((4, 2, 2) + rest)

    def at(value, index, axis):
        return lax.dynamic_index_in_dim(value, index, axis, keepdims=False)

    view = jnp.stack([at(view, core, 2), core_swap(at(view, 1 - core, 2))], axis=2)
    view = jnp.stack([at(view, x, 1), x_swap(at(view, 1 - x, 1))], axis=1)
    view = jnp.stack(
        [
            at(view, z, 0),
            z_up(at(view, (z + 1) % 4, 0)),
            z_two(at(view, (z + 2) % 4, 0)),
            z_down(at(view, (z + 3) % 4, 0)),
        ],
        axis=0,
    )
    return view.reshape(blocks.shape)


def reorder_kernel(index_ref, in_ref, out_ref):
    out_ref[...] = in_ref[...]


def reorder(blocks, index):
    shape = blocks.shape
    block = (1,) + shape[1:]
    return pl.pallas_call(
        reorder_kernel,
        grid_spec=pltpu.PrefetchScalarGridSpec(
            num_scalar_prefetch=1,
            grid=(shape[0],),
            in_specs=[pl.BlockSpec(block, lambda i, index: (index[i], 0, 0))],
            out_specs=pl.BlockSpec(block, lambda i, index: (i, 0, 0)),
        ),
        out_shape=jax.ShapeDtypeStruct(shape, blocks.dtype),
        compiler_params=pltpu.CompilerParams(vmem_limit_bytes=VMEM_LIMIT),
    )(index, blocks)


def swap_halves(values):
    lane = lax.broadcasted_iota(jnp.int32, values.shape, 1)
    return jnp.where(
        lane % RD < RD // 2, pltpu.roll(values, 2 * RD - RD // 2, 1), pltpu.roll(values, RD // 2, 1)
    )


def attend(proj, cosine, sine, id_col, id_row, lat_gain, w_exp):
    mixed = proj[:, HD : 2 * HD]
    turned = (mixed * cosine + swap_halves(mixed) * sine).astype(BF)
    q_rope, k_rope = turned[:, :RD], turned[:, RD:]
    q_main = proj[:, :HD].astype(BF)
    lat = proj[:, 2 * HD :]
    compressed = (lat * rms_scale(lat) * lat_gain).astype(BF)
    expanded = matmul(compressed, w_exp).astype(BF)
    k_main, values = expanded[:, :HD], expanded[:, HD:]
    scores = (mat_trans(q_main, k_main) + mat_trans(q_rope, k_rope)) * SCALE
    above = lax.broadcasted_iota(jnp.int32, scores.shape, 1)
    below = lax.broadcasted_iota(jnp.int32, scores.shape, 0)
    allowed = (id_col == id_row) & (above <= below)
    scores = jnp.where(allowed, scores, -1e30)
    expo = jnp.exp(scores - jnp.max(scores, axis=-1, keepdims=True))
    probs = expo / jnp.sum(expo, axis=-1, keepdims=True)
    return q_main, q_rope, k_main, k_rope, values, compressed, probs


def forward_kernel(
    x_ref, gain_ref, wp_ref, cos_ref, sin_ref, idc_ref, idr_ref, lg_ref, we_ref, wo_ref, part_ref, proj_ref, att_ref
):
    xf = x_ref[...].astype(F32)
    normed = (xf * rms_scale(xf) * gain_ref[...]).astype(BF)
    proj = matmul(normed, wp_ref[...])
    proj_ref[...] = proj
    values, probs = attend(
        proj, cos_ref[...], sin_ref[...], idc_ref[...], idr_ref[0], lg_ref[...], we_ref[...]
    )[4::2]
    attended = matmul(probs.astype(BF), values).astype(BF)
    att_ref[...] = attended
    part_ref[...] = mat_trans(attended, wo_ref[...]).astype(BF)


def backward_kernel(
    x_ref, g_ref, proj_ref, att_ref, gain_ref, wp_ref, cos_ref, sin_ref, idc_ref, idr_ref, lg_ref, we_ref, wo_ref,
    dn_ref, dl_ref, dwq_ref, dwo_ref, dwe_ref, dg_ref, acc_q, acc_o, acc_e, acc_g,
):
    step = pl.program_id(0)

    @pl.when(step == 0)
    def _():
        acc_q[...] = jnp.zeros_like(acc_q)
        acc_o[...] = jnp.zeros_like(acc_o)
        acc_e[...] = jnp.zeros_like(acc_e)
        acc_g[...] = jnp.zeros_like(acc_g)

    xf = x_ref[...].astype(F32)
    whitened = xf * rms_scale(xf)
    normed = (whitened * gain_ref[...]).astype(BF)
    grad = g_ref[...]
    cosine, sine = cos_ref[...], sin_ref[...]
    w_exp = we_ref[...]
    q_main, q_rope, k_main, k_rope, values, compressed, probs = attend(
        proj_ref[...], cosine, sine, idc_ref[...], idr_ref[0], lg_ref[...], w_exp
    )
    prob_low = probs.astype(BF)
    d_att = matmul(grad, wo_ref[...]).astype(BF)
    d_prob = mat_trans(d_att, values)
    d_values = contract(prob_low, d_att)
    d_scores = (probs * (d_prob - jnp.sum(probs * d_prob, axis=-1, keepdims=True))).astype(BF)
    d_mixed = jnp.concatenate([matmul(d_scores, k_rope), contract(d_scores, q_rope)], axis=1) * SCALE
    d_mixed = d_mixed * cosine - swap_halves(d_mixed) * sine
    d_query = jnp.concatenate([matmul(d_scores, k_main) * SCALE, d_mixed[:, :RD]], axis=1).astype(BF)
    d_expanded = jnp.concatenate([contract(d_scores, q_main) * SCALE, d_values], axis=1).astype(BF)
    dl_ref[...] = jnp.concatenate([mat_trans(d_expanded, w_exp), d_mixed[:, RD:]], axis=1).astype(BF)
    d_normed = mat_trans(d_query, wp_ref[...][:, : HD + RD])
    dn_ref[...] = d_normed.astype(BF)
    acc_g[...] += jnp.sum(d_normed * whitened, axis=0, keepdims=True)
    acc_q[...] += contract(d_query, normed)
    acc_o[...] += contract(att_ref[...], grad)
    acc_e[...] += contract(compressed, d_expanded)

    @pl.when(step == pl.num_programs(0) - 1)
    def _():
        dwq_ref[...] = acc_q[...].T.astype(BF)
        dwo_ref[...] = acc_o[...].T.astype(BF)
        dwe_ref[...] = acc_e[...].astype(BF)
        dg_ref[...] = acc_g[...]


def chunk_spec(width):
    return pl.BlockSpec((CHUNK, width), lambda i: (i, 0))


def whole_spec(array):
    return pl.BlockSpec(array.shape, lambda i: (0,) * array.ndim)


def row_spec():
    return pl.BlockSpec((1, 1, CHUNK), lambda i: (i, 0, 0))


def call(kernel, rows, args, specs, outs, out_specs, scratch=(), flops=0):
    size = sum(a.size * a.dtype.itemsize for a in list(args) + list(outs))
    return pl.pallas_call(
        kernel,
        grid=(rows // CHUNK,),
        in_specs=specs,
        out_specs=out_specs,
        out_shape=outs,
        scratch_shapes=list(scratch),
        compiler_params=pltpu.CompilerParams(vmem_limit_bytes=VMEM_LIMIT),
        cost_estimate=pl.CostEstimate(flops=flops, bytes_accessed=size, transcendentals=0),
    )(*args)


def attention_forward(x_all, gain, w_proj, tables, lat_gain, w_exp, w_out):
    rows, width = x_all.shape
    cosine, sine, id_col, id_row = tables
    args = (x_all, gain, w_proj, cosine, sine, id_col, id_row, lat_gain, w_exp, w_out)
    specs = [
        chunk_spec(width), whole_spec(gain), whole_spec(w_proj), chunk_spec(HD), chunk_spec(HD), chunk_spec(1),
        row_spec(), whole_spec(lat_gain), whole_spec(w_exp), whole_spec(w_out),
    ]
    outs = (
        jax.ShapeDtypeStruct((rows, width), BF),
        jax.ShapeDtypeStruct((rows, w_proj.shape[1]), F32),
        jax.ShapeDtypeStruct((rows, VD), BF),
    )
    out_specs = (chunk_spec(width), chunk_spec(w_proj.shape[1]), chunk_spec(VD))
    return call(forward_kernel, rows, args, specs, outs, out_specs, flops=2 * rows * width * 1024)


def attention_backward(x_all, grad, proj, attended, gain, w_proj, tables, lat_gain, w_exp, w_out):
    rows, width = x_all.shape
    cosine, sine, id_col, id_row = tables
    args = (x_all, grad, proj, attended, gain, w_proj, cosine, sine, id_col, id_row, lat_gain, w_exp, w_out)
    specs = [
        chunk_spec(width), chunk_spec(width), chunk_spec(proj.shape[1]), chunk_spec(VD), whole_spec(gain),
        whole_spec(w_proj), chunk_spec(HD), chunk_spec(HD), chunk_spec(1), row_spec(), whole_spec(lat_gain),
        whole_spec(w_exp), whole_spec(w_out),
    ]
    outs = (
        jax.ShapeDtypeStruct((rows, width), BF),
        jax.ShapeDtypeStruct((rows, LAT + RD), BF),
        jax.ShapeDtypeStruct((width, HD + RD), BF),
        jax.ShapeDtypeStruct((width, VD), BF),
        jax.ShapeDtypeStruct((LAT, HD + VD), BF),
        jax.ShapeDtypeStruct((1, width), F32),
    )
    out_specs = (chunk_spec(width), chunk_spec(LAT + RD)) + tuple(whole_spec(o) for o in outs[2:])
    scratch = (
        pltpu.VMEM((HD + RD, width), F32),
        pltpu.VMEM((VD, width), F32),
        pltpu.VMEM((LAT, HD + VD), F32),
        pltpu.VMEM((1, width), F32),
    )
    return call(backward_kernel, rows, args, specs, outs, out_specs, scratch, flops=2 * rows * width * 1024)


def enter_kernel(slots, tok_ref, g_ref, target_ref, gate_ref, sw_ref, rx_ref, rg_ref, rs_ref, act_ref, pre_ref):
    tok, grad = tok_ref[...], g_ref[...]
    slot = lax.broadcasted_iota(jnp.int32, (slots, CHUNK), 0)
    chosen = slot == target_ref[0]
    hot = chosen.astype(BF)
    share = jnp.sum(jnp.where(chosen, gate_ref[0], 0.0), axis=1, keepdims=True)
    rs_ref[...] = share
    rx_ref[...] = matmul(hot, tok).astype(BF)
    rg_ref[...] = (matmul(hot, grad) * share).astype(BF)
    third = sw_ref.shape[1] // 3
    gate_pre = matmul(tok, sw_ref[:, :third])
    up = matmul(tok, sw_ref[:, third : 2 * third])
    d_act = matmul(grad, sw_ref[:, 2 * third :])
    sigma = jax.nn.sigmoid(gate_pre)
    swish = gate_pre * sigma
    act_ref[...] = (swish * up).astype(BF)
    slope = sigma * (1.0 + gate_pre * (1.0 - sigma))
    pre_ref[:, :third] = (d_act * up * slope).astype(BF)
    pre_ref[:, third:] = (d_act * swish).astype(BF)


def enter_experts(tok, grad, target, gate, shared_w, slots):
    rows, width = tok.shape
    third = shared_w.shape[1] // 3
    per = slots * CHUNK // rows
    args = (tok, grad, target.reshape(-1, 1, CHUNK), gate.reshape(-1, 1, CHUNK), shared_w)
    specs = [chunk_spec(width), chunk_spec(width), row_spec(), row_spec(), whole_spec(shared_w)]
    outs = (
        jax.ShapeDtypeStruct((slots, width), BF),
        jax.ShapeDtypeStruct((slots, width), BF),
        jax.ShapeDtypeStruct((slots, 1), F32),
        jax.ShapeDtypeStruct((rows, third), BF),
        jax.ShapeDtypeStruct((rows, 2 * third), BF),
    )
    out_specs = (
        pl.BlockSpec((per, width), lambda i: (i, 0)),
        pl.BlockSpec((per, width), lambda i: (i, 0)),
        pl.BlockSpec((per, 1), lambda i: (i, 0)),
        chunk_spec(third),
        chunk_spec(2 * third),
    )
    flops = 2 * rows * width * (3 * third + 2 * per)
    return call(functools.partial(enter_kernel, per), rows, args, specs, outs, out_specs, flops=flops)


def leave_kernel(slots, rows_ref, target_ref, left_ref, right_ref, out_ref):
    slot = lax.broadcasted_iota(jnp.int32, (CHUNK, slots), 1)
    hot = (slot == target_ref[...]).astype(BF)
    out_ref[...] = (matmul(hot, rows_ref[...]) + mat_trans(left_ref[...], right_ref[...])).astype(BF)


def leave_experts(slot_rows, target, left, right):
    slots, width = slot_rows.shape
    rows = left.shape[0]
    per = slots * CHUNK // rows
    args = (slot_rows, target.reshape(-1, 1), left, right)
    specs = [
        pl.BlockSpec((per, width), lambda i: (i, 0)), chunk_spec(1), chunk_spec(left.shape[1]), whole_spec(right)
    ]
    outs = jax.ShapeDtypeStruct((rows, width), BF)
    flops = 2 * rows * width * (per + left.shape[1])
    return call(
        functools.partial(leave_kernel, per), rows, args, specs, (outs,), (chunk_spec(width),), flops=flops
    )[0]


def local(
    tokens, lengths, routes, gates, norm_in, latent_gain, norm_mid, w_query, w_latent, w_expand, w_output,
    shared_gate, shared_up, shared_down, expert_gate, expert_up, expert_down, cotangent,
):
    micro = lengths.shape[0]
    own_rows, width = tokens.shape
    rows = own_rows // micro
    experts = lax.axis_size("expert")
    ndp = lax.axis_size("dp")
    cap = rows * TOP * 4 // (3 * experts)
    blocks = experts * micro
    all_rows = experts * own_rows
    shard = width // (ndp * experts)
    ff_s = shared_gate.shape[1]
    ff_part = ff_s // experts
    ff_pad = -(-ff_part // 128) * 128
    ff_e = expert_gate.shape[2]
    half = width // 2
    me = lax.axis_index("expert")
    dp = lax.axis_index("dp")
    core, x, z = me % 2, (me // 2) % 2, me // 4
    place = (z, x, core)

    def turn(value):
        if ndp != 2:
            return value
        swapped = jnp.concatenate([value[..., half:], value[..., :half]], axis=-1)
        return jnp.where(dp == 1, swapped, value)

    def dp_swap(value):
        return lax.ppermute(value, "dp", [(0, 1), (1, 0)])

    def dp_gather(value):
        if ndp == 2:
            return jnp.stack([value, dp_swap(value)])
        return lax.all_gather(value, "dp", axis=0)

    def dp_scatter(value):
        if ndp == 2:
            return value[0].astype(F32) + dp_swap(value[1].astype(BF)).astype(F32)
        return lax.psum_scatter(value.astype(BF), "dp", scatter_dimension=0, tiled=False).astype(F32)

    number = jnp.arange(experts, dtype=jnp.int32)
    near_z, near_x, near_c = number % 4, (number // 4) % 2, number // 8
    row_index = ((z - near_z) % 4) * 4 + (near_x ^ x) * 2 + (near_c ^ core)
    n_z, n_x, n_c = number // 4, (number // 2) % 2, number % 2
    block_index = ((z - n_z) % 4) * 4 + (n_x ^ x) * 2 + (n_c ^ core)

    by_expert = jnp.sum(
        jnp.where(routes.T[None] == number[:, None, None], gates.T[None], 0.0), axis=1
    )
    facts = jnp.concatenate(
        [by_expert, jnp.pad(lengths.reshape(1, -1).astype(F32), ((0, 7), (0, own_rows - lengths.size)))], axis=0
    )
    facts = lax.all_gather(facts, "expert", axis=0)
    facts = jnp.take(facts, row_index, axis=0)
    gate_all = lax.dynamic_index_in_dim(facts, me, 1, keepdims=False).reshape(blocks, rows)
    lengths_all = facts[:, experts, : lengths.size].astype(jnp.int32).reshape(blocks, lengths.shape[1])

    gains = jnp.concatenate([norm_in, norm_mid, latent_gain])
    w_lat_rows = jnp.concatenate(
        [w_latent, jnp.pad(gains[None], ((0, 15), (0, w_latent.shape[1] - gains.shape[0])))], axis=0
    )
    w_lat_all = lax.all_gather(w_lat_rows, ("dp", "expert"), axis=0)
    gains = w_lat_all[:, shard].astype(F32)
    gain_in = turn(gains[:, :shard].reshape(1, width))
    gain_mid = turn(gains[:, shard : 2 * shard].reshape(1, width))
    gain_lat = gains[:, 2 * shard : 2 * shard + latent_gain.shape[0]].reshape(1, LAT)
    w_lat = w_lat_all[:, :shard].reshape(width, LAT + RD)
    w_lat_near = w_lat
    if ndp == 2:
        w_lat_near = jnp.where(dp == 1, jnp.concatenate([w_lat[half:], w_lat[:half]]), w_lat)

    lat_rows = w_expand.shape[0]
    groups = shard // lat_rows
    exp_cols = (HD + VD) // groups
    piece = jnp.concatenate(
        [
            w_query.reshape(shard, HEADS, HD + RD).transpose(1, 0, 2),
            w_expand.reshape(lat_rows, HEADS, groups, exp_cols).transpose(1, 2, 0, 3).reshape(HEADS, shard, exp_cols),
            w_output.reshape(HEADS, VD, shard).transpose(0, 2, 1),
        ],
        axis=2,
    )
    piece = reorder(exchange(piece, place), block_index)
    head_w = dp_gather(piece)
    exp_at = HD + RD
    out_at = exp_at + exp_cols
    w_exp = head_w[..., exp_at:out_at]
    if ndp == 2:
        w_exp = jnp.where(dp == 1, w_exp[::-1], w_exp)
    w_exp = w_exp.reshape(ndp * experts, groups, lat_rows, exp_cols).transpose(0, 2, 1, 3).reshape(LAT, HD + VD)
    w_out = head_w[..., out_at:].reshape(width, VD)
    w_proj = jnp.concatenate(
        [head_w[..., :exp_at].reshape(width, exp_at), w_lat_near[:, LAT:], w_lat_near[:, :LAT]], axis=1
    )

    piece = jnp.concatenate(
        [
            shared_gate.reshape(shard, experts, ff_part).transpose(1, 0, 2),
            shared_up.reshape(shard, experts, ff_part).transpose(1, 0, 2),
            shared_down.reshape(experts, ff_part, shard).transpose(0, 2, 1),
        ],
        axis=2,
    )
    piece = reorder(exchange(piece, place), block_index)
    shared_w = dp_gather(piece).reshape(width, 3 * ff_part)
    spare = jnp.zeros((width, ff_pad - ff_part), BF)
    shared_w = jnp.concatenate(
        [
            shared_w[:, :ff_part], spare, shared_w[:, ff_part : 2 * ff_part], spare, shared_w[:, 2 * ff_part :], spare
        ],
        axis=1,
    )

    gate_up = jnp.concatenate([expert_gate[0], expert_up[0]], axis=1)
    gate_up = dp_gather(gate_up).reshape(width, 2 * ff_e)
    down = dp_gather(expert_down[0])
    down = jnp.concatenate([down[i] for i in range(ndp)], axis=1)

    position, doc = layout(lengths_all, rows)
    freq = jnp.power(10000.0, -2.0 * jnp.arange(RD // 2, dtype=F32) / RD)
    theta = position.reshape(all_rows, 1) * freq
    cosine, sine = jnp.cos(theta), jnp.sin(theta)
    cosine = jnp.concatenate([cosine] * 4, axis=1)
    sine = jnp.concatenate([-sine, sine, -sine, sine], axis=1)
    ids = doc + 4 * jnp.arange(blocks, dtype=jnp.int32)[:, None]
    tables = (cosine, sine, ids.reshape(all_rows, 1), ids.reshape(-1, 1, CHUNK))
    routed = (gate_all > 0.0).astype(jnp.int32)
    in_chunk = jnp.arange(blocks, dtype=jnp.int32)[:, None] % (CHUNK // rows)
    target = jnp.where(routed > 0, in_chunk * cap + jnp.cumsum(routed, axis=1) - 1, -1)

    x_near = turn(tokens)
    x_all = gather_rows(x_near)
    part, proj, attended = attention_forward(x_all, gain_in, w_proj, tables, gain_lat, w_exp, w_out)
    xf = x_near.astype(F32)
    mid = xf + scatter_rows(part)
    scale_mid = rms_scale(mid)
    normed_mid = (mid * scale_mid * gain_mid).astype(BF)
    grad_near = turn(cotangent)

    tok_all = gather_rows(normed_mid)
    grad_all = gather_rows(grad_near.astype(BF))
    rows_x, rows_g, share, s_act, d_s_pre = enter_experts(
        tok_all, grad_all, target, gate_all, shared_w, blocks * cap
    )
    pre = matmul(rows_x, gate_up)
    e_gate, e_up = pre[:, :ff_e], pre[:, ff_e:]
    sigma = jax.nn.sigmoid(e_gate)
    e_swish = e_gate * sigma
    e_slope = sigma * (1.0 + e_gate * (1.0 - sigma))
    e_act = (e_swish * e_up).astype(BF)
    d_e_act = mat_trans(rows_g, down)
    d_pre = jnp.concatenate([(d_e_act * e_up * e_slope).astype(BF), (d_e_act * e_swish).astype(BF)], axis=1)
    d_rows = mat_trans(d_pre, gate_up).astype(BF)
    d_part = leave_experts(d_rows, target, d_s_pre, shared_w[:, : 2 * ff_pad])
    d_mid_normed = scatter_rows(d_part)
    e_out = (matmul(e_act, down) * share).astype(BF)
    out_part = leave_experts(e_out, target, s_act, shared_w[:, 2 * ff_pad :])
    out = turn(mid + scatter_rows(out_part)).astype(BF)

    if ndp == 2:
        d_down = matmul(e_act.T, rows_g[:, :half]) + dp_swap(contract(e_act, rows_g[:, half:]).astype(BF)).astype(F32)
        d_gu = contract(rows_x[:, :half], d_pre) + dp_swap(contract(rows_x[:, half:], d_pre).astype(BF)).astype(F32)
    else:
        d_down = lax.psum_scatter(
            contract(e_act, rows_g).astype(BF), "dp", scatter_dimension=1, tiled=True
        ).astype(F32)
        d_gu = lax.psum_scatter(contract(rows_x, d_pre).astype(BF), "dp", scatter_dimension=0, tiled=True).astype(F32)
    d_shared = jnp.concatenate([contract(tok_all, d_s_pre), contract(grad_all, s_act)], axis=1).astype(BF)
    d_shared = jnp.concatenate(
        [d_shared[:, i * ff_pad : i * ff_pad + ff_part] for i in range(3)], axis=1
    ).reshape(ndp, experts, shard, 3 * ff_part)
    d_shared = dp_scatter(d_shared).astype(BF)
    d_shared = reorder(exchange(d_shared, place), block_index).astype(F32)
    grad_sg, grad_su = (
        d_shared[:, :, i * ff_part : (i + 1) * ff_part].transpose(1, 0, 2).reshape(shard, ff_s) for i in range(2)
    )
    grad_sd = d_shared[:, :, 2 * ff_part :].transpose(0, 2, 1).reshape(ff_s, shard)

    d_mid_in, d_gain_mid = rms_back(d_mid_normed, mid, scale_mid, gain_mid)
    d_mid = grad_near + d_mid_in
    grad_attn = gather_rows(d_mid.astype(BF))
    d_norm_part, d_lat_part, d_wq, d_wo, d_we, d_gain_part = attention_backward(
        x_all, grad_attn, proj, attended, gain_in, w_proj, tables, gain_lat, w_exp, w_out
    )
    d_lat_own = scatter_rows(d_lat_part)
    lat_own = proj[:own_rows, 2 * HD :]
    d_lat_in, d_gain_lat = rms_back(d_lat_own[:, :LAT], lat_own, rms_scale(lat_own), gain_lat)
    d_latent = jnp.concatenate([d_lat_in, d_lat_own[:, LAT:]], axis=1).astype(BF)
    scale_in = rms_scale(xf)
    normed_own = turn((xf * scale_in * gain_in).astype(BF))
    d_wl = contract(normed_own, d_latent).astype(BF).reshape(ndp * experts, shard, LAT + RD)
    d_normed_own = mat_trans(d_latent, w_lat_near)
    d_gain_in = turn(d_gain_part[0] + jnp.sum(d_normed_own * xf * scale_in, axis=0))
    d_gains = jnp.concatenate(
        [
            d_gain_in.reshape(ndp * experts, shard),
            turn(d_gain_mid).reshape(ndp * experts, shard),
            d_gain_lat.reshape(ndp * experts, LAT // (ndp * experts)),
        ],
        axis=1,
    ).astype(BF)
    d_gains = jnp.pad(d_gains[:, None], ((0, 0), (0, 15), (0, LAT + RD - d_gains.shape[1])))
    d_wl = lax.psum_scatter(
        jnp.concatenate([d_wl, d_gains], axis=1), ("dp", "expert"), scatter_dimension=0, tiled=False
    ).astype(F32)
    d_normed = scatter_rows(d_norm_part) + d_normed_own
    d_in, _ = rms_back(d_normed, xf, scale_in, gain_in)
    d_tokens = turn(d_mid + d_in)

    d_we = d_we.reshape(ndp * experts, lat_rows, groups, exp_cols).transpose(0, 2, 1, 3)
    d_we = d_we.reshape(ndp, experts, shard, exp_cols)
    if ndp == 2:
        d_we = jnp.where(dp == 1, d_we[::-1], d_we)
    d_head = jnp.concatenate(
        [d_wq.reshape(ndp, experts, shard, HD + RD), d_we, d_wo.reshape(ndp, experts, shard, VD)], axis=3
    )
    d_head = dp_scatter(d_head).astype(BF)
    d_head = reorder(exchange(d_head, place), block_index).astype(F32)
    grad_wq = d_head[:, :, :exp_at].transpose(1, 0, 2).reshape(shard, HEADS * (HD + RD))
    grad_we = d_head[:, :, exp_at:out_at].reshape(HEADS, groups, lat_rows, exp_cols).transpose(2, 0, 1, 3)
    grad_we = grad_we.reshape(lat_rows, HEADS * (HD + VD))
    grad_wo = d_head[:, :, out_at:].transpose(0, 2, 1).reshape(HEADS * VD, shard)

    last = 2 * shard + latent_gain.shape[0]
    return (
        out,
        d_tokens,
        d_wl[shard, :shard],
        d_wl[shard, 2 * shard : last],
        d_wl[shard, shard : 2 * shard],
        grad_wq,
        d_wl[:shard],
        grad_we,
        grad_wo,
        grad_sg,
        grad_su,
        grad_sd,
        d_gu[None, :, :ff_e],
        d_gu[None, :, ff_e:],
        d_down[None],
    )


def solution(mesh):
    rows = P(("dp", "expert"), None)
    vector = P(("dp", "expert"))
    columns = P(None, ("dp", "expert"))
    by_row = P("expert", "dp", None)
    by_column = P("expert", None, "dp")
    return jax.shard_map(
        local,
        mesh=mesh,
        in_specs=(
            rows, rows, rows, rows, vector, vector, vector, rows, rows, rows, columns, rows, rows, columns, by_row,
            by_row, by_column, rows,
        ),
        out_specs=(
            rows, rows, vector, vector, vector, rows, rows, rows, columns, rows, rows, columns, by_row, by_row,
            by_column,
        ),
        check_vma=False,
    )
```

time: 2640 us -> 1200 us (0.45)
  waiting for transfers between devices: 2000 us -> 444 us
  blocking collectives: 228 us -> 21.5 us
  matrix products: 260 us -> 120 us
  starting transfers between devices: 24.7 us -> 161 us
  Pallas kernels: 0 us -> 132 us
  other arithmetic: 34 us -> 131 us
  local copies, waits for them, and re-layouts: 72.6 us -> 167 us
    reduce_scatter x10 -> x1, waiting for transfers between devices: 1400 us -> 57.4 us  [local(): lax.psum_scatter(jnp.concatenate([d_wl, d_gains], axis=1), ('dp', 'expert...]
    all_gather x10 -> x1, waiting for transfers between devices: 591 us -> 0.01 us  [local(): w_lat_all = lax.all_gather(w_lat_rows, ('dp', 'expert'), axis=0)]
    ppermute x0 -> x109, waiting for transfers between devices: none -> 386 us  [the longest x101 292 us: move(): return lax.ppermute(value, 'expert', [(i, to(i)) for i in range(16)])]
    unnamed x2 -> x0, blocking collectives: 228 us -> none
    ppermute x0 -> x109, starting transfers between devices: none -> 161 us  [the longest x101 151 us: move(): return lax.ppermute(value, 'expert', [(i, to(i)) for i in range(16)])]
    pallas_call x0 -> x9, Pallas kernels: none -> 132 us  [the longest x5 93.2 us: call(): pl.pallas_call(kernel, grid=(rows // CHUNK,), in_specs=specs, out_specs=o...]
    dot_general x19 -> x3, matrix products: 94.5 us -> 41.1 us  [matmul(): return jnp.dot(left, right, preferred_element_type=F32)]
    dot_general x10 -> x6, matrix products: 93.2 us -> 43.6 us  [contract(): lax.dot_general(left, right, (((0,), (0,)), ((), ())), preferred_element_...]
  transfers between devices with their start and end apart: 24 -> 111, of which waited for: 17 -> 46; matrix products, arithmetic and copies ran while one was open for 14% -> 31% of each run, Pallas kernels for 0% -> 10%
where the time goes in v1:
time: 1200 us; the launch traced here: 1190 us
  waiting for transfers between devices  444 us (37%)
  local copies, waits for them, and re-layouts  167 us (14%)
  starting transfers between devices  161 us (13%)
  Pallas kernels  132 us (11%)
  other arithmetic  131 us (11%)
  matrix products  120 us (10%)
  blocking collectives  21.5 us (2%)
  between operations  16.1 us (1%)
    ppermute x101, waiting for transfers between devices, move(): return lax.ppermute(value, 'expert', [(i, to(i)) for i in range(16)])  292 us
    ppermute x101, starting transfers between devices, move(): return lax.ppermute(value, 'expert', [(i, to(i)) for i in range(16)])  151 us
    ppermute x8, waiting for transfers between devices, dp_swap(): return lax.ppermute(value, 'dp', [(0, 1), (1, 0)])  94 us
    pallas_call x5, Pallas kernels, call(): pl.pallas_call(kernel, grid=(rows // CHUNK,), in_specs=specs, out_specs=o...  93.2 us
    reduce_scatter x1, waiting for transfers between devices, local(): lax.psum_scatter(jnp.concatenate([d_wl, d_gains], axis=1), ('dp', 'expert...  57.4 us
    unnamed x224, local copies, waits for them, and re-layouts  49.5 us
    dot_general x6, matrix products, contract(): lax.dot_general(left, right, (((0,), (0,)), ((), ())), preferred_element_...  43.6 us
    dot_general x3, matrix products, matmul(): return jnp.dot(left, right, preferred_element_type=F32)  41.1 us
  transfers between devices with their start and end apart: 111, of which 46 were waited for; matrix products, arithmetic and copies ran while one was open for 31% of the time, Pallas kernels for 10%

profile of v1, /device:TPU:0, one launch (start us, length us, event | category | flops | bytes accessed | tf_op | source)
XLA Modules:
  0.0 1191.0 jit_solution(11599406448507408124)
XLA Ops:
  21.1 21.5 %all-gather.1 = f32[384,128]{1,0:T(8,128)S(1)} all-gather(f32[24,128]{1,0:T(8,128)S(1)} %select_maximum_fusion), channel_id=3, replica_groups=mesh['dp'=2,'expert'=16] {'expert'}, dimensions={0}, use_global_device_ids=true | all-gather | bytes 208896 | tf_op jit(solution)/shard_map/all_gather | solution.py:427
  70.8 12.8 %collective-permute-done.1 = bf16[128,2048]{1,0:T(8,128)(2,1)} collective-permute-done((bf16[128,2048]{1,0:T(8,128)(2,1)}, bf16[128,2048]{1,0:T(8,128)(2,1)}, u32[]{:S(2)}, u32[]{:S(2)}) %collective-permute-start.1) | collective-permute-done | bytes 524320 | tf_op jit(solution)/shard_map/ppermute | solution.py:58
  182.1 24.8 %shard_map.290 = (bf16[2048,2048]{1,0:T(8,128)(2,1)}, f32[2048,768]{1,0:T(8,128)}, bf16[2048,128]{1,0:T(8,128)(2,1)}) custom-call(bf16[2048,2048]{1,0:T(8,128)(2,1)} %constant_dynamic-update-slice_fusion.x_ref, f32[1,2048]{1,0:T(1,128)} %broadcast_select_fusion.2.gain_ref, bf16[2048,768]{1,0:T(8,128)(2,1)} %pad_maximum_fusion.7.wp_ref, ...), custom_call_target="tpu_custom_call" | custom-call | flops 8589934592 | bytes 29648896 | tf_op jit(solution)/shard_map/pallas_call | solution.py:251
  270.2 11.0 collective-permute-done.45
  300.4 15.8 %collective-permute-start.22 = (bf16[128,2048]{1,0:T(8,128)(2,1)S(1)}, bf16[128,2048]{1,0:T(8,128)(2,1)S(1)}, u32[]{:S(2)}, u32[]{:S(2)}) collective-permute-start(bf16[128,2048]{1,0:T(8,128)(2,1)S(1)} %fusion.46), channel_id=1, source_target_pairs={{0,12},{1,13},{2,14},{3,15},{4,0},{5,1},{6,2},{7,3},{8,4},{9,5},{1... | collective-permute-start | bytes 1572872 | tf_op jit(solution)/shard_map/ppermute | solution.py:58
  343.0 15.7 %collective-permute-start.23 = (bf16[128,2048]{1,0:T(8,128)(2,1)}, bf16[128,2048]{1,0:T(8,128)(2,1)S(1)}, u32[]{:S(2)}, u32[]{:S(2)}) collective-permute-start(bf16[128,2048]{1,0:T(8,128)(2,1)} %fusion.48), channel_id=1, source_target_pairs={{0,12},{1,13},{2,14},{3,15},{4,0},{5,1},{6,2},{7,3},{8,4},{9,5},{1... | collective-permute-start | bytes 1572872 | tf_op jit(solution)/shard_map/ppermute | solution.py:58
  371.1 64.8 %collective-permute-done.47 = bf16[16,64,528]{2,1,0:T(8,128)(2,1)} collective-permute-done((bf16[16,64,528]{2,1,0:T(8,128)(2,1)S(1)}, bf16[16,64,528]{2,1,0:T(8,128)(2,1)}, u32[]{:S(2)}, u32[]{:S(2)}) %collective-permute-start.47) | collective-permute-done | bytes 1081376 | tf_op jit(solution)/shard_map/ppermute | solution.py:403
  437.7 11.5 collective-permute-start.25
  494.4 11.2 collective-permute-done.29
  532.1 16.7 %shard_map.292 = (bf16[1024,2048]{1,0:T(8,128)(2,1)}, bf16[1024,2048]{1,0:T(8,128)(2,1)}, f32[1024,1]{1,0:T(8,128)}, bf16[2048,256]{1,0:T(8,128)(2,1)}, bf16[2048,512]{1,0:T(8,128)(2,1)}) custom-call(bf16[2048,2048]{1,0:T(8,128)(2,1)} %constant_dynamic-update-slice_fusion.10.tok_ref, bf16[2048,2048]{1,0:T(8,128)(2,1)} %constant_dynamic-update-slice_fusion.20.g_ref, ...), custom_call_target="tpu_custom_call" | custom-call | flops 8589934592 | bytes 31477760 | tf_op jit(solution)/shard_map/pallas_call | solution.py:251
  550.1 18.7 %fusion.188 = f32[1024,2816]{1,0:T(8,128)} fusion(bf16[1024,2048]{1,0:T(8,128)(2,1)} %get-tuple-element.30, bf16[2048,2816]{1,0:T(8,128)(2,1)} %bitcast.196), kind=kOutput, calls=%fused_computation.483 | convolution fusion | flops 11811160064 | bytes 27262976 | tf_op jit(solution)/shard_map/dot_general | solution.py:25
  568.8 15.2 %multiply_convert_fusion.2 = (bf16[1024,1408]{1,0:T(8,128)(2,1)S(1)}, bf16[1024,1408]{1,0:T(8,128)(2,1)S(1)}, bf16[1024,1408]{1,0:T(8,128)(2,1)}) fusion(f32[1024,2816]{1,0:T(8,128)} %fusion.188, bf16[1024,2048]{1,0:T(8,128)(2,1)} %get-tuple-element.33, bf16[1408,1024]{1,0:T(8,128)(2,1)} %collective-permute-done.49, bf16[1408,1024]{1,0:T(8,128)(2,1)} %bitcast.59), kind=kOutput, calls=%fused_computation.11 | convolution fusion | flops 5938741248 | bytes 30146560 | tf_op jit(solution)/shard_map/dot_general | solution.py:29
  584.0 13.4 %multiply_convert_fusion.rows_ref = bf16[1024,2048]{1,0:T(8,128)(2,1)} fusion(bf16[1024,1408]{1,0:T(8,128)(2,1)} %get-tuple-element.69, f32[1024]{0:T(1024)S(1)} %reduce.2, bf16[1408,1024]{1,0:T(8,128)(2,1)} %collective-permute-done.49, bf16[1408,1024]{1,0:T(8,128)(2,1)} %bitcast.59), kind=kOutput, calls=%fused_computation.3 | convolution fusion | flops 5921308672 | bytes 12849152 | tf_op jit(solution)/shard_map/dot_general | solution.py:25
  597.4 11.1 shard_map.293
  613.8 16.3 %convolution_convert_fusion.1.rows_ref = bf16[1024,2048]{1,0:T(8,128)(2,1)} fusion(bf16[2048,2816]{1,0:T(8,128)(2,1)} %bitcast.197, bf16[1024,1408]{1,0:T(8,128)(2,1)S(1)} %get-tuple-element.66, bf16[1024,1408]{1,0:T(8,128)(2,1)S(1)} %get-tuple-element.65), kind=kOutput, calls=%fused_computation.24 | convolution fusion | flops 11824791552 | bytes 21495808 | tf_op jit(solution)/shard_map/dot_general | solution.py:29
  630.0 12.8 %shard_map.294 = bf16[2048,2048]{1,0:T(8,128)(2,1)} custom-call(bf16[1024,2048]{1,0:T(8,128)(2,1)} %convolution_convert_fusion.1.rows_ref, s32[2048,1]{1,0:T(8,128)} %broadcast_select_fusion.target_ref, bf16[2048,512]{1,0:T(8,128)(2,1)} %get-tuple-element.34.left_ref, bf16[2048,512]{1,0:T(8,128)(2,1)} %pad_maximum_fusion.16.right_ref), custom_call_target="tpu_custom_call" | custom-call | flops 5368709120 | bytes 16785408 | tf_op jit(solution)/shard_map/pallas_call | solution.py:251
  678.1 10.9 collective-permute-done.64
  694.7 16.8 %collective-permute-done.63 = bf16[128,2048]{1,0:T(8,128)(2,1)S(1)} collective-permute-done((bf16[128,2048]{1,0:T(8,128)(2,1)S(1)}, bf16[128,2048]{1,0:T(8,128)(2,1)S(1)}, u32[]{:S(2)}, u32[]{:S(2)}) %collective-permute-start.63) | collective-permute-done | bytes 524320 | tf_op jit(solution)/shard_map/ppermute | solution.py:58
  721.0 12.9 %collective-permute-done.62 = bf16[128,2048]{1,0:T(8,128)(2,1)S(1)} collective-permute-done((bf16[128,2048]{1,0:T(8,128)(2,1)S(1)}, bf16[128,2048]{1,0:T(8,128)(2,1)S(1)}, u32[]{:S(2)}, u32[]{:S(2)}) %collective-permute-start.62) | collective-permute-done | bytes 524320 | tf_op jit(solution)/shard_map/ppermute | solution.py:58
  769.1 12.0 %collective-permute-done.68 = bf16[128,2048]{1,0:T(8,128)(2,1)} collective-permute-done((bf16[128,2048]{1,0:T(8,128)(2,1)}, bf16[128,2048]{1,0:T(8,128)(2,1)}, u32[]{:S(2)}, u32[]{:S(2)}) %collective-permute-start.68) | collective-permute-done | bytes 524320 | tf_op jit(solution)/shard_map/ppermute | solution.py:58
  886.9 27.9 %shard_map.295 = (bf16[2048,2048]{1,0:T(8,128)(2,1)}, bf16[2048,576]{1,0:T(8,128)(2,1)}, bf16[2048,192]{1,0:T(8,128)(2,1)}, bf16[2048,128]{1,0:T(8,128)(2,1)}, b...) custom-call(bf16[2048,2048]{1,0:T(8,128)(2,1)} %constant_dynamic-update-slice_fusion.x_ref, ...), custom_call_target="tpu_custom_call" | custom-call | flops 8589934592 | bytes 41977856 | tf_op jit(solution)/shard_map/pallas_call | solution.py:251
  1038.7 29.2 %collective-permute-done.95 = bf16[16,64,384]{2,1,0:T(8,128)(2,1)} collective-permute-done((bf16[16,64,384]{2,1,0:T(8,128)(2,1)}, bf16[16,64,384]{2,1,0:T(8,128)(2,1)}, u32[]{:S(2)}, u32[]{:S(2)}) %collective-permute-start.95) | collective-permute-done | bytes 786464 | tf_op jit(solution)/shard_map/ppermute | solution.py:403
  1071.6 12.3 %convert_add_fusion = f32[1024,2816]{1,0:T(8,128)} fusion(bf16[1024,2816]{1,0:T(8,128)(2,1)} %collective-permute-done.107, bf16[1024,2048]{1,0:T(8,128)(2,1)} %get-tuple-element.30, bf16[1024,1408]{1,0:T(8,128)(2,1)S(1)} %copy-done.27, bf16[1024,1408]{1,0:T(8,128)(2,1)S(1)} %copy-done.24), kind=kOutput, calls=%fused_computation.2 | convolution fusion | flops 5922881536 | bytes 25165824 | tf_op jit(solution)/shard_map/dot_general | solution.py:33
  1123.9 57.4 %reduce-scatter.2.cloned.1.call-done = bf16[1,80,576]{2,1,0:T(8,128)(2,1)} async-done(((bf16[32,80,576]{2,1,0:T(8,128)(2,1)}), bf16[1,80,576]{2,1,0:T(8,128)(2,1)}) %reduce-scatter.2.cloned.1.call-update) | async-done | bytes 92176 | tf_op jit(solution)/shard_map/reduce_scatter | solution.py:577
  (682 shorter events, 702.3 us)
Async XLA Ops:
  7.2 162.0 %all-gather.4.cloned.1.call-start = ((), (), s32[]{:S(2)}) async-start(), calls=%async_computation.2 | async-start | bytes 3379200 | tf_op jit(solution)/shard_map/all_gather | solution.py:436
  10.2 119.3 %collective-permute-start.3 = (bf16[128,2048]{1,0:T(8,128)(2,1)S(1)}, bf16[128,2048]{1,0:T(8,128)(2,1)}, u32[]{:S(2)}, u32[]{:S(2)}) collective-permute-start(bf16[128,2048]{1,0:T(8,128)(2,1)S(1)} %get-tuple-element.53), channel_id=1, source_target_pairs={{0,2},{1,3},{2,0},{3,1},{4,6},{5,7},{6,4},{7,5},{8,10},{9,11},{10,... | collective-permute-start | bytes 1572872 | tf_op jit(solution)/shard_map/ppermute | solution.py:58
  13.2 39.5 %collective-permute-start = (bf16[128,2048]{1,0:T(8,128)(2,1)S(1)}, bf16[128,2048]{1,0:T(8,128)(2,1)}, u32[]{:S(2)}, u32[]{:S(2)}) collective-permute-start(bf16[128,2048]{1,0:T(8,128)(2,1)S(1)} %get-tuple-element.53), channel_id=1, source_target_pairs={{0,4},{1,5},{2,6},{3,7},{4,8},{5,9},{6,10},{7,11},{8,12},{9,13},{1... | collective-permute-start | bytes 1572872 | tf_op jit(solution)/shard_map/ppermute | solution.py:58
  17.1 1164.1 %reduce-scatter.2.cloned.1.call-start = ((), (), s32[]{:S(2)}) async-start(), calls=%async_computation.1 | async-start | bytes 3379200 | tf_op jit(solution)/shard_map/reduce_scatter | solution.py:577
  20.8 42.3 %collective-permute-start.9 = (bf16[4,2,64,384]{3,2,1,0:T(8,128)(2,1)S(1)}, bf16[4,2,64,384]{3,2,1,0:T(8,128)(2,1)S(1)}, u32[]{:S(2)}, u32[]{:S(2)}) collective-permute-start(bf16[4,2,64,384]{3,2,1,0:T(8,128)(2,1)S(1)} %get-tuple-element.155), channel_id=1, source_target_pairs={{0,1},{1,0},{2,3},{3,2},{4,5},{5,4},{6,7},{7,6},{8,9},{9,8},{10,11... | collective-permute-start | bytes 1179656 | tf_op jit(solution)/shard_map/ppermute | solution.py:58
  104.7 125.4 %collective-permute-start.42 = (bf16[4,2,64,528]{3,2,1,0:T(8,128)(2,1)}, bf16[4,2,64,528]{3,2,1,0:T(8,128)(2,1)}, u32[]{:S(2)}, u32[]{:S(2)}) collective-permute-start(bf16[4,2,64,528]{3,2,1,0:T(8,128)(2,1)} %get-tuple-element.134), channel_id=1, source_target_pairs={{0,1},{1,0},{2,3},{3,2},{4,5},{5,4},{6,7},{7,6},{8,9},{9,8},{10,11... | collective-permute-start | bytes 1622024 | tf_op jit(solution)/shard_map/ppermute | solution.py:58
  245.5 48.9 %collective-permute-start.35 = (bf16[128,2048]{1,0:T(8,128)(2,1)S(1)}, bf16[128,2048]{1,0:T(8,128)(2,1)S(1)}, u32[]{:S(2)}, u32[]{:S(2)}) collective-permute-start(bf16[128,2048]{1,0:T(8,128)(2,1)S(1)} %collective-permute-done.34), channel_id=1, source_target_pairs={{0,4},{1,5},{2,6},{3,7},{4,8},{5,9},{6,10},{7,11},{8,12},{9,13},{1... | collective-permute-start | bytes 1572872 | tf_op jit(solution)/shard_map/ppermute | solution.py:58
  281.7 231.1 %collective-permute-start.48 = (bf16[1024,2816]{1,0:T(8,128)(2,1)}, bf16[1024,2816]{1,0:T(8,128)(2,1)}, u32[]{:S(2)}, u32[]{:S(2)}) collective-permute-start(bf16[1024,2816]{1,0:T(8,128)(2,1)} %get-tuple-element.87), channel_id=1, source_target_pairs={{0,16},{16,0},{1,17},{17,1},{2,18},{18,2},{3,19},{19,3},{4,20},{20... | collective-permute-start | bytes 17301512 | tf_op jit(solution)/shard_map/ppermute | solution.py:403
  331.8 104.2 %collective-permute-start.47 = (bf16[16,64,528]{2,1,0:T(8,128)(2,1)S(1)}, bf16[16,64,528]{2,1,0:T(8,128)(2,1)}, u32[]{:S(2)}, u32[]{:S(2)}) collective-permute-start(bf16[16,64,528]{2,1,0:T(8,128)(2,1)S(1)} %copy-done.15), channel_id=1, source_target_pairs={{0,16},{16,0},{1,17},{17,1},{2,18},{18,2},{3,19},{19,3},{4,20},{20... | collective-permute-start | bytes 3244040 | tf_op jit(solution)/shard_map/ppermute | solution.py:403
  332.3 132.9 %collective-permute-start.40 = (bf16[512,2048]{1,0:T(8,128)(2,1)}, bf16[512,2048]{1,0:T(8,128)(2,1)}, u32[]{:S(2)}, u32[]{:S(2)}) collective-permute-start(bf16[512,2048]{1,0:T(8,128)(2,1)} %pad_maximum_fusion.14), channel_id=1, source_target_pairs={{0,1},{1,0},{2,3},{3,2},{4,5},{5,4},{6,7},{7,6},{8,9},{9,8},{10,11... | collective-permute-start | bytes 6291464 | tf_op jit(solution)/shard_map/ppermute | solution.py:58
  361.4 108.9 %collective-permute-start.41 = (bf16[512,2048]{1,0:T(8,128)(2,1)}, bf16[512,2048]{1,0:T(8,128)(2,1)}, u32[]{:S(2)}, u32[]{:S(2)}) collective-permute-start(bf16[512,2048]{1,0:T(8,128)(2,1)} %pad_maximum_fusion.15), channel_id=1, source_target_pairs={{0,1},{1,0},{2,3},{3,2},{4,5},{5,4},{6,7},{7,6},{8,9},{9,8},{10,11... | collective-permute-start | bytes 6291464 | tf_op jit(solution)/shard_map/ppermute | solution.py:58
  369.4 68.3 %collective-permute-start.24 = (bf16[128,2048]{1,0:T(8,128)(2,1)S(1)}, bf16[128,2048]{1,0:T(8,128)(2,1)}, u32[]{:S(2)}, u32[]{:S(2)}) collective-permute-start(bf16[128,2048]{1,0:T(8,128)(2,1)S(1)} %get-tuple-element.62), channel_id=1, source_target_pairs={{0,4},{1,5},{2,6},{3,7},{4,8},{5,9},{6,10},{7,11},{8,12},{9,13},{1... | collective-permute-start | bytes 1572872 | tf_op jit(solution)/shard_map/ppermute | solution.py:58
  483.2 85.6 %collective-permute-start.49 = (bf16[1408,1024]{1,0:T(8,128)(2,1)}, bf16[1408,1024]{1,0:T(8,128)(2,1)}, u32[]{:S(2)}, u32[]{:S(2)}) collective-permute-start(bf16[1408,1024]{1,0:T(8,128)(2,1)} %bitcast.59), channel_id=1, source_target_pairs={{0,16},{16,0},{1,17},{17,1},{2,18},{18,2},{3,19},{19,3},{4,20},{20... | collective-permute-start | bytes 8650760 | tf_op jit(solution)/shard_map/ppermute | solution.py:403
  613.2 44.8 %collective-permute-start.51 = (bf16[512,2048]{1,0:T(8,128)(2,1)}, bf16[512,2048]{1,0:T(8,128)(2,1)S(1)}, u32[]{:S(2)}, u32[]{:S(2)}) collective-permute-start(bf16[512,2048]{1,0:T(8,128)(2,1)} %get-tuple-element.80), channel_id=1, source_target_pairs={{0,1},{1,0},{2,3},{3,2},{4,5},{5,4},{6,7},{7,6},{8,9},{9,8},{10,11... | collective-permute-start | bytes 6291464 | tf_op jit(solution)/shard_map/ppermute | solution.py:58
  613.7 44.4 %collective-permute-start.50 = (bf16[512,2048]{1,0:T(8,128)(2,1)}, bf16[512,2048]{1,0:T(8,128)(2,1)}, u32[]{:S(2)}, u32[]{:S(2)}) collective-permute-start(bf16[512,2048]{1,0:T(8,128)(2,1)} %get-tuple-element.81), channel_id=1, source_target_pairs={{0,1},{1,0},{2,3},{3,2},{4,5},{5,4},{6,7},{7,6},{8,9},{9,8},{10,11... | collective-permute-start | bytes 6291464 | tf_op jit(solution)/shard_map/ppermute | solution.py:58
  676.0 40.8 %collective-permute-start.54 = (bf16[128,2048]{1,0:T(8,128)(2,1)S(1)}, bf16[128,2048]{1,0:T(8,128)(2,1)S(1)}, u32[]{:S(2)}, u32[]{:S(2)}) collective-permute-start(bf16[128,2048]{1,0:T(8,128)(2,1)S(1)} %get-tuple-element.114), channel_id=1, source_target_pairs={{0,2},{1,3},{2,0},{3,1},{4,6},{5,7},{6,4},{7,5},{8,10},{9,11},{10,... | collective-permute-start | bytes 1572872 | tf_op jit(solution)/shard_map/ppermute | solution.py:58
  693.1 47.0 %collective-permute-start.53 = (bf16[128,2048]{1,0:T(8,128)(2,1)S(1)}, bf16[128,2048]{1,0:T(8,128)(2,1)S(1)}, u32[]{:S(2)}, u32[]{:S(2)}) collective-permute-start(bf16[128,2048]{1,0:T(8,128)(2,1)S(1)} %get-tuple-element.115), channel_id=1, source_target_pairs={{0,2},{1,3},{2,0},{3,1},{4,6},{5,7},{6,4},{7,5},{8,10},{9,11},{10,... | collective-permute-start | bytes 1572872 | tf_op jit(solution)/shard_map/ppermute | solution.py:58
  719.4 38.7 %collective-permute-start.52 = (bf16[128,2048]{1,0:T(8,128)(2,1)}, bf16[128,2048]{1,0:T(8,128)(2,1)}, u32[]{:S(2)}, u32[]{:S(2)}) collective-permute-start(bf16[128,2048]{1,0:T(8,128)(2,1)} %get-tuple-element.112), channel_id=1, source_target_pairs={{0,2},{1,3},{2,0},{3,1},{4,6},{5,7},{6,4},{7,5},{8,10},{9,11},{10,... | collective-permute-start | bytes 1572872 | tf_op jit(solution)/shard_map/ppermute | solution.py:58
  798.1 48.9 %collective-permute-start.73 = (bf16[128,2048]{1,0:T(8,128)(2,1)S(1)}, bf16[128,2048]{1,0:T(8,128)(2,1)S(1)}, u32[]{:S(2)}, u32[]{:S(2)}) collective-permute-start(bf16[128,2048]{1,0:T(8,128)(2,1)S(1)} %collective-permute-done.69), channel_id=1, source_target_pairs={{0,2},{1,3},{2,0},{3,1},{4,6},{5,7},{6,4},{7,5},{8,10},{9,11},{10,... | collective-permute-start | bytes 1572872 | tf_op jit(solution)/shard_map/ppermute | solution.py:58
  806.9 46.9 %collective-permute-start.74 = (bf16[128,2048]{1,0:T(8,128)(2,1)S(1)}, bf16[128,2048]{1,0:T(8,128)(2,1)S(1)}, u32[]{:S(2)}, u32[]{:S(2)}) collective-permute-start(bf16[128,2048]{1,0:T(8,128)(2,1)S(1)} %collective-permute-done.70), channel_id=1, source_target_pairs={{0,2},{1,3},{2,0},{3,1},{4,6},{5,7},{6,4},{7,5},{8,10},{9,11},{10,... | collective-permute-start | bytes 1572872 | tf_op jit(solution)/shard_map/ppermute | solution.py:58
  815.6 44.3 %collective-permute-start.104 = (bf16[2,2,64,528]{3,2,1,0:T(8,128)(2,1)S(1)}, bf16[2,2,64,528]{3,2,1,0:T(8,128)(2,1)S(1)}, u32[]{:S(2)}, u32[]{:S(2)}) collective-permute-start(bf16[2,2,64,528]{3,2,1,0:T(8,128)(2,1)S(1)} %get-tuple-element.121), channel_id=1, source_target_pairs={{0,4},{1,5},{2,6},{3,7},{4,8},{5,9},{6,10},{7,11},{8,12},{9,13},{1... | collective-permute-start | bytes 811016 | tf_op jit(solution)/shard_map/ppermute | solution.py:58
  860.0 69.0 %collective-permute-start.108 = (bf16[1408,1024]{1,0:T(8,128)(2,1)}, bf16[1408,1024]{1,0:T(8,128)(2,1)}, u32[]{:S(2)}, u32[]{:S(2)}) collective-permute-start(bf16[1408,1024]{1,0:T(8,128)(2,1)} %convolution_convert_fusion.2), channel_id=1, source_target_pairs={{0,16},{16,0},{1,17},{17,1},{2,18},{18,2},{3,19},{19,3},{4,20},{20... | collective-permute-start | bytes 8650760 | tf_op jit(solution)/shard_map/ppermute | solution.py:403
  860.9 210.7 %collective-permute-start.107 = (bf16[1024,2816]{1,0:T(8,128)(2,1)}, bf16[1024,2816]{1,0:T(8,128)(2,1)}, u32[]{:S(2)}, u32[]{:S(2)}) collective-permute-start(bf16[1024,2816]{1,0:T(8,128)(2,1)} %convolution_convert_fusion), channel_id=1, source_target_pairs={{0,16},{16,0},{1,17},{17,1},{2,18},{18,2},{3,19},{19,3},{4,20},{20... | collective-permute-start | bytes 17301512 | tf_op jit(solution)/shard_map/ppermute | solution.py:403
  998.3 69.6 %collective-permute-start.95 = (bf16[16,64,384]{2,1,0:T(8,128)(2,1)}, bf16[16,64,384]{2,1,0:T(8,128)(2,1)}, u32[]{:S(2)}, u32[]{:S(2)}) collective-permute-start(bf16[16,64,384]{2,1,0:T(8,128)(2,1)} %slice_bitcast_fusion.6), channel_id=1, source_target_pairs={{0,16},{16,0},{1,17},{17,1},{2,18},{18,2},{3,19},{19,3},{4,20},{20... | collective-permute-start | bytes 2359304 | tf_op jit(solution)/shard_map/ppermute | solution.py:403
  (183 other events, 4756.8 us)
Sparse Core Ops, SparseCore 0:
  17.2 68.0 all-gather.3
  1038.8 142.3 reduce-scatter.1

commit v2 on v0

v2 whole, which is shorter than its diff:
```python
import functools

import jax
import jax.numpy as jnp
from jax import lax
from jax.experimental import pallas as pl
from jax.experimental.pallas import tpu as pltpu
from jax.sharding import PartitionSpec as P

HEADS = 16
HD = 128
RD = 64
VD = 128
LAT = 512
TOP = 6
EPS = 1e-06
CHUNK = 256
SCALE = (HD + RD) ** (-0.5)
BF = jnp.bfloat16
F32 = jnp.float32
VMEM_LIMIT = 60 * 1024 * 1024
Q_COLS = 2 * (HD + RD)
O_COLS = 2 * VD
E_COLS = 128
LAT_AT = Q_COLS
ROT_AT = Q_COLS + LAT
PROJ = ROT_AT + 128
W_COLS = Q_COLS + O_COLS + E_COLS
HIDDEN_TILE = 256


def matmul(left, right):
    return jnp.dot(left, right, preferred_element_type=F32)


def mat_trans(left, right):
    return lax.dot_general(left, right, (((1,), (1,)), ((), ())), preferred_element_type=F32)


def contract(left, right):
    return lax.dot_general(left, right, (((0,), (0,)), ((), ())), preferred_element_type=F32)


def rms_scale(values):
    return lax.rsqrt(jnp.mean(values * values, axis=-1, keepdims=True) + EPS)


def rms_back(incoming, values, scale, gain):
    scaled = incoming * gain
    inner = jnp.mean(scaled * values, axis=-1, keepdims=True)
    grad_in = scale * (scaled - values * scale * scale * inner)
    grad_gain = jnp.sum(incoming * values * scale, axis=0)
    return (grad_in, grad_gain)


def layout(lengths, rows):
    ends = jnp.cumsum(lengths, axis=-1)
    place = jnp.arange(rows, dtype=jnp.int32)
    passed = (place[None, :, None] >= ends[:, None, :]).astype(jnp.int32)
    doc = jnp.sum(passed, axis=-1)
    start = jnp.sum(passed * lengths[:, None, :], axis=-1)
    return ((place[None, :] - start).astype(F32), doc)


def after(value, *others):
    return lax.optimization_barrier((value,) + others)[0]


def low(value):
    return value.astype(BF)


def wide(value):
    return value.astype(F32)


def move(value, to):
    return lax.ppermute(value, "expert", [(i, to(i)) for i in range(16)])


def z_up(value):
    return move(value, lambda i: (i + 4) % 16)


def z_down(value):
    return move(value, lambda i: (i + 12) % 16)


def z_two(value):
    return move(value, lambda i: (i + 8) % 16)


def x_swap(value):
    return move(value, lambda i: i ^ 2)


def core_swap(value):
    return move(value, lambda i: i ^ 1)


class Clock:
    def __init__(self, go):
        self.last = ()
        self.go = go
        self.queue = []

    def add(self, array):
        self.queue.append([array, 0, []])
        return self.queue[-1]

    def next_rows(self, size):
        moves, entries = [], []
        for entry in self.queue:
            array, start, _ = entry
            total = array.shape[0]
            line = array.size // total * array.dtype.itemsize
            count = round(size / line / 32) * 32
            if start == total or count < 64:
                continue
            stop = start + count
            stop = total if total - stop < 64 else stop
            entry[1] = stop
            moves.append((self.go, array[start:stop]))
            entries.append(entry)
            size -= (stop - start) * line
        return moves, entries

    def slot(self, *moves, begin=(), end=(), work=(), feed=0):
        fed, entries = self.next_rows(feed * 1e6)
        moves = fed + list(moves)
        count, late = len(moves), len(moves) + len(begin)
        args, tree = jax.tree.flatten([list(rest) for _, *rest in work])
        values = [value for _, value in moves + list(begin)]
        tied = lax.optimization_barrier(tuple(values + args) + self.last)
        moved = [go(value) for (go, _), value in zip(moves, tied)]
        begun = [go(value) for (go, _), value in zip(begin, tied[count:])]
        args = jax.tree.unflatten(tree, tied[late : late + len(args)])
        made = [job[0](*some) for job, some in zip(work, args)]
        flat, tree = jax.tree.flatten(made)
        self.last = lax.optimization_barrier(tuple(moved) + tuple(end) + tuple(flat))
        moved, ended = list(self.last[:count]), list(self.last[count : count + len(end)])
        for entry in entries:
            entry[2].append(moved.pop(0))
        return moved, begun, ended, jax.tree.unflatten(tree, self.last[count + len(end) :])


    def tie(self, value):
        return lax.optimization_barrier((value,) + self.last)[0]


def joined(entry):
    assert entry[1] == entry[0].shape[0]
    return jnp.concatenate(entry[2], axis=0)


def at(value, index, axis):
    return lax.dynamic_index_in_dim(value, index, axis, keepdims=False)


def whole_call(kernel, args, outs, scratch=(), flops=0, scalars=None):
    size = sum(a.size * a.dtype.itemsize for a in list(args) + list(outs))
    vmem = pl.BlockSpec(memory_space=pltpu.VMEM)
    specs = [vmem] * len(args)
    if scalars is not None:
        args = [scalars] + list(args)
        specs = [pl.BlockSpec(memory_space=pltpu.SMEM)] + specs
    return pl.pallas_call(
        kernel,
        in_specs=specs,
        out_specs=[vmem] * len(outs),
        out_shape=list(outs),
        scratch_shapes=list(scratch),
        compiler_params=pltpu.CompilerParams(vmem_limit_bytes=VMEM_LIMIT),
        cost_estimate=pl.CostEstimate(flops=flops, bytes_accessed=size, transcendentals=0),
    )(*args)


def shaped(shape, kind):
    return jax.ShapeDtypeStruct(shape, kind)


def reorder_kernel(count, parts, index_ref, *refs):
    for in_ref, out_ref in zip(refs[: len(refs) // 2], refs[len(refs) // 2 :]):
        pad = out_ref.shape[2] // parts
        width = in_ref.shape[2] // parts
        for i in range(count):
            value = in_ref[index_ref[i]]
            if pad == width:
                out_ref[i] = value
            else:
                spare = jnp.zeros((value.shape[0], pad - width), value.dtype)
                for part in range(parts):
                    cut = value[:, part * width : (part + 1) * width]
                    out_ref[i, :, part * pad : (part + 1) * pad] = jnp.concatenate([cut, spare], axis=1)


def shared_kernel_in(count, parts, index_ref, *refs):
    in_refs, (both_ref, down_ref) = refs[:-2], refs[-2:]
    pad = down_ref.shape[1]
    for k, in_ref in enumerate(in_refs):
        rows, columns = in_ref.shape[1], in_ref.shape[2] // parts
        spare = jnp.zeros((rows, pad - columns), in_ref.dtype)
        for i in range(count):
            value = in_ref[index_ref[i]]
            line = slice((k * count + i) * rows, (k * count + i + 1) * rows)
            for part in range(parts):
                cut = jnp.concatenate([value[:, part * columns : (part + 1) * columns], spare], axis=1)
                if part < parts - 1:
                    both_ref[line, part * pad : (part + 1) * pad] = cut
                else:
                    down_ref[line, :] = cut


def shared_weights(arrays, index, pad):
    rows = sum(a.shape[0] * a.shape[1] for a in arrays)
    outs = [shaped((rows, 2 * pad), BF), shaped((rows, pad), BF)]
    return whole_call(functools.partial(shared_kernel_in, index.shape[0], 3), arrays, outs, scalars=index)


def reorder(arrays, index, parts=1, pad=0):
    count = index.shape[0]
    outs = [shaped(a.shape[:2] + (a.shape[2] if not pad else parts * pad,), a.dtype) for a in arrays]
    return whole_call(functools.partial(reorder_kernel, count, parts), arrays, outs, scalars=index)


def swap_halves(values):
    lane = lax.broadcasted_iota(jnp.int32, values.shape, 1)
    return jnp.where(
        lane % RD < RD // 2, pltpu.roll(values, 2 * RD - RD // 2, 1), pltpu.roll(values, RD // 2, 1)
    )


def probabilities(q_main, q_rot, k_main, k_rot, allowed):
    scores = (mat_trans(q_main, k_main) + mat_trans(q_rot, k_rot)) * SCALE
    scores = jnp.where(allowed, scores, -1e30)
    expo = jnp.exp(scores - jnp.max(scores, axis=-1, keepdims=True))
    return expo / jnp.sum(expo, axis=-1, keepdims=True)


def allowed_pairs(id_col, id_row):
    shape = (id_col.shape[0], id_row.shape[1])
    key = lax.broadcasted_iota(jnp.int32, shape, 1)
    query = lax.broadcasted_iota(jnp.int32, shape, 0)
    return (id_col == id_row) & (key <= query)


def pair(refs, j):
    pieces, start = [], 0
    for ref in refs:
        low_row, high_row = max(start, CHUNK * j), min(start + ref.shape[0], CHUNK * (j + 1))
        if low_row < high_row:
            pieces.append(ref[low_row - start : high_row - start, :])
        start += ref.shape[0]
    return pieces[0] if len(pieces) == 1 else jnp.concatenate(pieces, axis=0)


def forward_kernel(ndp, layout_of, count, split, place_ref, *refs):
    x_refs, refs = refs[:8], refs[8:]
    w_refs, refs = refs[: len(layout_of)], refs[len(layout_of) :]
    wl_refs, refs = refs[:count], refs[count:]
    we_ref, gain_ref, lg_ref, cos_ref, sin_ref, idc_ref, idr_ref = refs[:7]
    near_ref, far_ref, q_ref, kr_ref, lat_ref, kv_ref, att_ref, wp_ref, wo_ref, exp_ref = refs[7:]
    other_rows = [(ref, i) for ref in wl_refs for i in range(ref.shape[0])]
    dp, z, x, core = place_ref[0], place_ref[1], place_ref[2], place_ref[3]
    block = w_refs[0].shape[1]
    shard = block // 2
    spare = jnp.zeros((shard, 128 - RD), BF)
    turn = 0
    for w_ref, (far, j, first) in zip(w_refs, layout_of):
        y = j ^ dp if ndp == 2 else j
        for k in range(w_ref.shape[0]):
            row = ((y * 4 + lax.rem(z + 4 - first - k, 4)) * 2 + (x ^ far)) * block
            row = pl.multiple_of(row, block)
            wp_ref[pl.ds(row, block), :Q_COLS] = w_ref[k, :, :Q_COLS]
            wo_ref[pl.ds(row, block), :] = w_ref[k, :, Q_COLS : Q_COLS + O_COLS]
            if not split:
                continue
            here = pl.multiple_of(row + core * shard, shard)
            there = pl.multiple_of(row + (1 - core) * shard, shard)
            for at_row, lat in ((here, w_ref[k, :, W_COLS:]), (there, other_rows[turn][0][other_rows[turn][1]])):
                wp_ref[pl.ds(at_row, shard), LAT_AT : LAT_AT + 384] = lat[:shard, :]
                wp_ref[pl.ds(at_row, shard), LAT_AT + 384 :] = lat[shard:, :256]
            turn += 1
            small = shard // 4
            for c in range(2):
                for g in range(4):
                    at_row = pl.multiple_of(row // 4 + c * small, small)
                    exp_ref[pl.ds(at_row, small), g * HD : (g + 1) * HD] = w_ref[
                        k, c * shard + g * small : c * shard + (g + 1) * small, Q_COLS + O_COLS : W_COLS
                    ]
    if not split:
        for i, (wl_ref, _) in enumerate(other_rows):
            wp_ref[i * shard : (i + 1) * shard, LAT_AT:] = jnp.concatenate([wl_ref[i, :shard, :], spare], axis=1)
        exp_ref[...] = we_ref[...]
    gain, lat_gain = gain_ref[...], lg_ref[...]
    for j in range(4):
        rows = slice(CHUNK * j, CHUNK * (j + 1))
        xf = wide(pair(x_refs, j))
        normed = low(xf * rms_scale(xf) * gain)
        proj = matmul(normed, wp_ref[...])
        cosine, sine = cos_ref[rows, :], sin_ref[rows, :]
        q_mix = proj[:, 2 * HD : Q_COLS]
        k_mix = proj[:, ROT_AT:]
        q_rot = low(q_mix * cosine + swap_halves(q_mix) * sine)
        k_rot = k_mix * cosine + swap_halves(k_mix) * sine
        k_turned = low(pltpu.roll(k_rot, RD, 1))
        k_rot = low(k_rot)
        q_main = low(proj[:, : 2 * HD])
        lat = proj[:, LAT_AT:ROT_AT]
        lat_ref[rows, :] = lat
        compressed = low(lat * rms_scale(lat) * lat_gain)
        expanded = low(matmul(compressed, exp_ref[...]))
        q_ref[rows, : 2 * HD] = q_main
        q_ref[rows, 2 * HD :] = q_rot
        kr_ref[rows, :] = k_rot
        kv_ref[rows, :] = expanded
        allowed = allowed_pairs(idc_ref[rows, :], idr_ref[j])
        attended = []
        for head, k_side in ((0, k_rot), (1, k_turned)):
            k_main = expanded[:, 2 * head * HD : (2 * head + 1) * HD]
            values = expanded[:, (2 * head + 1) * HD : (2 * head + 2) * HD]
            probs = probabilities(q_main[:, head * HD : (head + 1) * HD], q_rot, k_main, k_side, allowed)
            attended.append(low(matmul(low(probs), values)))
        attended = jnp.concatenate(attended, axis=1)
        att_ref[rows, :] = attended
        put_half(near_ref, far_ref, j, 4, low(mat_trans(attended, wo_ref[...])))


def put_half(near_ref, far_ref, j, count, value):
    ref = near_ref if j < count // 2 else far_ref
    j = j % (count // 2)
    ref[j * CHUNK : (j + 1) * CHUNK, :] = value


def attention_forward(place, x_pieces, weights, layout_of, w_lat, w_exp, gain, lat_gain, tables, split):
    own, width = x_pieces[0].shape
    rows = 8 * own
    args = list(x_pieces) + list(weights) + list(w_lat) + [w_exp, gain, lat_gain] + list(tables)
    outs = [shaped((rows // 2, width), BF)] * 2 + [
        shaped((rows, Q_COLS), BF),
        shaped((rows, 128), BF),
        shaped((rows, LAT), F32),
        shaped((rows, 4 * HD), BF),
        shaped((rows, O_COLS), BF),
        shaped((width, PROJ), BF),
        shaped((width, O_COLS), BF),
        shaped((LAT, 4 * HD), BF),
    ]
    kernel = functools.partial(forward_kernel, lax.axis_size("dp"), layout_of, len(w_lat), split)
    flops = 2 * rows * width * (PROJ + O_COLS)
    out = whole_call(kernel, args, outs, flops=flops, scalars=place)
    return out[:2], out[2:]


def backward_kernel(count, place_ref, *refs):
    x_refs, g_refs, refs = refs[:8], refs[8 : 8 + count], refs[8 + count :]
    q_ref, kr_ref, lat_ref, kv_ref, att_ref, wp_ref, wo_ref, we_ref, gain_ref, lg_ref = refs[:10]
    cos_ref, sin_ref, idc_ref, idr_ref = refs[10:14]
    dn_ref, dw_ref, dl_ref, de_ref, dg_ref, dlg_ref, acc_q, acc_o, acc_e = refs[14:]
    z, core = place_ref[1], place_ref[3]
    own = x_refs[0].shape[0]
    gain, w_exp, lat_gain = gain_ref[...], we_ref[...], lg_ref[...]

    def add(acc, value, first):
        acc[...] = value if first else acc[...] + value

    for j in range(4):
        rows = slice(CHUNK * j, CHUNK * (j + 1))
        xf = wide(pair(x_refs, j))
        whitened = xf * rms_scale(xf)
        normed = low(whitened * gain)
        lat = lat_ref[rows, :]
        lat_scale = rms_scale(lat)
        white_lat = lat * lat_scale
        grad = pair(g_refs, j)
        cosine, sine = cos_ref[rows, :], sin_ref[rows, :]
        d_att = low(matmul(grad, wo_ref[...]))
        q_rot, k_rot = q_ref[rows, 2 * HD :], kr_ref[rows, :]
        k_turned = low(pltpu.roll(wide(k_rot), RD, 1))
        allowed = allowed_pairs(idc_ref[rows, :], idr_ref[j])
        d_main, d_expanded = [], []
        dq_mix = None
        dk_mix = None
        for head, k_side in ((0, k_rot), (1, k_turned)):
            q_main = q_ref[rows, head * HD : (head + 1) * HD]
            k_main = kv_ref[rows, 2 * head * HD : (2 * head + 1) * HD]
            values = kv_ref[rows, (2 * head + 1) * HD : (2 * head + 2) * HD]
            probs = probabilities(q_main, q_rot, k_main, k_side, allowed)
            d_out = d_att[:, head * HD : (head + 1) * HD]
            d_prob = mat_trans(d_out, values)
            d_values = contract(low(probs), d_out)
            d_scores = low(probs * (d_prob - jnp.sum(probs * d_prob, axis=-1, keepdims=True)))
            d_main.append(matmul(d_scores, k_main) * SCALE)
            d_expanded += [contract(d_scores, q_main) * SCALE, d_values]
            dq_one = matmul(d_scores, k_side)
            dk_one = contract(d_scores, q_rot)
            dq_mix = dq_one if head == 0 else dq_mix + dq_one
            dk_mix = dk_one if head == 0 else dk_mix + pltpu.roll(dk_one, RD, 1)
        dq_mix = dq_mix * SCALE
        dk_mix = dk_mix * SCALE
        dq_mix = dq_mix * cosine - swap_halves(dq_mix) * sine
        dk_mix = dk_mix * cosine - swap_halves(dk_mix) * sine
        dk_mix = jnp.where(lax.broadcasted_iota(jnp.int32, dk_mix.shape, 1) < RD, dk_mix, 0.0)
        d_expanded = low(jnp.concatenate(d_expanded, axis=1))
        d_comp = mat_trans(d_expanded, w_exp)
        scaled = d_comp * lat_gain
        d_lat = lat_scale * (scaled - white_lat * jnp.mean(scaled * white_lat, axis=-1, keepdims=True))
        d_proj = low(jnp.concatenate(d_main + [dq_mix, d_lat, dk_mix], axis=1))
        d_normed = mat_trans(d_proj, wp_ref[...])
        part = low(d_normed)
        for k in range(2):
            piece = 2 * j + k
            place = lax.rem(z + 4 - piece % 4, 4) * 2 + (core ^ (piece // 4))
            dn_ref[pl.ds(pl.multiple_of(place * own, own), own), :] = part[k * own : (k + 1) * own, :]
        add(dg_ref, jnp.sum(d_normed * whitened, axis=0, keepdims=True), j == 0)
        add(dlg_ref, jnp.sum(d_comp * white_lat, axis=0, keepdims=True), j == 0)
        add(acc_q, contract(d_proj, normed), j == 0)
        add(acc_o, contract(att_ref[rows, :], grad), j == 0)
        add(acc_e, contract(low(white_lat * lat_gain), d_expanded), j == 0)
    dw_ref[:, :Q_COLS] = low(acc_q[:Q_COLS, :].T)
    dw_ref[:, Q_COLS:] = low(acc_o[...].T)
    dl_ref[...] = low(acc_q[Q_COLS:, :].T)
    de_ref[...] = low(acc_e[...])


def attention_backward(place, x_pieces, g_pieces, saved, gain, lat_gain, tables):
    own, width = x_pieces[0].shape
    q, kr, lat, kv, att, wp, wo, w_exp = saved
    args = list(x_pieces) + list(g_pieces) + [q, kr, lat, kv, att, wp, wo, w_exp, gain, lat_gain] + list(tables)
    outs = [
        shaped((8 * own, width), BF),
        shaped((width, Q_COLS + O_COLS), BF),
        shaped((width, PROJ - Q_COLS), BF),
        shaped((LAT, 4 * HD), BF),
        shaped((1, width), F32),
        shaped((1, LAT), F32),
    ]
    scratch = (
        pltpu.VMEM((PROJ, width), F32), pltpu.VMEM((O_COLS, width), F32), pltpu.VMEM((LAT, 4 * HD), F32)
    )
    flops = 2 * 8 * own * width * (2 * PROJ + 2 * O_COLS)
    kernel = functools.partial(backward_kernel, len(g_pieces))
    return whole_call(kernel, args, outs, scratch, flops=flops, scalars=place)


def enter_grad_kernel(slots, *refs):
    g_refs, (target_ref, gate_ref, rg0_ref, rg1_ref, rs_ref) = refs[:-5], refs[-5:]
    half = rg0_ref.shape[1]
    for j in range(8):
        grad = pair(g_refs, j)
        chosen = lax.broadcasted_iota(jnp.int32, (slots, CHUNK), 0) == target_ref[j]
        share = jnp.sum(jnp.where(chosen, gate_ref[j], 0.0), axis=1, keepdims=True)
        rs_ref[j * slots : (j + 1) * slots, :] = share
        value = low(matmul(low(chosen), grad) * share)
        rg0_ref[j * slots : (j + 1) * slots, :] = value[:, :half]
        rg1_ref[j * slots : (j + 1) * slots, :] = value[:, half:]


def dispatch_kernel(slots, *refs):
    t_refs, (target_ref, rx0_ref, rx1_ref) = refs[:-3], refs[-3:]
    half = rx0_ref.shape[1]
    for j in range(8):
        chosen = lax.broadcasted_iota(jnp.int32, (slots, CHUNK), 0) == target_ref[j]
        value = low(matmul(low(chosen), pair(t_refs, j)))
        rx0_ref[j * slots : (j + 1) * slots, :] = value[:, :half]
        rx1_ref[j * slots : (j + 1) * slots, :] = value[:, half:]


def hidden_shared_kernel(*refs):
    t_refs, (sgu_ref, da_ref, act_ref, pre_ref) = refs[:-4], refs[-4:]
    third = sgu_ref.shape[1] // 2
    for j in range(8):
        rows = slice(j * CHUNK, (j + 1) * CHUNK)
        both = matmul(pair(t_refs, j), sgu_ref[...])
        gate_pre, up = both[:, :third], both[:, third:]
        d_act = da_ref[rows, :]
        sigma = jax.nn.sigmoid(gate_pre)
        swish = gate_pre * sigma
        act_ref[rows, :] = low(swish * up)
        pre_ref[rows, :third] = low(d_act * up * (sigma * (1.0 + gate_pre * (1.0 - sigma))))
        pre_ref[rows, third:] = low(d_act * swish)


def enter_grad(g_pieces, target, gate, slots):
    own, width = g_pieces[0].shape
    args = list(g_pieces) + [target, gate]
    outs = [shaped((slots, width // 2), BF)] * 2 + [shaped((slots, 1), F32)]
    flops = 32 * own * width * (slots // 8)
    return whole_call(functools.partial(enter_grad_kernel, slots // 8), args, outs, flops=flops)


def dispatch(t_pieces, target, slots):
    own, width = t_pieces[0].shape
    args = list(t_pieces) + [target]
    outs = [shaped((slots, width // 2), BF)] * 2
    flops = 32 * own * width * (slots // 8)
    return whole_call(functools.partial(dispatch_kernel, slots // 8), args, outs, flops=flops)


def shared_grad_in_kernel(*refs):
    g_refs, (sd_ref, da_ref) = refs[:-2], refs[-2:]
    for j in range(8):
        da_ref[j * CHUNK : (j + 1) * CHUNK, :] = matmul(pair(g_refs, j), sd_ref[...])


def hidden_shared(t_pieces, g_pieces, s_both, s_down):
    own, width = t_pieces[0].shape
    third = s_down.shape[1]
    flops = 32 * own * width * third
    d_act = whole_call(
        shared_grad_in_kernel, list(g_pieces) + [s_down], [shaped((16 * own, third), F32)], flops=flops
    )[0]
    args = list(t_pieces) + [s_both, d_act]
    outs = [shaped((16 * own, third), BF), shaped((16 * own, 2 * third), BF)]
    return whole_call(hidden_shared_kernel, args, outs, flops=2 * flops)


def hidden_kernel(x0_ref, x1_ref, r0_ref, r1_ref, g0_ref, g1_ref, u0_ref, u1_ref, d0_ref, d1_ref, act_ref, dg_ref, du_ref):
    step = 256
    for j in range(x0_ref.shape[0] // step):
        rows = slice(j * step, (j + 1) * step)
        x0, x1 = x0_ref[rows, :], x1_ref[rows, :]
        gate = matmul(x0, g0_ref[...]) + matmul(x1, g1_ref[...])
        up = matmul(x0, u0_ref[...]) + matmul(x1, u1_ref[...])
        d_act = mat_trans(r0_ref[rows, :], d0_ref[...]) + mat_trans(r1_ref[rows, :], d1_ref[...])
        sigma = jax.nn.sigmoid(gate)
        swish = gate * sigma
        act_ref[rows, :] = low(swish * up)
        dg_ref[rows, :] = low(d_act * up * (sigma * (1.0 + gate * (1.0 - sigma))))
        du_ref[rows, :] = low(d_act * swish)


def tiled_call(kernel, steps, args, specs, outs, out_specs, scratch=(), flops=0, aliases=None):
    size = sum(a.size * a.dtype.itemsize for a in list(args) + list(outs))
    return pl.pallas_call(
        kernel,
        grid=(steps,),
        in_specs=specs,
        out_specs=out_specs,
        out_shape=outs,
        scratch_shapes=list(scratch),
        input_output_aliases=aliases or {},
        compiler_params=pltpu.CompilerParams(vmem_limit_bytes=VMEM_LIMIT),
        cost_estimate=pl.CostEstimate(flops=flops, bytes_accessed=size, transcendentals=0),
    )(*args)


def whole_spec(array):
    return pl.BlockSpec(array.shape, lambda i: (0,) * array.ndim)


def expert_hidden(rows_x, rows_g, own, other):
    slots, half = rows_x[0].shape
    hidden = own[0].shape[1]
    tile = HIDDEN_TILE
    by_column = pl.BlockSpec((half, tile), lambda i: (0, i))
    by_row = pl.BlockSpec((tile, half), lambda i: (i, 0))
    args = list(rows_x) + list(rows_g) + [own[0], other[0], own[1], other[1], own[2], other[2]]
    specs = [whole_spec(value) for value in args[:4]] + [by_column] * 4 + [by_row] * 2
    outs = [shaped((slots, hidden), BF)] * 3
    out_specs = [pl.BlockSpec((slots, tile), lambda i: (0, i))] * 3
    flops = 12 * slots * half * hidden
    return tiled_call(hidden_kernel, -(-hidden // tile), args, specs, outs, out_specs, flops=flops)


def back_kernel(per, dg_ref, du_ref, g0_ref, g1_ref, u0_ref, u1_ref, target_ref, left_ref, right_ref, near_ref, far_ref, rows_ref):
    steps = pl.num_programs(0) // 2
    own = pl.program_id(0) < steps

    @pl.when(own)
    def _():
        rows_ref[...] = low(mat_trans(dg_ref[...], g0_ref[...]) + mat_trans(du_ref[...], u0_ref[...]))

    @pl.when(jnp.logical_not(own))
    def _():
        rows_ref[...] = low(mat_trans(dg_ref[...], g1_ref[...]) + mat_trans(du_ref[...], u1_ref[...]))

    right = right_ref[...]
    for j in range(8):
        hot = low(lax.broadcasted_iota(jnp.int32, (CHUNK, per), 1) == target_ref[j * CHUNK : (j + 1) * CHUNK, :])
        out = matmul(hot, rows_ref[j * per : (j + 1) * per, :])
        put_half(near_ref, far_ref, j, 8, low(out + mat_trans(left_ref[j * CHUNK : (j + 1) * CHUNK, :], right)))


def expert_back(d_gate, d_up, own, other, target, left, right):
    slots, hidden = d_gate.shape
    rows, columns = left.shape
    width = right.shape[0]
    tile = 256
    steps = width // tile // 2
    near = pl.BlockSpec((tile, hidden), lambda i: (jnp.minimum(i, steps - 1), 0))
    far = pl.BlockSpec((tile, hidden), lambda i: (jnp.maximum(i - steps, 0), 0))
    args = [d_gate, d_up, own[0], other[0], own[1], other[1], target, left, right]
    specs = [whole_spec(d_gate), whole_spec(d_up)] + [near, far] * 2
    specs += [whole_spec(target), whole_spec(left), pl.BlockSpec((tile, columns), lambda i: (i, 0))]
    outs = [shaped((rows // 2, width), BF)] * 2
    out_specs = [pl.BlockSpec((rows // 2, tile), lambda i: (0, i))] * 2
    flops = 4 * slots * width * hidden + 2 * rows * width * (columns + slots // 8)
    return tiled_call(
        functools.partial(back_kernel, slots // 8), 2 * steps, args, specs, outs, out_specs,
        (pltpu.VMEM((slots, tile), BF),), flops=flops,
    )


def out_kernel(per, index_ref, act_ref, share_ref, d0_ref, d1_ref, target_ref, left_ref, right_ref, out_ref, rows_ref):
    steps = pl.num_programs(0) // 2
    own = pl.program_id(0) < steps

    @pl.when(own)
    def _():
        rows_ref[...] = low(matmul(act_ref[...], d0_ref[...]) * share_ref[...])

    @pl.when(jnp.logical_not(own))
    def _():
        rows_ref[...] = low(matmul(act_ref[...], d1_ref[...]) * share_ref[...])

    right = right_ref[...]
    piece = CHUNK // 2
    for j in range(8):
        hot = low(lax.broadcasted_iota(jnp.int32, (CHUNK, per), 1) == target_ref[j * CHUNK : (j + 1) * CHUNK, :])
        out = matmul(hot, rows_ref[j * per : (j + 1) * per, :])
        out = low(out + mat_trans(left_ref[j * CHUNK : (j + 1) * CHUNK, :], right))
        for k in range(2):
            row = pl.multiple_of(index_ref[2 * j + k] * piece, piece)
            out_ref[pl.ds(row, piece), :] = out[k * piece : (k + 1) * piece, :]


def expert_out(act, share, own, other, target, left, right, index):
    slots, hidden = act.shape
    rows, columns = left.shape
    width = right.shape[0]
    tile = 256
    steps = width // tile // 2
    args = [index, act, share, own[2], other[2], target, left, right]
    specs = [
        pl.BlockSpec(memory_space=pltpu.SMEM), whole_spec(act), whole_spec(share),
        pl.BlockSpec((hidden, tile), lambda i: (0, jnp.minimum(i, steps - 1))),
        pl.BlockSpec((hidden, tile), lambda i: (0, jnp.maximum(i - steps, 0))),
        whole_spec(target), whole_spec(left), pl.BlockSpec((tile, columns), lambda i: (i, 0)),
    ]
    outs = [shaped((rows, width), BF)]
    out_specs = [pl.BlockSpec((rows, tile), lambda i: (0, i))]
    flops = 2 * slots * width * hidden + 2 * rows * width * (columns + slots // 8)
    return tiled_call(
        functools.partial(out_kernel, slots // 8), 2 * steps, args, specs, outs, out_specs,
        (pltpu.VMEM((slots, tile), BF),), flops=flops,
    )[0]


def shared_kernel(part, count, *refs):
    t_refs, g_refs, (pre_ref, act_ref, out_ref, acc_t, acc_g) = refs[:count], refs[count:-5], refs[-5:]
    pad = act_ref.shape[1]
    for j in range(8):
        rows = slice(j * CHUNK, (j + 1) * CHUNK)
        by_tok = contract(pre_ref[rows, :], pair(t_refs, j))
        by_grad = contract(act_ref[rows, :], pair(g_refs, j))
        acc_t[...] = by_tok if j == 0 else acc_t[...] + by_tok
        acc_g[...] = by_grad if j == 0 else acc_g[...] + by_grad
    parts = [acc_t[:part, :], acc_t[pad : pad + part, :], acc_g[:part, :]]
    spare = -3 * part % 128
    if spare:
        parts.append(jnp.zeros((spare, acc_t.shape[1]), F32))
    out_ref[...] = low(jnp.concatenate(parts, axis=0).T[:, : 3 * part])


def shared_gradient(t_pieces, g_pieces, pre, act, part):
    own, width = t_pieces[0].shape
    args = list(t_pieces) + list(g_pieces) + [pre, act]
    outs = [shaped((width, 3 * part), BF)]
    scratch = (pltpu.VMEM((pre.shape[1], width), F32), pltpu.VMEM((act.shape[1], width), F32))
    flops = 32 * own * width * (pre.shape[1] + act.shape[1])
    return whole_call(functools.partial(shared_kernel, part, len(t_pieces)), args, outs, scratch, flops=flops)[0]


def local(
    tokens, lengths, routes, gates, norm_in, latent_gain, norm_mid, w_query, w_latent, w_expand, w_output,
    shared_gate, shared_up, shared_down, expert_gate, expert_up, expert_down, cotangent,
):
    micro = lengths.shape[0]
    own_rows, width = tokens.shape
    rows = own_rows // micro
    experts = lax.axis_size("expert")
    ndp = lax.axis_size("dp")
    two = ndp == 2
    cap = rows * TOP * 4 // (3 * experts)
    blocks = experts * micro
    all_rows = experts * own_rows
    devices = ndp * experts
    shard = width // devices
    lat_rows = w_expand.shape[0]
    lat_cols = w_latent.shape[1]
    ff_s = shared_gate.shape[1]
    ff_part = ff_s // experts
    ff_pad = -(-ff_part // 128) * 128
    half = width // 2
    me = lax.axis_index("expert")
    dp = lax.axis_index("dp")
    core, x, z = me % 2, (me // 2) % 2, me // 4
    scalars = jnp.stack([dp, z, x, core]).astype(jnp.int32)

    def turn(value):
        if not two:
            return value
        swapped = jnp.concatenate([value[..., half:], value[..., :half]], axis=-1)
        return jnp.where(dp == 1, swapped, value)

    def dp_swap(value):
        return lax.ppermute(value, "dp", [(0, 1), (1, 0)])

    clock = Clock(dp_swap)

    def lane(value):
        return [(dp_swap, value)] if two else []

    def dp_gather(value, axis):
        return lax.all_gather(value, "dp", axis=axis, tiled=True)

    def dp_scatter(value, axis=0):
        return lax.psum_scatter(value, "dp", scatter_dimension=axis, tiled=True)

    def cut(value, k):
        return value[k * own_rows : (k + 1) * own_rows]

    number = jnp.arange(experts, dtype=jnp.int32)
    near_z, near_x, near_c = number % 4, (number // 4) % 2, number // 8
    row_index = ((z + 4 - near_z) % 4) * 4 + (near_x ^ x) * 2 + (near_c ^ core)
    few_index = jnp.concatenate([row_index[:4], row_index[8:12]])
    n_z, n_x, n_c = number // 4, (number // 2) % 2, number % 2
    block_index = ((z + 4 - n_z) % 4) * 4 + (n_x ^ x) * 2 + (n_c ^ core)

    pairs = HEADS // 2
    groups = shard // lat_rows
    piece = w_query.reshape(shard, pairs, 2, HD + RD).transpose(1, 0, 2, 3)
    piece = jnp.concatenate(
        [
            piece[..., :HD].reshape(pairs, shard, 2 * HD),
            piece[..., HD:].reshape(pairs, shard, 2 * RD),
            w_output.reshape(pairs, O_COLS, shard).transpose(0, 2, 1),
            w_expand.reshape(lat_rows, pairs, groups, E_COLS).transpose(1, 2, 0, 3).reshape(pairs, shard, E_COLS),
        ],
        axis=2,
    )
    piece = piece.reshape(4, 2, shard, W_COLS)
    kept, away = at(piece, core, 1), at(piece, 1 - core, 1)

    by_expert = jnp.sum(jnp.where(routes.T[None] == number[:, None, None], gates.T[None], 0.0), axis=1)
    gate_high = low(by_expert)
    gate_low = low(by_expert - wide(gate_high))

    def as_row(value):
        return jnp.pad(value.reshape(1, -1), ((0, 0), (0, own_rows - value.size)))

    small = [as_row(norm_in), as_row(norm_mid), as_row(latent_gain), as_row(low(lengths)), gate_high, gate_low]
    small = jnp.concatenate(small, axis=0)
    small_rows = 48
    small = jnp.pad(small, ((0, small_rows - small.shape[0]), (0, 0)))

    s_piece = jnp.concatenate(
        [
            shared_gate.reshape(shard, experts, ff_part).transpose(1, 0, 2),
            shared_up.reshape(shard, experts, ff_part).transpose(1, 0, 2),
            shared_down.reshape(experts, ff_part, shard).transpose(0, 2, 1),
        ],
        axis=2,
    ).reshape(4, 2, 2, shard, 3 * ff_part)
    own_expert = (expert_gate[0], expert_up[0], expert_down[0])
    x0 = tokens
    g0 = low(turn(cotangent))

    if two:
        fetched = [clock.add(value) for value in (own_expert[2], own_expert[0], own_expert[1])]
        wide_lat = jnp.pad(w_latent, ((0, 0), (0, 640 - lat_cols)))
        low_rows = jnp.pad(small, ((0, shard - small_rows), (0, 0)))
        lat = jnp.concatenate([wide_lat[:, :384], jnp.concatenate([wide_lat[:, 384:], low_rows], axis=1)], axis=0)
    else:
        lat = small
    moved, _, _, _ = clock.slot((core_swap, away), (z_two, lat), (z_up, lat), (z_down, lat), (z_up, x0))
    x1 = moved[4]
    lats = jnp.stack([lat, moved[2], moved[1], moved[3]])
    facts = lats[:, shard : shard + small_rows, 256:] if two else lats
    w_own = jnp.where(
        core == 0, jnp.concatenate([kept, moved[0]], axis=1), jnp.concatenate([moved[0], kept], axis=1)
    )
    moved, _, _, _ = clock.slot(
        (z_two, at(w_own, (z + 2) % 4, 0)),
        (z_up, at(w_own, (z + 1) % 4, 0)),
        (z_down, at(w_own, (z + 3) % 4, 0)),
        (core_swap, facts),
        feed=0.75,
    )
    w_own = jnp.stack([at(w_own, z, 0), moved[1], moved[0], moved[2]])
    facts_few = jnp.concatenate([facts, moved[3]])
    if two:
        w_own = jnp.concatenate([w_own, lats], axis=2)
    s_kept, s_away = at(s_piece, core, 2), at(s_piece, 1 - core, 2)

    def tables_of(facts):
        lengths_few = facts[:, 3, : lengths.size].astype(jnp.int32).reshape(8 * micro, lengths.shape[1])
        position, doc = layout(lengths_few, rows)
        freq = jnp.power(10000.0, -2.0 * jnp.arange(RD // 2, dtype=F32) / RD)
        theta = position.reshape(-1, 1) * freq
        cosine, sine = jnp.cos(theta), jnp.sin(theta)
        cosine = jnp.concatenate([cosine] * 4, axis=1)
        sine = jnp.concatenate([-sine, sine, -sine, sine], axis=1)
        ids = doc + 4 * jnp.arange(8 * micro, dtype=jnp.int32)[:, None]
        return cosine, sine, ids.reshape(-1, 1), ids.reshape(-1, 1, CHUNK)

    moved, _, _, made = clock.slot(
        (x_swap, w_own), (z_up, x1), (z_up, g0), *lane(w_own), (core_swap, x0), work=[(tables_of, facts_few)]
    )
    tables = made[0]
    w_x, x2, g1 = moved[:3]
    cx0 = moved[-1]
    if two:
        w_y = moved[3]
        lat_near = jnp.concatenate([lats, w_x[..., W_COLS:], w_y[..., W_COLS:]])
        moved, _, _, _ = clock.slot(
            (x_swap, w_y[:2]), (dp_swap, w_x[2:]), (z_up, x2), (core_swap, x1), (core_swap, lat_near)
        )
        w_far, x3, cx1, lat_other = moved[:2], *moved[2:]
        lat_far = jnp.concatenate([w_far[0][..., W_COLS:], w_far[1][..., W_COLS:]])
        device = jnp.arange(devices, dtype=jnp.int32)
        place = (device // 2 % 2 ^ x) + 2 * (device // 16 ^ dp)
        place = (device % 2 ^ core) * 16 + place * 4 + (z + 4 - device // 4 % 4) % 4
        moved, _, _, _ = clock.slot((core_swap, lat_far), (core_swap, x3), (core_swap, x2), feed=0.35)
        cx3, cx2 = moved[1:]
        weights = [w_own, w_x, w_y] + w_far
        layout_of = ((0, 0, 0), (1, 0, 0), (0, 1, 0), (1, 1, 0), (1, 1, 2))
        w_lat = [lat_other, moved[0]]
        every = [lat_near, lat_far, lat_other, moved[0]]
        facts = reorder([jnp.concatenate([part[:, shard : shard + 16, 256:] for part in every])], place)[0]
        gain_in = wide(facts[:, 0, :shard]).reshape(1, width)
        gain_lat = wide(facts[:, 2, :lat_rows]).reshape(1, LAT)
        w_exp = gain_lat
    else:
        x3 = z_up(x2)
        cx1, cx2, cx3 = core_swap(x1), core_swap(x2), core_swap(x3)
        near, far = dp_gather(w_own[None], 0), dp_gather(w_x[None], 0)
        weights = [near[i] for i in range(ndp)] + [far[i] for i in range(ndp)]
        layout_of = tuple((side, j, 0) for side in range(2) for j in range(ndp))
        w_lat = lax.all_gather(w_latent, ("dp", "expert"), axis=0)
        w_lat = [w_lat[i][None] for i in range(devices)]
        facts = lax.all_gather(small, ("dp", "expert"), axis=0)
        w_exp = jnp.concatenate([value[..., Q_COLS + O_COLS :] for value in weights], axis=0)
        w_exp = w_exp.reshape(2, ndp, 4, 2 * shard, E_COLS).transpose(1, 2, 0, 3, 4)
        w_exp = w_exp.reshape(devices // 2, -1, E_COLS)
        chips = jnp.arange(devices // 2, dtype=jnp.int32)
        chip_index = chips // 8 * 8 + ((z + 4 - chips // 2 % 4) % 4) * 2 + (chips % 2 ^ x)
        w_exp = reorder([w_exp], chip_index)[0]
        w_exp = w_exp.reshape(devices, groups, lat_rows, E_COLS).transpose(0, 2, 1, 3).reshape(LAT, groups * E_COLS)
        gain_in = wide(facts[:, 0, :shard]).reshape(1, width)
        gain_lat = wide(facts[:, 2, :lat_rows]).reshape(1, LAT)
        every = None

    def facts_of(facts, every):
        if two:
            facts = reorder([jnp.concatenate([part[:, shard : shard + small_rows, 256:] for part in every])], place)[0]
        return facts, wide(facts[:, 1, :shard]).reshape(1, width)

    def routing_of(facts):
        group = wide(lax.dynamic_slice_in_dim(facts, dp * experts, experts, 0))
        gate_all = group[:, 4 : 4 + 2 * experts].reshape(experts, 2, experts, own_rows)
        gate_all = jnp.take(at(gate_all, me, 2).sum(axis=1), row_index, axis=0).reshape(blocks, rows)
        routed = (gate_all > 0.0).astype(jnp.int32)
        in_chunk = jnp.arange(blocks, dtype=jnp.int32)[:, None] % (CHUNK // rows)
        target = jnp.where(routed > 0, in_chunk * cap + jnp.cumsum(routed, axis=1) - 1, -1)
        return target.reshape(all_rows, 1), target.reshape(-1, 1, CHUNK), gate_all.reshape(-1, 1, CHUNK)

    def small_facts(facts, every):
        facts, gain_mid = facts_of(facts, every)
        return routing_of(facts) + (gain_mid,)

    x_pieces = [x0, x1, x2, x3, cx0, cx1, cx2, cx3]
    moved, _, _, made = clock.slot(
        (x_swap, g0), (z_up, g1), (core_swap, s_away),
        feed=0.9,
        work=[
            (
                lambda *a: attention_forward(*a[:3], layout_of, *a[3:], split=two),
                scalars, x_pieces, weights, w_lat, w_exp, gain_in, gain_lat, tables,
            )
        ],
    )
    gx0, g2 = moved[:2]
    s_piece = jnp.stack([s_kept, moved[2]], axis=2)
    (part_near, part_far), saved = made[0]

    s_kept, s_away = at(s_piece, x, 1), at(s_piece, 1 - x, 1)
    moved, _, _, _ = clock.slot((core_swap, part_far), (z_up, g2), (x_swap, g1), feed=0.6)
    g3, gx1 = moved[1:]
    g_near = jnp.concatenate([g0, g1, g2, g3])
    terms = [wide(cut(part_near, k)) + wide(cut(moved[0], k)) for k in range(4)]
    moved, _, _, made = clock.slot(
        (z_down, low(terms[3])), (x_swap, g2), work=[(small_facts, facts, every)], feed=0.67
    )
    gx2 = moved[1]
    target_col, target_row, gate_row, gain_mid = made[0]
    moved, _, _, _ = clock.slot(
        (z_down, low(terms[2] + wide(moved[0]))), (x_swap, g3), (core_swap, g_near), feed=0.67
    )
    gx3, cg_near = moved[1:]
    moved, _, _, _ = clock.slot((z_down, low(terms[1] + wide(moved[0]))), (x_swap, s_away), feed=0.67)
    s_piece = jnp.stack([s_kept, moved[1]], axis=1)
    xf = wide(tokens)
    mid = xf + terms[0] + wide(moved[0])
    scale_mid = rms_scale(mid)
    t0 = turn(low(mid * scale_mid * gain_mid))

    slots = blocks * cap
    g_far = jnp.concatenate([gx0, gx1, gx2, gx3])
    moved, _, _, _ = clock.slot((z_up, t0), (x_swap, t0), feed=0.67)
    t1, tx0 = moved
    moved, _, _, _ = clock.slot((z_up, t1), (x_swap, t1), (core_swap, g_far), feed=0.67)
    t2, tx1, cg_far = moved
    g_pieces = [g0, g1, g2, g3, gx0, gx1, gx2, gx3, cg_near, cg_far]
    moved, _, _, made = clock.slot(
        (z_up, t2), (x_swap, t2),
        feed=0.67,
        work=[(functools.partial(enter_grad, slots=slots), g_pieces, target_row, gate_row)],
    )
    t3, tx2 = moved
    *rows_g, share = made[0]
    t_near = jnp.concatenate([t0, t1, t2, t3])
    moved, s_begun, _, _ = clock.slot(
        (x_swap, t3), (core_swap, t_near), begin=[(z_two, at(s_piece, (z + 2) % 4, 0))], feed=0.67
    )
    tx3, ct_near = moved
    t_far = jnp.concatenate([tx0, tx1, tx2, tx3])
    moved, more, _, _ = clock.slot(
        (core_swap, t_far),
        begin=[(z_up, at(s_piece, (z + 1) % 4, 0)), (z_down, at(s_piece, (z + 3) % 4, 0))],
        feed=0.67,
    )
    t_pieces = [t0, t1, t2, t3, tx0, tx1, tx2, tx3, ct_near, moved[0]]

    _, _, ended, made = clock.slot(
        end=more + s_begun, work=[(functools.partial(dispatch, slots=slots), t_pieces, target_row)], feed=2.0
    )
    rows_x = made[0]
    s_piece = jnp.stack([at(s_piece, z, 0), ended[0], ended[2], ended[1]]).reshape(experts, shard, 3 * ff_part)
    if two:
        own, other = own_expert, [joined(fetched[i]) for i in (1, 2, 0)]
    else:
        full = [dp_gather(own_expert[0], 0), dp_gather(own_expert[1], 0), dp_gather(own_expert[2], 1)]
        own = [full[0][:half], full[1][:half], full[2][:, :half]]
        other = [full[0][half:], full[1][half:], full[2][:, half:]]
    s_got, _, _, made = clock.slot(*lane(s_piece), work=[(expert_hidden, rows_x, rows_g, own, other)])
    e_act, d_gate, d_up = made[0]
    s_pieces = [s_piece, s_got[0]] if two else jnp.split(dp_gather(s_piece[None], 0), ndp)
    s_pieces = [value.reshape(s_piece.shape) for value in s_pieces]
    _, _, _, made = clock.slot(work=[(contract, e_act, rows_g[1])])
    if two:
        sent = [clock.add(low(made[0]))]

    _, _, _, made = clock.slot(
        feed=0.2, work=[(lambda *a: shared_weights(a, block_index, ff_pad), *s_pieces)]
    )
    s_both, s_down = made[0]
    _, _, _, made = clock.slot(work=[(hidden_shared, t_pieces, g_pieces, s_both, s_down)], feed=0.8)
    s_act, d_s_pre = made[0]
    _, _, _, made = clock.slot(
        work=[(expert_back, d_gate, d_up, own, other, target_col, d_s_pre, s_both)], feed=1.3
    )
    near, far = made[0]
    quads = 4 * own_rows
    moved, _, _, made = clock.slot((core_swap, far[quads:]), work=[(contract, rows_x[1], d_gate)], feed=0.25)
    if two:
        sent.append(clock.add(low(made[0])))
    away = [low(wide(cut(near[quads:], k)) + wide(cut(moved[0], k))) for k in range(4)]
    moved, _, _, made = clock.slot(
        (x_swap, away[3]), (core_swap, far[:quads]), work=[(contract, rows_x[1], d_up)], feed=0.65
    )
    if two:
        sent.append(clock.add(low(made[0])))
    home = [wide(cut(near, k)) + wide(cut(moved[1], k)) for k in range(4)]
    moved, _, _, made = clock.slot(
        (x_swap, away[2]), (z_down, low(home[3] + wide(moved[0]))),
        feed=0.85,
        work=[(expert_out, e_act, share, own, other, target_col, s_act, s_down, row_index)],
    )
    out_part = made[0]
    moved, _, _, made = clock.slot(
        (x_swap, away[1]), (z_down, low(home[2] + wide(moved[0]) + wide(moved[1]))),
        work=[(contract, e_act, rows_g[0])], feed=0.65,
    )
    d_down_home = made[0]
    moved, _, _, made = clock.slot(
        (x_swap, away[0]), (z_down, low(home[1] + wide(moved[0]) + wide(moved[1]))),
        work=[(contract, rows_x[0], d_gate)], feed=0.65,
    )
    d_gate_home = made[0]
    out_sum = lax.psum_scatter(clock.tie(out_part), "expert", scatter_dimension=0, tiled=True)
    d_mid_normed = turn(home[0] + wide(moved[0]) + wide(moved[1]))
    d_mid_in, d_gain_mid = rms_back(d_mid_normed, mid, scale_mid, gain_mid)
    d_mid = cotangent + d_mid_in

    a0 = low(d_mid)
    moved, _, _, made = clock.slot(
        (z_up, a0),
        feed=0.7,
        work=[(functools.partial(shared_gradient, part=ff_part), t_pieces, g_pieces, d_s_pre, s_act)],
    )
    a1 = moved[0]
    d_shared = made[0].reshape(ndp, experts, shard, 3 * ff_part)
    part = experts // 2
    moved, _, _, made = clock.slot((z_up, a1), *lane(d_shared[1, :part]), work=[(contract, rows_x[0], d_up)])
    a2, s_got = moved[0], moved[1:]
    d_up_home = made[0]
    moved, _, _, _ = clock.slot((z_up, a2), *lane(d_shared[1, part:]))
    a3 = moved[0]
    if two:
        d_shared = low(wide(d_shared[0]) + wide(jnp.concatenate([s_got[0], moved[1]])))
    else:
        d_shared = dp_scatter(d_shared)[0]
    d_shared = d_shared.reshape(4, 2, 2, shard, 3 * ff_part)
    a_near = jnp.concatenate([a0, a1, a2, a3])
    moved, _, _, _ = clock.slot((core_swap, a_near), feed=0.25)
    a_pieces = [a0, a1, a2, a3, moved[0]]
    moved, _, _, made = clock.slot(
        (z_two, at(d_shared, (z + 2) % 4, 0)), (z_up, at(d_shared, (z + 1) % 4, 0)),
        (z_down, at(d_shared, (z + 3) % 4, 0)),
        feed=1.0,
        work=[(attention_backward, scalars, x_pieces, a_pieces, saved, gain_in, gain_lat, tables)],
    )
    d_shared = jnp.stack([at(d_shared, z, 0), moved[1], moved[0], moved[2]])
    d_norm, d_head, d_wl, d_we, d_gain_in, d_gain_lat = made[0]
    same_x = [[i for i in range(experts) if i // 2 % 2 == side] for side in range(2)]
    d_normed = lax.psum_scatter(d_norm, "expert", scatter_dimension=0, axis_index_groups=same_x, tiled=True)

    d_we = d_we.reshape(devices, lat_rows, groups, E_COLS).transpose(0, 2, 1, 3).reshape(width, E_COLS)
    d_head = jnp.concatenate([d_head, d_we], axis=1).reshape(ndp, 4, 2, 2 * shard, W_COLS)
    gains = [d_gain_in.reshape(width, 1), d_gain_mid.reshape(width, 1)]
    gains.append(jnp.pad(d_gain_lat.reshape(devices, lat_rows), ((0, 0), (0, shard - lat_rows))).reshape(width, 1))
    d_wl = jnp.concatenate([d_wl[:, :lat_cols]] + [low(value) for value in gains], axis=1)
    d_wl = jnp.pad(d_wl, ((0, 0), (0, -d_wl.shape[1] % 128))).reshape(ndp, 4, 2, 2, shard, -1)
    s_kept, s_away = at(d_shared, x, 1), at(d_shared, 1 - x, 1)
    if two:
        first, second = d_head[:, :2], d_head[:, 2:]
        moved, _, _, _ = clock.slot(
            (x_swap, at(first, 1 - x, 2)), (dp_swap, at(second, 1 - dp, 0)), (core_swap, at(d_wl, 1 - core, 3))
        )
        first = wide(at(first, x, 2)) + wide(moved[0])
        second = wide(at(second, dp, 0)) + wide(moved[1])
        d_wl = wide(at(d_wl, core, 3)) + wide(moved[2])
        moved, _, _, _ = clock.slot(
            (dp_swap, low(at(first, 1 - dp, 0))), (x_swap, low(at(second, 1 - x, 1))),
            (x_swap, low(at(d_wl, 1 - x, 2))), feed=0.6,
        )
        first = at(first, dp, 0) + wide(moved[0])
        second = at(second, x, 1) + wide(moved[1])
        d_wl = at(d_wl, x, 2) + wide(moved[2])
        d_head = low(jnp.concatenate([first, second]))
    else:
        d_head = wide(at(d_head, x, 2)) + wide(x_swap(at(d_head, 1 - x, 2)))
        d_head = dp_scatter(low(d_head))[0]
        d_wl = wide(at(d_wl, core, 3)) + wide(core_swap(at(d_wl, 1 - core, 3)))
        d_wl = at(d_wl, x, 2) + wide(x_swap(low(at(d_wl, 1 - x, 2))))
    moved, _, ended, _ = clock.slot(
        (z_two, at(d_head, (z + 2) % 4, 0)), (z_down, at(d_head, (z + 3) % 4, 0)),
        (z_up, at(d_head, (z + 1) % 4, 0)), (x_swap, s_away), *(lane(low(at(d_wl, 1 - dp, 0))) if two else []),
        end=[out_sum], feed=2.0,
    )
    d_head = jnp.stack([at(d_head, z, 0), moved[1], moved[0], moved[2]]).reshape(4, 2, shard, W_COLS)
    d_shared = jnp.stack([s_kept, moved[3]], axis=1)
    d_wl = at(d_wl, dp, 0) + wide(moved[4]) if two else wide(dp_scatter(low(d_wl))[0])
    out = low(mid + turn(wide(ended[0])))
    s_kept, s_away = at(d_shared, core, 2), at(d_shared, 1 - core, 2)
    moved, _, ended, _ = clock.slot(
        (core_swap, at(d_head, 1 - core, 1)), (z_two, low(at(d_wl, (z + 2) % 4, 0))),
        (z_down, low(at(d_wl, (z + 3) % 4, 0))), (z_up, low(at(d_wl, (z + 1) % 4, 0))), (core_swap, s_away),
        end=[d_normed],
    )
    d_head = jnp.stack([at(d_head, core, 1), moved[0]], axis=1).reshape(pairs, shard, W_COLS)
    d_wl = at(d_wl, z, 0) + wide(moved[1]) + wide(moved[2]) + wide(moved[3])
    d_shared = jnp.stack([s_kept, moved[4]], axis=2).reshape(experts, shard, 3 * ff_part)
    d_normed = wide(ended[0])

    if two:
        got = [wide(joined(entry)) for entry in sent]
        d_expert = [d_gate_home + got[1], d_up_home + got[2], d_down_home + got[0]]
    else:
        d_expert = [
            wide(dp_scatter(low(jnp.concatenate([contract(value, d) for value in rows_x]))))
            for d in (d_gate, d_up)
        ]
        d_expert.append(wide(dp_scatter(low(jnp.concatenate([contract(e_act, value) for value in rows_g], axis=1)), 1)))
    d_in, _ = rms_back(d_normed, xf, rms_scale(xf), gain_in)
    d_tokens = d_mid + d_in
    d_shared = wide(reorder([d_shared], block_index)[0])
    grad_sg, grad_su = (
        d_shared[:, :, i * ff_part : (i + 1) * ff_part].transpose(1, 0, 2).reshape(shard, ff_s) for i in range(2)
    )
    grad_sd = d_shared[:, :, 2 * ff_part :].transpose(0, 2, 1).reshape(ff_s, shard)
    pair_number = jnp.arange(pairs, dtype=jnp.int32)
    pair_index = ((pair_number // 2 + 4 - z) % 4) * 2 + (pair_number % 2 ^ core)
    d_head = wide(reorder([d_head], pair_index)[0])
    grad_wq = jnp.concatenate(
        [
            d_head[..., : 2 * HD].reshape(pairs, shard, 2, HD),
            d_head[..., 2 * HD : Q_COLS].reshape(pairs, shard, 2, RD),
        ],
        axis=3,
    )
    grad_wq = grad_wq.transpose(1, 0, 2, 3).reshape(shard, HEADS * (HD + RD))
    grad_wo = d_head[..., Q_COLS : Q_COLS + O_COLS].transpose(0, 2, 1).reshape(HEADS * VD, shard)
    grad_we = d_head[..., Q_COLS + O_COLS :].reshape(pairs, groups, lat_rows, E_COLS).transpose(2, 0, 1, 3)
    grad_we = grad_we.reshape(lat_rows, HEADS * (HD + VD))
    return (
        out,
        d_tokens,
        d_wl[:, lat_cols],
        d_wl[:lat_rows, lat_cols + 2],
        d_wl[:, lat_cols + 1],
        grad_wq,
        d_wl[:, :lat_cols],
        grad_we,
        grad_wo,
        grad_sg,
        grad_su,
        grad_sd,
        d_expert[0][None],
        d_expert[1][None],
        d_expert[2][None],
    )


def solution(mesh):
    rows = P(("dp", "expert"), None)
    vector = P(("dp", "expert"))
    columns = P(None, ("dp", "expert"))
    by_row = P("expert", "dp", None)
    by_column = P("expert", None, "dp")
    return jax.shard_map(
        local,
        mesh=mesh,
        in_specs=(
            rows, rows, rows, rows, vector, vector, vector, rows, rows, rows, columns, rows, rows, columns, by_row,
            by_row, by_column, rows,
        ),
        out_specs=(
            rows, rows, vector, vector, vector, rows, rows, rows, columns, rows, rows, columns, by_row, by_row,
            by_column,
        ),
        check_vma=False,
    )
```

time: 2640 us -> 866 us (0.33)
  waiting for transfers between devices: 2000 us -> 279 us
  blocking collectives: 228 us -> 0 us
  matrix products: 260 us -> 35 us
  Pallas kernels: 0 us -> 184 us
  starting transfers between devices: 24.7 us -> 112 us
  local copies, waits for them, and re-layouts: 72.6 us -> 144 us
  other arithmetic: 34 us -> 86.8 us
    reduce_scatter x10 -> x2, waiting for transfers between devices: 1400 us -> 0.01 us  [the longest x1 0.01 us: local(): lax.psum_scatter(clock.tie(out_part), 'expert', scatter_dimension=0, tile...]
    all_gather x10 -> x0, waiting for transfers between devices: 591 us -> none  [the longest x1 113 us: local(): lax.all_gather(shared_up, ('dp', 'expert'), axis=0, tiled=True)]
    ppermute x0 -> x112, waiting for transfers between devices: none -> 279 us  [the longest x75 214 us: move(): return lax.ppermute(value, 'expert', [(i, to(i)) for i in range(16)])]
    unnamed x2 -> x0, blocking collectives: 228 us -> none
    pallas_call x0 -> x15, Pallas kernels: none -> 184 us  [the longest x12 110 us: whole_call(): pl.pallas_call(kernel, in_specs=specs, out_specs=[vmem] * len(outs), out_...]
    dot_general x29 -> x0, matrix products: 166 us -> none  [the longest x10 80.9 us: matmul(): return jnp.dot(left, right, preferred_element_type=jnp.float32)]
    ppermute x0 -> x112, starting transfers between devices: none -> 112 us  [the longest x75 75.1 us: move(): return lax.ppermute(value, 'expert', [(i, to(i)) for i in range(16)])]
    dot_general x10 -> x6, matrix products: 93.2 us -> 35 us  [contract(): lax.dot_general(left, right, (((0,), (0,)), ((), ())), preferred_element_...]
  transfers between devices with their start and end apart: 24 -> 114, of which waited for: 17 -> 45; matrix products, arithmetic and copies ran while one was open for 14% -> 20% of each run, Pallas kernels for 0% -> 21%
where the time goes in v2:
time: 866 us; the launch traced here: 857 us
  waiting for transfers between devices  279 us (32%)
  Pallas kernels  184 us (21%)
  local copies, waits for them, and re-layouts  144 us (17%)
  starting transfers between devices  112 us (13%)
  other arithmetic  86.8 us (10%)
  matrix products  35 us (4%)
  between operations  16.6 us (2%)
    ppermute x75, waiting for transfers between devices, move(): return lax.ppermute(value, 'expert', [(i, to(i)) for i in range(16)])  214 us
    pallas_call x12, Pallas kernels, whole_call(): pl.pallas_call(kernel, in_specs=specs, out_specs=[vmem] * len(outs), out_...  110 us
    ppermute x75, starting transfers between devices, move(): return lax.ppermute(value, 'expert', [(i, to(i)) for i in range(16)])  75.1 us
    pallas_call x3, Pallas kernels, tiled_call(): pl.pallas_call(kernel, grid=(steps,), in_specs=specs, out_specs=out_specs...  74.4 us
    ppermute x37, waiting for transfers between devices, dp_swap(): return lax.ppermute(value, 'dp', [(0, 1), (1, 0)])  65.2 us
    unnamed x297, local copies, waits for them, and re-layouts  39.5 us
    ppermute x37, starting transfers between devices, dp_swap(): return lax.ppermute(value, 'dp', [(0, 1), (1, 0)])  36.8 us
    dot_general x6, matrix products, contract(): lax.dot_general(left, right, (((0,), (0,)), ((), ())), preferred_element_...  35 us
  transfers between devices with their start and end apart: 114, of which 45 were waited for; matrix products, arithmetic and copies ran while one was open for 20% of the time, Pallas kernels for 21%

profile of v2, /device:TPU:0, one launch (start us, length us, event | category | flops | bytes accessed | tf_op | source)
XLA Modules:
  0.0 857.0 jit_solution(15565779967685102807)
XLA Ops:
  25.2 11.6 %collective-permute-done.4.refs_1_ = bf16[128,2048]{1,0:T(8,128)(2,1)} collective-permute-done((bf16[128,2048]{1,0:T(8,128)(2,1)S(1)}, bf16[128,2048]{1,0:T(8,128)(2,1)}, u32[]{:S(2)}, u32[]{:S(2)}) %collective-permute-start.4) | collective-permute-done | bytes 524320 | tf_op jit(solution)/shard_map/ppermute | solution.py:78
  48.1 9.0 %collective-permute-done.6 = bf16[128,768]{1,0:T(8,128)(2,1)S(1)} collective-permute-done((bf16[128,768]{1,0:T(8,128)(2,1)S(1)}, bf16[128,768]{1,0:T(8,128)(2,1)S(1)}, u32[]{:S(2)}, u32[]{:S(2)}) %collective-permute-start.6) | collective-permute-done | bytes 196640 | tf_op jit(solution)/shard_map/ppermute | solution.py:78
  71.0 8.6 %collective-permute-done.11.refs_2_ = bf16[128,2048]{1,0:T(8,128)(2,1)} collective-permute-done((bf16[128,2048]{1,0:T(8,128)(2,1)}, bf16[128,2048]{1,0:T(8,128)(2,1)}, u32[]{:S(2)}, u32[]{:S(2)}) %collective-permute-start.11) | collective-permute-done | bytes 524320 | tf_op jit(solution)/shard_map/ppermute | solution.py:78
  79.6 8.9 %collective-permute-done.12.refs_1_.refs_11_ = bf16[128,2048]{1,0:T(8,128)(2,1)S(1)} collective-permute-done((bf16[128,2048]{1,0:T(8,128)(2,1)S(1)}, bf16[128,2048]{1,0:T(8,128)(2,1)S(1)}, u32[]{:S(2)}, u32[]{:S(2)}) %collective-permute-start.12) | collective-permute-done | bytes 524320 | tf_op jit(solution)/shard_map/ppermute | solution.py:78
  140.0 17.9 %shard_map.290 = (bf16[512,2048]{1,0:T(8,128)(2,1)}, bf16[512,2048]{1,0:T(8,128)(2,1)}, bf16[1024,384]{1,0:T(8,128)(2,1)}, bf16[1024,128]{1,0:T(8,128)(2,1)}, f3...) custom-call(s32[4]{0:T(128)} %pad_add_fusion.place_ref, ...), custom_call_target="tpu_custom_call" | custom-call | flops 5368709120 | bytes 26234880 | tf_op jit(solution)/shard_map/pallas_call | solution.py:167
  168.1 11.8 %collective-permute-done.30.refs_3_.refs_13_ = bf16[128,2048]{1,0:T(8,128)(2,1)S(1)} collective-permute-done((bf16[128,2048]{1,0:T(8,128)(2,1)S(1)}, bf16[128,2048]{1,0:T(8,128)(2,1)S(1)}, u32[]{:S(2)}, u32[]{:S(2)}) %collective-permute-start.30) | collective-permute-done | bytes 524320 | tf_op jit(solution)/shard_map/ppermute | solution.py:78
  213.9 10.7 %collective-permute-done.37 = bf16[128,2048]{1,0:T(8,128)(2,1)S(1)} collective-permute-done((bf16[128,2048]{1,0:T(8,128)(2,1)}, bf16[128,2048]{1,0:T(8,128)(2,1)S(1)}, u32[]{:S(2)}, u32[]{:S(2)}) %collective-permute-start.37) | collective-permute-done | bytes 524320 | tf_op jit(solution)/shard_map/ppermute | solution.py:78
  231.5 11.1 %collective-permute-done.41 = bf16[128,2048]{1,0:T(8,128)(2,1)S(1)} collective-permute-done((bf16[128,2048]{1,0:T(8,128)(2,1)S(1)}, bf16[128,2048]{1,0:T(8,128)(2,1)S(1)}, u32[]{:S(2)}, u32[]{:S(2)}) %collective-permute-start.41) | collective-permute-done | bytes 524320 | tf_op jit(solution)/shard_map/ppermute | solution.py:78
  250.0 13.1 %collective-permute-done.44.refs_1_ = bf16[128,2048]{1,0:T(8,128)(2,1)S(1)} collective-permute-done((bf16[128,2048]{1,0:T(8,128)(2,1)S(1)}, bf16[128,2048]{1,0:T(8,128)(2,1)S(1)}, u32[]{:S(2)}, u32[]{:S(2)}) %collective-permute-start.44) | collective-permute-done | bytes 524320 | tf_op jit(solution)/shard_map/ppermute | solution.py:78
  265.8 14.1 %collective-permute-done.47.refs_2_ = bf16[128,2048]{1,0:T(8,128)(2,1)} collective-permute-done((bf16[128,2048]{1,0:T(8,128)(2,1)S(1)}, bf16[128,2048]{1,0:T(8,128)(2,1)}, u32[]{:S(2)}, u32[]{:S(2)}) %collective-permute-start.47) | collective-permute-done | bytes 524320 | tf_op jit(solution)/shard_map/ppermute | solution.py:78
  299.7 13.7 %collective-permute-done.54.refs_7_ = bf16[128,2048]{1,0:T(8,128)(2,1)S(1)} collective-permute-done((bf16[128,2048]{1,0:T(8,128)(2,1)}, bf16[128,2048]{1,0:T(8,128)(2,1)S(1)}, u32[]{:S(2)}, u32[]{:S(2)}) %collective-permute-start.54) | collective-permute-done | bytes 524320 | tf_op jit(solution)/shard_map/ppermute | solution.py:78
  325.0 14.2 %collective-permute-done.56 = bf16[224,1408]{1,0:T(8,128)(2,1)S(1)} collective-permute-done((bf16[224,1408]{1,0:T(8,128)(2,1)S(1)}, bf16[224,1408]{1,0:T(8,128)(2,1)S(1)}, u32[]{:S(2)}, u32[]{:S(2)}) %collective-permute-start.56) | collective-permute-done | bytes 630816 | tf_op jit(solution)/shard_map/ppermute | solution.py:708
  355.3 8.5 collective-permute-done.61
  370.5 27.1 %shard_map.294 = (bf16[1024,1408]{1,0:T(8,128)(2,1)}, bf16[1024,1408]{1,0:T(8,128)(2,1)}, bf16[1024,1408]{1,0:T(8,128)(2,1)}) custom-call(bf16[1024,1024]{1,0:T(8,128)(2,1)} %get-tuple-element.847.x0_ref, bf16[1024,1024]{1,0:T(8,128)(2,1)} %get-tuple-element.776.x1_ref, bf16[1024,1024]{1,0:T(8,128)(2,1)} %get-tuple-element.802.r0_ref, ...), custom_call_target="tpu_custom_call" | custom-call | flops 17716740096 | bytes 34340864 | tf_op jit(solution)/shard_map/pallas_call | solution.py:535
  422.3 11.2 %shard_map.297 = (bf16[2048,256]{1,0:T(8,128)(2,1)}, bf16[2048,512]{1,0:T(8,128)(2,1)}) custom-call(bf16[128,2048]{1,0:T(8,128)(2,1)} %copy-done.26, bf16[128,2048]{1,0:T(8,128)(2,1)} %copy-done.41, bf16[128,2048]{1,0:T(8,128)(2,1)} %collective-permute-done.47.refs_2_, bf16[128,2048]{1,0:T(8,128)(2,1)} %collective-permute-done.51.refs_3_, ...), custom_call_target="tpu_custom_call" | custom-call | flops 4294967296 | bytes 15728640 | tf_op jit(solution)/shard_map/pallas_call | solution.py:167
  435.4 28.6 %shard_map.298 = (bf16[1024,2048]{1,0:T(8,128)(2,1)}, bf16[1024,2048]{1,0:T(8,128)(2,1)}) custom-call(bf16[1024,1408]{1,0:T(8,128)(2,1)} %get-tuple-element.811.dg_ref, bf16[1024,1408]{1,0:T(8,128)(2,1)} %get-tuple-element.848.du_ref, bf16[1024,1408]{1,0:T(8,128)(2,1)} %bitcast.263, bf16[1024,1408]{1,0:T(8,128)(2,1)} %copy-done.116, ...), custom_call_target="tpu_custom_call" | custom-call | flops 17179869184 | bytes 29892608 | tf_op jit(solution)/shard_map/pallas_call | solution.py:535
  501.7 18.7 %shard_map.299 = bf16[2048,2048]{1,0:T(8,128)(2,1)} custom-call(s32[16]{0:T(128)} %get-tuple-element.786.index_ref, bf16[1024,1408]{1,0:T(8,128)(2,1)} %get-tuple-element.801.act_ref, f32[1024,1]{1,0:T(8,128)} %get-tuple-element.788.share_ref, bf16[1408,1024]{1,0:T(8,128)(2,1)} %bitcast.265, bf16[1408,1024]{1,0:T(8,128)(2,1)} %copy-done.114, ...), custom_call_target="tpu_custom_call" | custom-call | flops 9126805504 | bytes 19148864 | tf_op jit(solution)/shard_map/pallas_call | solution.py:535
  532.5 8.3 fusion.145
  573.9 17.2 %shard_map.300 = bf16[2048,528]{1,0:T(8,128)(2,1)} custom-call(bf16[128,2048]{1,0:T(8,128)(2,1)} %copy-done.26, bf16[128,2048]{1,0:T(8,128)(2,1)} %copy-done.41, bf16[128,2048]{1,0:T(8,128)(2,1)} %collective-permute-done.47.refs_2_, bf16[128,2048]{1,0:T(8,128)(2,1)} %collective-permute-done.51.refs_3_, bf16[128,2048]{1,0:T(8,128)(2,1)} %copy-done.42, ...), custom_call_target="tpu_custom_call" | custom-call | flops 6442450944 | bytes 22085632 | tf_op jit(solution)/shard_map/pallas_call | solution.py:167
  601.2 16.8 %collective-permute-done.84.refs_10_ = bf16[128,2048]{1,0:T(8,128)(2,1)S(1)} collective-permute-done((bf16[128,2048]{1,0:T(8,128)(2,1)S(1)}, bf16[128,2048]{1,0:T(8,128)(2,1)S(1)}, u32[]{:S(2)}, u32[]{:S(2)}) %collective-permute-start.84) | collective-permute-done | bytes 524320 | tf_op jit(solution)/shard_map/ppermute | solution.py:78
  622.2 26.4 %collective-permute-done.86.refs_11_ = bf16[128,2048]{1,0:T(8,128)(2,1)S(1)} collective-permute-done((bf16[128,2048]{1,0:T(8,128)(2,1)S(1)}, bf16[128,2048]{1,0:T(8,128)(2,1)S(1)}, u32[]{:S(2)}, u32[]{:S(2)}) %collective-permute-start.86) | collective-permute-done | bytes 524320 | tf_op jit(solution)/shard_map/ppermute | solution.py:78
  681.2 29.8 %shard_map.301 = (bf16[1024,2048]{1,0:T(8,128)(2,1)}, bf16[2048,640]{1,0:T(8,128)(2,1)}, bf16[2048,640]{1,0:T(8,128)(2,1)}, bf16[512,512]{1,0:T(8,128)(2,1)}, f32[1,2048]{1,0:T(1,128)}, /*index=5*/f32[1,512]{1,0:T(1,128)}) custom-call(s32[4]{0:T(128)} %pad_add_fusion.place_ref, bf16[128,2048]{1,0:T(8,128)(2,1)} %refs_0_.1, ...), custom_call_target="tpu_custom_call" | custom-call | flops 10737418240 | bytes 29913088 | tf_op jit(solution)/shard_map/pallas_call | solution.py:167
  728.7 7.9 add_bitcast_fusion
  758.6 13.1 %collective-permute-done.98 = bf16[2,128,768]{2,1,0:T(8,128)(2,1)S(1)} collective-permute-done((bf16[2,128,768]{2,1,0:T(8,128)(2,1)S(1)}, bf16[2,128,768]{2,1,0:T(8,128)(2,1)S(1)}, u32[]{:S(2)}, u32[]{:S(2)}) %collective-permute-start.98) | collective-permute-done | bytes 393248 | tf_op jit(solution)/shard_map/ppermute | solution.py:708
  (765 shorter events, 482.0 us)
Async XLA Ops:
  7.3 790.0 %reduce-scatter.3.cloned.1.call-start = ((), (), s32[]{:S(2)}) async-start(), calls=%async_computation.2 | async-start | bytes 8912896 | tf_op jit(solution)/shard_map/reduce_scatter | solution.py:992
  59.2 29.2 %collective-permute-start.10 = (bf16[4,128,1152]{2,1,0:T(8,128)(2,1)S(1)}, bf16[4,128,1152]{2,1,0:T(8,128)(2,1)}, u32[]{:S(2)}, u32[]{:S(2)}) collective-permute-start(bf16[4,128,1152]{2,1,0:T(8,128)(2,1)S(1)} %maximum_maximum_fusion.refs_8_), channel_id=1, source_target_pairs={{0,2},{1,3},{2,0},{3,1},{4,6},{5,7},{6,4},{7,5},{8,10},{9,11},{10,... | collective-permute-start | bytes 3538952 | tf_op jit(solution)/shard_map/ppermute | solution.py:78
  60.8 27.7 %collective-permute-start.13 = (bf16[4,128,1152]{2,1,0:T(8,128)(2,1)S(1)}, bf16[4,128,1152]{2,1,0:T(8,128)(2,1)}, u32[]{:S(2)}, u32[]{:S(2)}) collective-permute-start(bf16[4,128,1152]{2,1,0:T(8,128)(2,1)S(1)} %maximum_maximum_fusion.refs_8_), channel_id=1, source_target_pairs={{0,16},{16,0},{1,17},{17,1},{2,18},{18,2},{3,19},{19,3},{4,20},{20... | collective-permute-start | bytes 3538952 | tf_op jit(solution)/shard_map/ppermute | solution.py:708
  133.5 24.4 %collective-permute-start.24 = (bf16[448,1024]{1,0:T(8,128)(2,1)}, bf16[448,1024]{1,0:T(8,128)(2,1)S(1)}, u32[]{:S(2)}, u32[]{:S(2)}) collective-permute-start(bf16[448,1024]{1,0:T(8,128)(2,1)} %slice_bitcast_fusion.4), channel_id=1, source_target_pairs={{0,16},{16,0},{1,17},{17,1},{2,18},{18,2},{3,19},{19,3},{4,20},{20... | collective-permute-start | bytes 2752520 | tf_op jit(solution)/shard_map/ppermute | solution.py:708
  134.0 23.9 %collective-permute-start.25 = (bf16[128,2048]{1,0:T(8,128)(2,1)S(1)}, bf16[128,2048]{1,0:T(8,128)(2,1)S(1)}, u32[]{:S(2)}, u32[]{:S(2)}) collective-permute-start(bf16[128,2048]{1,0:T(8,128)(2,1)S(1)} %fusion.17.refs_0_.refs_10_), channel_id=1, source_target_pairs={{0,2},{1,3},{2,0},{3,1},{4,6},{5,7},{6,4},{7,5},{8,10},{9,11},{10,... | collective-permute-start | bytes 1572872 | tf_op jit(solution)/shard_map/ppermute | solution.py:78
  158.0 22.7 %collective-permute-start.29 = (bf16[512,2048]{1,0:T(8,128)(2,1)}, bf16[512,2048]{1,0:T(8,128)(2,1)}, u32[]{:S(2)}, u32[]{:S(2)}) collective-permute-start(bf16[512,2048]{1,0:T(8,128)(2,1)} %get-tuple-element.586), channel_id=1, source_target_pairs={{0,1},{1,0},{2,3},{3,2},{4,5},{5,4},{6,7},{7,6},{8,9},{9,8},{10,11... | collective-permute-start | bytes 6291464 | tf_op jit(solution)/shard_map/ppermute | solution.py:78
  316.3 22.8 %collective-permute-start.57 = (bf16[512,2048]{1,0:T(8,128)(2,1)S(1)}, bf16[512,2048]{1,0:T(8,128)(2,1)}, u32[]{:S(2)}, u32[]{:S(2)}) collective-permute-start(bf16[512,2048]{1,0:T(8,128)(2,1)S(1)} %pad_maximum_fusion.3), channel_id=1, source_target_pairs={{0,1},{1,0},{2,3},{3,2},{4,5},{5,4},{6,7},{7,6},{8,9},{9,8},{10,11... | collective-permute-start | bytes 6291464 | tf_op jit(solution)/shard_map/ppermute | solution.py:78
  339.2 27.9 %collective-permute-start.58 = (bf16[352,1408]{1,0:T(8,128)(2,1)}, bf16[352,1408]{1,0:T(8,128)(2,1)S(1)}, u32[]{:S(2)}, u32[]{:S(2)}) collective-permute-start(bf16[352,1408]{1,0:T(8,128)(2,1)} %slice_bitcast_fusion.3), channel_id=1, source_target_pairs={{0,16},{16,0},{1,17},{17,1},{2,18},{18,2},{3,19},{19,3},{4,20},{20... | collective-permute-start | bytes 2973704 | tf_op jit(solution)/shard_map/ppermute | solution.py:708
  340.3 23.4 %collective-permute-start.61 = (bf16[2,2,64,528]{3,2,1,0:T(8,128)(2,1)}, bf16[2,2,64,528]{3,2,1,0:T(8,128)(2,1)S(1)}, u32[]{:S(2)}, u32[]{:S(2)}) collective-permute-start(bf16[2,2,64,528]{3,2,1,0:T(8,128)(2,1)} %get-tuple-element.674), channel_id=1, source_target_pairs={{0,8},{1,9},{2,10},{3,11},{4,12},{5,13},{6,14},{7,15},{8,0},{9,1},... | collective-permute-start | bytes 811016 | tf_op jit(solution)/shard_map/ppermute | solution.py:78
  369.5 28.7 %collective-permute-start.62 = (bf16[16,64,528]{2,1,0:T(8,128)(2,1)S(1)}, bf16[16,64,528]{2,1,0:T(8,128)(2,1)}, u32[]{:S(2)}, u32[]{:S(2)}) collective-permute-start(bf16[16,64,528]{2,1,0:T(8,128)(2,1)S(1)} %bitcast.255), channel_id=1, source_target_pairs={{0,16},{16,0},{1,17},{17,1},{2,18},{18,2},{3,19},{19,3},{4,20},{20... | collective-permute-start | bytes 3244040 | tf_op jit(solution)/shard_map/ppermute | solution.py:708
  410.4 23.1 %collective-permute-start.64 = (bf16[384,1024]{1,0:T(8,128)(2,1)S(1)}, bf16[384,1024]{1,0:T(8,128)(2,1)S(1)}, u32[]{:S(2)}, u32[]{:S(2)}) collective-permute-start(bf16[384,1024]{1,0:T(8,128)(2,1)S(1)} %slice.498), channel_id=1, source_target_pairs={{0,16},{16,0},{1,17},{17,1},{2,18},{18,2},{3,19},{19,3},{4,20},{20... | collective-permute-start | bytes 2359304 | tf_op jit(solution)/shard_map/ppermute | solution.py:708
  434.5 29.5 %collective-permute-start.65 = (bf16[640,1024]{1,0:T(8,128)(2,1)}, bf16[640,1024]{1,0:T(8,128)(2,1)S(1)}, u32[]{:S(2)}, u32[]{:S(2)}) collective-permute-start(bf16[640,1024]{1,0:T(8,128)(2,1)} %slice.497), channel_id=1, source_target_pairs={{0,16},{16,0},{1,17},{17,1},{2,18},{18,2},{3,19},{19,3},{4,20},{20... | collective-permute-start | bytes 3932168 | tf_op jit(solution)/shard_map/ppermute | solution.py:708
  562.0 256.2 %reduce-scatter.5.cloned.1.call-start = ((), (), s32[]{:S(2)}) async-start(), calls=%async_computation.3 | async-start | bytes 4718592 | tf_op jit(solution)/shard_map/reduce_scatter | solution.py:1028
  593.4 24.6 %collective-permute-start.84 = (bf16[128,2048]{1,0:T(8,128)(2,1)S(1)}, bf16[128,2048]{1,0:T(8,128)(2,1)S(1)}, u32[]{:S(2)}, u32[]{:S(2)}) collective-permute-start(bf16[128,2048]{1,0:T(8,128)(2,1)S(1)} %collective-permute-done.83.refs_9_), channel_id=1, source_target_pairs={{0,4},{1,5},{2,6},{3,7},{4,8},{5,9},{6,10},{7,11},{8,12},{9,13},{1... | collective-permute-start | bytes 1572872 | tf_op jit(solution)/shard_map/ppermute | solution.py:78
  593.5 24.5 %collective-permute-start.85 = (bf16[8,64,528]{2,1,0:T(8,128)(2,1)S(1)}, bf16[8,64,528]{2,1,0:T(8,128)(2,1)S(1)}, u32[]{:S(2)}, u32[]{:S(2)}) collective-permute-start(bf16[8,64,528]{2,1,0:T(8,128)(2,1)S(1)} %get-tuple-element.846), channel_id=1, source_target_pairs={{0,16},{16,0},{1,17},{17,1},{2,18},{18,2},{3,19},{19,3},{4,20},{20... | collective-permute-start | bytes 1622024 | tf_op jit(solution)/shard_map/ppermute | solution.py:708
  618.0 30.6 %collective-permute-start.87 = (bf16[8,64,528]{2,1,0:T(8,128)(2,1)S(1)}, bf16[8,64,528]{2,1,0:T(8,128)(2,1)}, u32[]{:S(2)}, u32[]{:S(2)}) collective-permute-start(bf16[8,64,528]{2,1,0:T(8,128)(2,1)S(1)} %get-tuple-element.853), channel_id=1, source_target_pairs={{0,16},{16,0},{1,17},{17,1},{2,18},{18,2},{3,19},{19,3},{4,20},{20... | collective-permute-start | bytes 1622024 | tf_op jit(solution)/shard_map/ppermute | solution.py:708
  618.1 30.5 %collective-permute-start.86 = (bf16[128,2048]{1,0:T(8,128)(2,1)S(1)}, bf16[128,2048]{1,0:T(8,128)(2,1)S(1)}, u32[]{:S(2)}, u32[]{:S(2)}) collective-permute-start(bf16[128,2048]{1,0:T(8,128)(2,1)S(1)} %collective-permute-done.84.refs_10_), channel_id=1, source_target_pairs={{0,4},{1,5},{2,6},{3,7},{4,8},{5,9},{6,10},{7,11},{8,12},{9,13},{1... | collective-permute-start | bytes 1572872 | tf_op jit(solution)/shard_map/ppermute | solution.py:78
  650.0 24.4 %collective-permute-start.89 = (bf16[512,2048]{1,0:T(8,128)(2,1)S(1)}, bf16[512,2048]{1,0:T(8,128)(2,1)}, u32[]{:S(2)}, u32[]{:S(2)}) collective-permute-start(bf16[512,2048]{1,0:T(8,128)(2,1)S(1)} %pad_maximum_fusion.4), channel_id=1, source_target_pairs={{0,1},{1,0},{2,3},{3,2},{4,5},{5,4},{6,7},{7,6},{8,9},{9,8},{10,11... | collective-permute-start | bytes 6291464 | tf_op jit(solution)/shard_map/ppermute | solution.py:78
  675.0 36.0 %collective-permute-start.91 = (bf16[2,2,64,528]{3,2,1,0:T(8,128)(2,1)}, bf16[2,2,64,528]{3,2,1,0:T(8,128)(2,1)S(1)}, u32[]{:S(2)}, u32[]{:S(2)}) collective-permute-start(bf16[2,2,64,528]{3,2,1,0:T(8,128)(2,1)} %get-tuple-element.861), channel_id=1, source_target_pairs={{0,8},{1,9},{2,10},{3,11},{4,12},{5,13},{6,14},{7,15},{8,0},{9,1},... | collective-permute-start | bytes 811016 | tf_op jit(solution)/shard_map/ppermute | solution.py:78
  675.0 36.0 %collective-permute-start.92 = (bf16[2,2,64,528]{3,2,1,0:T(8,128)(2,1)}, bf16[2,2,64,528]{3,2,1,0:T(8,128)(2,1)}, u32[]{:S(2)}, u32[]{:S(2)}) collective-permute-start(bf16[2,2,64,528]{3,2,1,0:T(8,128)(2,1)} %get-tuple-element.862), channel_id=1, source_target_pairs={{0,4},{1,5},{2,6},{3,7},{4,8},{5,9},{6,10},{7,11},{8,12},{9,13},{1... | collective-permute-start | bytes 811016 | tf_op jit(solution)/shard_map/ppermute | solution.py:78
  676.4 34.7 %collective-permute-start.93 = (bf16[2,2,64,528]{3,2,1,0:T(8,128)(2,1)}, bf16[2,2,64,528]{3,2,1,0:T(8,128)(2,1)}, u32[]{:S(2)}, u32[]{:S(2)}) collective-permute-start(bf16[2,2,64,528]{3,2,1,0:T(8,128)(2,1)} %get-tuple-element.863), channel_id=1, source_target_pairs={{0,12},{1,13},{2,14},{3,15},{4,0},{5,1},{6,2},{7,3},{8,4},{9,5},{1... | collective-permute-start | bytes 811016 | tf_op jit(solution)/shard_map/ppermute | solution.py:78
  680.1 31.0 %collective-permute-start.90 = (bf16[352,1408]{1,0:T(8,128)(2,1)}, bf16[352,1408]{1,0:T(8,128)(2,1)S(1)}, u32[]{:S(2)}, u32[]{:S(2)}) collective-permute-start(bf16[352,1408]{1,0:T(8,128)(2,1)} %slice.502), channel_id=1, source_target_pairs={{0,16},{16,0},{1,17},{17,1},{2,18},{18,2},{3,19},{19,3},{4,20},{20... | collective-permute-start | bytes 2973704 | tf_op jit(solution)/shard_map/ppermute | solution.py:708
  749.3 23.7 %collective-permute-start.97 = (bf16[224,1408]{1,0:T(8,128)(2,1)S(1)}, bf16[224,1408]{1,0:T(8,128)(2,1)S(1)}, u32[]{:S(2)}, u32[]{:S(2)}) collective-permute-start(bf16[224,1408]{1,0:T(8,128)(2,1)S(1)} %copy-done.71), channel_id=1, source_target_pairs={{0,16},{16,0},{1,17},{17,1},{2,18},{18,2},{3,19},{19,3},{4,20},{20... | collective-permute-start | bytes 1892360 | tf_op jit(solution)/shard_map/ppermute | solution.py:708
  773.7 22.7 %collective-permute-start.105 = (bf16[4,2,64,528]{3,2,1,0:T(8,128)(2,1)S(1)}, bf16[4,2,64,528]{3,2,1,0:T(8,128)(2,1)S(1)}, u32[]{:S(2)}, u32[]{:S(2)}) collective-permute-start(bf16[4,2,64,528]{3,2,1,0:T(8,128)(2,1)S(1)} %get-tuple-element.926), channel_id=1, source_target_pairs={{0,2},{1,3},{2,0},{3,1},{4,6},{5,7},{6,4},{7,5},{8,10},{9,11},{10,... | collective-permute-start | bytes 1622024 | tf_op jit(solution)/shard_map/ppermute | solution.py:78
  (225 other events, 2781.3 us)
Sparse Core Ops, SparseCore 0:
  562.2 121.7 reduce-scatter.2
  726.2 48.2 reduce-scatter.4

commit v3 on v2

--- a/solution.py
+++ b/solution.py
@@ -2,6 +2,8 @@
 
 import jax
 import jax.numpy as jnp
+import ml_dtypes
+import numpy as np
 from jax import lax
 from jax.experimental import pallas as pl
 from jax.experimental.pallas import tpu as pltpu
@@ -53,19 +55,6 @@
     return (grad_in, grad_gain)
 
 
-def layout(lengths, rows):
-    ends = jnp.cumsum(lengths, axis=-1)
-    place = jnp.arange(rows, dtype=jnp.int32)
-    passed = (place[None, :, None] >= ends[:, None, :]).astype(jnp.int32)
-    doc = jnp.sum(passed, axis=-1)
-    start = jnp.sum(passed * lengths[:, None, :], axis=-1)
-    return ((place[None, :] - start).astype(F32), doc)
-
-
-def after(value, *others):
-    return lax.optimization_barrier((value,) + others)[0]
-
-
 def low(value):
     return value.astype(BF)
 
@@ -244,6 +233,49 @@
     return (id_col == id_row) & (key <= query)
 
 
+def angle_table(rows):
+    freq = np.power(np.float32(10000.0), np.float32(-2.0) * np.arange(RD // 2, dtype=np.float32) / np.float32(RD))
+    theta = np.arange(rows, dtype=np.float32)[:, None] * freq.astype(np.float32)
+    cosine, sine = np.cos(theta), np.sin(theta)
+    terms = []
+    for value in (np.concatenate([cosine] * 4, axis=1), np.concatenate([-sine, sine, -sine, sine], axis=1)):
+        rest = value.astype(np.float32)
+        for _ in range(3):
+            term = rest.astype(ml_dtypes.bfloat16)
+            terms.append(term)
+            rest = rest - term.astype(np.float32)
+    return np.concatenate(terms, axis=1)
+
+
+def chunk_layout(facts_ref, j, rows, shape):
+    count = CHUNK // rows
+    number = lax.broadcasted_iota(jnp.int32, shape, 0 if shape[0] == CHUNK else 1)
+    block, place = number // rows, number % rows
+    doc, start, ends = 0, 0, [0] * count
+    for k in range(3):
+        lengths = [facts_ref[4 + (j * count + b) * 4 + k] for b in range(count)]
+        ends = [end + length for end, length in zip(ends, lengths)]
+        end, length = ends[-1], lengths[-1]
+        for b in range(count - 2, -1, -1):
+            end = jnp.where(block == b, ends[b], end)
+            length = jnp.where(block == b, lengths[b], length)
+        passed = place >= end
+        doc = doc + passed.astype(jnp.int32)
+        start = start + jnp.where(passed, length, 0)
+    return place - start, doc + 4 * block
+
+
+def chunk_tables(facts_ref, table_ref, j):
+    rows = table_ref.shape[0]
+    position, id_col = chunk_layout(facts_ref, j, rows, (CHUNK, 1))
+    id_row = chunk_layout(facts_ref, j, rows, (1, CHUNK))[1]
+    hot = low(lax.broadcasted_iota(jnp.int32, (CHUNK, rows), 1) == position)
+    terms = matmul(hot, table_ref[...])
+    cosine = terms[:, :128] + terms[:, 128:256] + terms[:, 256:384]
+    sine = terms[:, 384:512] + terms[:, 512:640] + terms[:, 640:]
+    return cosine, sine, allowed_pairs(id_col, id_row)
+
+
 def pair(refs, j):
     pieces, start = [], 0
     for ref in refs:
@@ -254,16 +286,17 @@
     return pieces[0] if len(pieces) == 1 else jnp.concatenate(pieces, axis=0)
 
 
-def forward_kernel(ndp, layout_of, count, split, place_ref, *refs):
-    x_refs, refs = refs[:8], refs[8:]
+def forward_kernel(ndp, layout_of, pieces, count, split, place_ref, *refs):
+    x_refs, refs = refs[:pieces], refs[pieces:]
     w_refs, refs = refs[: len(layout_of)], refs[len(layout_of) :]
     wl_refs, refs = refs[:count], refs[count:]
-    we_ref, gain_ref, lg_ref, cos_ref, sin_ref, idc_ref, idr_ref = refs[:7]
-    near_ref, far_ref, q_ref, kr_ref, lat_ref, kv_ref, att_ref, wp_ref, wo_ref, exp_ref = refs[7:]
+    we_ref, gains_ref, lg_ref, table_ref = refs[:4]
+    near_ref, far_ref, q_ref, kr_ref, lat_ref, kv_ref, att_ref, wp_ref, wo_ref, exp_ref, gain_ref, mid_ref, lgo_ref = refs[4:]
     other_rows = [(ref, i) for ref in wl_refs for i in range(ref.shape[0])]
     dp, z, x, core = place_ref[0], place_ref[1], place_ref[2], place_ref[3]
     block = w_refs[0].shape[1]
     shard = block // 2
+    lat_rows = jnp.zeros((4, 128), F32)
     spare = jnp.zeros((shard, 128 - RD), BF)
     turn = 0
     for w_ref, (far, j, first) in zip(w_refs, layout_of):
@@ -280,6 +313,14 @@
             for at_row, lat in ((here, w_ref[k, :, W_COLS:]), (there, other_rows[turn][0][other_rows[turn][1]])):
                 wp_ref[pl.ds(at_row, shard), LAT_AT : LAT_AT + 384] = lat[:shard, :]
                 wp_ref[pl.ds(at_row, shard), LAT_AT + 384 :] = lat[shard:, :256]
+            here_rows, there_rows = (
+                wide(lat[shard : shard + 16, 256:]) for lat in (w_ref[k, :, W_COLS:], other_rows[turn][0][other_rows[turn][1]])
+            )
+            left = jnp.where(core == 0, here_rows[:1, :], there_rows[:1, :])
+            right = jnp.where(core == 0, there_rows[:1, :], here_rows[:1, :])
+            gain_ref[:, pl.ds(row, block)] = jnp.concatenate([left[:, :shard], right[:, :shard]], axis=1)
+            mid_ref[:, pl.ds(row, block)] = jnp.concatenate([left[:, shard:], right[:, shard:]], axis=1)
+            lat_rows = lat_rows + here_rows[1:5, :] + there_rows[1:5, :]
             turn += 1
             small = shard // 4
             for c in range(2):
@@ -292,13 +333,18 @@
         for i, (wl_ref, _) in enumerate(other_rows):
             wp_ref[i * shard : (i + 1) * shard, LAT_AT:] = jnp.concatenate([wl_ref[i, :shard, :], spare], axis=1)
         exp_ref[...] = we_ref[...]
-    gain, lat_gain = gain_ref[...], lg_ref[...]
+        gain_ref[...] = gains_ref[:1, :]
+        mid_ref[...] = gains_ref[1:2, :]
+        lgo_ref[...] = lg_ref[...]
+    else:
+        lgo_ref[...] = jnp.concatenate([lat_rows[i : i + 1, :] for i in range(4)], axis=1)
+    gain, lat_gain = gain_ref[...], lgo_ref[...]
     for j in range(4):
         rows = slice(CHUNK * j, CHUNK * (j + 1))
         xf = wide(pair(x_refs, j))
         normed = low(xf * rms_scale(xf) * gain)
         proj = matmul(normed, wp_ref[...])
-        cosine, sine = cos_ref[rows, :], sin_ref[rows, :]
+        cosine, sine, allowed = chunk_tables(place_ref, table_ref, j)
         q_mix = proj[:, 2 * HD : Q_COLS]
         k_mix = proj[:, ROT_AT:]
         q_rot = low(q_mix * cosine + swap_halves(q_mix) * sine)
@@ -314,7 +360,6 @@
         q_ref[rows, 2 * HD :] = q_rot
         kr_ref[rows, :] = k_rot
         kv_ref[rows, :] = expanded
-        allowed = allowed_pairs(idc_ref[rows, :], idr_ref[j])
         attended = []
         for head, k_side in ((0, k_rot), (1, k_turned)):
             k_main = expanded[:, 2 * head * HD : (2 * head + 1) * HD]
@@ -332,10 +377,10 @@
     ref[j * CHUNK : (j + 1) * CHUNK, :] = value
 
 
-def attention_forward(place, x_pieces, weights, layout_of, w_lat, w_exp, gain, lat_gain, tables, split):
+def attention_forward(place, x_pieces, weights, layout_of, w_lat, w_exp, gains, lat_gain, table, split):
     own, width = x_pieces[0].shape
     rows = 8 * own
-    args = list(x_pieces) + list(weights) + list(w_lat) + [w_exp, gain, lat_gain] + list(tables)
+    args = list(x_pieces) + list(weights) + list(w_lat) + [w_exp, gains, lat_gain, table]
     outs = [shaped((rows // 2, width), BF)] * 2 + [
         shaped((rows, Q_COLS), BF),
         shaped((rows, 128), BF),
@@ -345,19 +390,22 @@
         shaped((width, PROJ), BF),
         shaped((width, O_COLS), BF),
         shaped((LAT, 4 * HD), BF),
+        shaped((1, width), F32),
+        shaped((1, width), F32),
+        shaped((1, LAT), F32),
     ]
-    kernel = functools.partial(forward_kernel, lax.axis_size("dp"), layout_of, len(w_lat), split)
+    kernel = functools.partial(forward_kernel, lax.axis_size("dp"), layout_of, len(x_pieces), len(w_lat), split)
     flops = 2 * rows * width * (PROJ + O_COLS)
     out = whole_call(kernel, args, outs, flops=flops, scalars=place)
     return out[:2], out[2:]
 
 
-def backward_kernel(count, place_ref, *refs):
-    x_refs, g_refs, refs = refs[:8], refs[8 : 8 + count], refs[8 + count :]
-    q_ref, kr_ref, lat_ref, kv_ref, att_ref, wp_ref, wo_ref, we_ref, gain_ref, lg_ref = refs[:10]
-    cos_ref, sin_ref, idc_ref, idr_ref = refs[10:14]
-    dn_ref, dw_ref, dl_ref, de_ref, dg_ref, dlg_ref, acc_q, acc_o, acc_e = refs[14:]
-    z, core = place_ref[1], place_ref[3]
+def backward_kernel(pieces, count, lat_rows, place_ref, *refs):
+    x_refs, g_refs, refs = refs[:pieces], refs[pieces : pieces + count], refs[pieces + count :]
+    q_ref, kr_ref, lat_ref, kv_ref, att_ref, wp_ref, wo_ref, we_ref, gain_ref, mid_ref, lg_ref, dm_ref = refs[:12]
+    table_ref, dn_ref, dw_ref, dl_ref, de_ref, acc_q, acc_o, acc_e, dg_ref, dlg_ref = refs[12:]
+    split = len(dw_ref.shape) > 2
+    dp, z, x, core = place_ref[0], place_ref[1], place_ref[2], place_ref[3]
     own = x_refs[0].shape[0]
     gain, w_exp, lat_gain = gain_ref[...], we_ref[...], lg_ref[...]
 
@@ -373,11 +421,10 @@
         lat_scale = rms_scale(lat)
         white_lat = lat * lat_scale
         grad = pair(g_refs, j)
-        cosine, sine = cos_ref[rows, :], sin_ref[rows, :]
+        cosine, sine, allowed = chunk_tables(place_ref, table_ref, j)
         d_att = low(matmul(grad, wo_ref[...]))
         q_rot, k_rot = q_ref[rows, 2 * HD :], kr_ref[rows, :]
         k_turned = low(pltpu.roll(wide(k_rot), RD, 1))
-        allowed = allowed_pairs(idc_ref[rows, :], idr_ref[j])
         d_main, d_expanded = [], []
         dq_mix = None
         dk_mix = None
@@ -417,30 +464,96 @@
         add(acc_q, contract(d_proj, normed), j == 0)
         add(acc_o, contract(att_ref[rows, :], grad), j == 0)
         add(acc_e, contract(low(white_lat * lat_gain), d_expanded), j == 0)
-    dw_ref[:, :Q_COLS] = low(acc_q[:Q_COLS, :].T)
-    dw_ref[:, Q_COLS:] = low(acc_o[...].T)
-    dl_ref[...] = low(acc_q[Q_COLS:, :].T)
-    de_ref[...] = low(acc_e[...])
-
-
-def attention_backward(place, x_pieces, g_pieces, saved, gain, lat_gain, tables):
+    shard = acc_q.shape[1] * lat_rows // LAT
+    lane = lax.broadcasted_iota(jnp.int32, (LAT, acc_q.shape[1]), 1)
+    line = lax.broadcasted_iota(jnp.int32, (LAT, acc_q.shape[1]), 0)
+    spread = low((line // lat_rows == lane // shard) & (line % lat_rows == lane % shard))
+    spread = matmul(low(jnp.broadcast_to(dlg_ref[...], (8, LAT))), spread)[:1, :]
+    acc_q[ROT_AT + RD : ROT_AT + RD + 8, :] = jnp.concatenate(
+        [dg_ref[...], dm_ref[...], spread, jnp.zeros((5, acc_q.shape[1]), F32)], axis=0
+    )
+    if not split:
+        dw_ref[:, :Q_COLS] = low(acc_q[:Q_COLS, :].T)
+        dw_ref[:, Q_COLS : Q_COLS + O_COLS] = low(acc_o[...].T)
+        dl_ref[...] = low(acc_q[Q_COLS:, :].T)
+        de_ref[...] = low(acc_e[...])
+        return
+    block = 2 * shard
+    for number in range(acc_q.shape[1] // block):
+        y, zz, xx = number // 8, number // 2 % 4, number % 2
+        lanes = slice(number * block, (number + 1) * block)
+        slot = (x ^ xx) * 4 + y * 2 + zz if zz < 2 else 8 + (dp ^ y) * 4 + (zz - 2) * 2 + xx
+        dw_ref[slot, :, :Q_COLS] = low(acc_q[:Q_COLS, lanes].T)
+        dw_ref[slot, :, Q_COLS : Q_COLS + O_COLS] = low(acc_o[:, lanes].T)
+        for c in range(2):
+            for g in range(4):
+                row = c * shard + g * lat_rows
+                i = number * 2 + c
+                dw_ref[slot, row : row + lat_rows, Q_COLS + O_COLS :] = low(
+                    acc_e[i * lat_rows : (i + 1) * lat_rows, g * HD : (g + 1) * HD]
+                )
+        both = low(acc_q[Q_COLS:, lanes].T)
+        for c in range(2):
+            dl_ref[core ^ c, number, :, :] = both[c * shard : (c + 1) * shard, :]
+
+
+def attention_backward(place, x_pieces, g_pieces, saved, d_gain_mid, table, lat_rows):
     own, width = x_pieces[0].shape
-    q, kr, lat, kv, att, wp, wo, w_exp = saved
-    args = list(x_pieces) + list(g_pieces) + [q, kr, lat, kv, att, wp, wo, w_exp, gain, lat_gain] + list(tables)
+    q, kr, lat, kv, att, wp, wo, w_exp, gain, mid, lat_gain = saved
+    args = list(x_pieces) + list(g_pieces)
+    args += [q, kr, lat, kv, att, wp, wo, w_exp, gain, mid, lat_gain, d_gain_mid, table]
     outs = [
         shaped((8 * own, width), BF),
-        shaped((width, Q_COLS + O_COLS), BF),
+        shaped((width, W_COLS), BF),
         shaped((width, PROJ - Q_COLS), BF),
-        shaped((LAT, 4 * HD), BF),
-        shaped((1, width), F32),
-        shaped((1, LAT), F32),
+        shaped((LAT, 4 * HD) if lat_rows % 16 else (16, 128), BF),
     ]
+    shard = width * lat_rows // LAT
+    if not lat_rows % 16:
+        outs[1] = shaped((width // (2 * shard), 2 * shard, W_COLS), BF)
+        outs[2] = shaped((2, width // (2 * shard), shard, PROJ - Q_COLS), BF)
     scratch = (
-        pltpu.VMEM((PROJ, width), F32), pltpu.VMEM((O_COLS, width), F32), pltpu.VMEM((LAT, 4 * HD), F32)
+        pltpu.VMEM((PROJ, width), F32), pltpu.VMEM((O_COLS, width), F32), pltpu.VMEM((LAT, 4 * HD), F32),
+        pltpu.VMEM((1, width), F32), pltpu.VMEM((1, LAT), F32),
     )
     flops = 2 * 8 * own * width * (2 * PROJ + 2 * O_COLS)
-    kernel = functools.partial(backward_kernel, len(g_pieces))
-    return whole_call(kernel, args, outs, scratch, flops=flops, scalars=place)
+    kernel = functools.partial(backward_kernel, len(x_pieces), len(g_pieces), lat_rows)
+    d_norm, d_head, d_wl, d_we = whole_call(kernel, args, outs, scratch, flops=flops, scalars=place)
+    if lat_rows % 16:
+        d_we = d_we.reshape(width // shard, lat_rows, 4, E_COLS).transpose(0, 2, 1, 3).reshape(width, E_COLS)
+        d_head = jnp.concatenate([d_head[:, : Q_COLS + O_COLS], d_we], axis=1)
+    return d_norm, d_head, d_wl
+
+
+def routing_kernel(first, lanes, slots, me_ref, *refs):
+    in_refs, (row_ref, gate_ref, col_ref) = refs[:4], refs[4:]
+    mine = lax.broadcasted_iota(jnp.int32, (16, 128), 0) == me_ref[0]
+    gates = []
+    for ref, lane in zip(in_refs, lanes):
+        for k in range(4):
+            both = wide(ref[k, first : first + 32, lane : lane + 128])
+            gates.append(jnp.sum(jnp.where(mine, both[:16, :] + both[16:, :], 0.0), axis=0, keepdims=True))
+    gates = jnp.concatenate(gates, axis=0)
+    routed = gates > 0.0
+    line = lax.broadcasted_iota(jnp.int32, (128, 128), 0)
+    column = lax.broadcasted_iota(jnp.int32, (128, 128), 1)
+    before = low((line <= column) & (line // 64 == column // 64))
+    count = matmul(low(routed), before)
+    source = lax.broadcasted_iota(jnp.int32, (16, 128), 0)
+    token = lax.broadcasted_iota(jnp.int32, (16, 128), 1)
+    block = ((source % 2) * 2 + token // 64).astype(F32)
+    target = jnp.where(routed, block * slots + count - 1.0, -1.0)
+    turned = target.T
+    for k in range(16):
+        part = slice((k % 2) * 128, (k % 2 + 1) * 128)
+        row_ref[k // 2, :, part] = target[k : k + 1, :].astype(jnp.int32)
+        gate_ref[k // 2, :, part] = gates[k : k + 1, :]
+        col_ref[k * 128 : (k + 1) * 128, :] = turned[:, k : k + 1].astype(jnp.int32)
+
+
+def routing(me, arrays, first, lanes, slots):
+    outs = [shaped((8, 1, CHUNK), jnp.int32), shaped((8, 1, CHUNK), F32), shaped((8 * CHUNK, 1), jnp.int32)]
+    return whole_call(functools.partial(routing_kernel, first, lanes, slots), arrays, outs, scalars=me)
 
 
 def enter_grad_kernel(slots, *refs):
@@ -466,14 +579,14 @@
         rx1_ref[j * slots : (j + 1) * slots, :] = value[:, half:]
 
 
-def hidden_shared_kernel(*refs):
-    t_refs, (sgu_ref, da_ref, act_ref, pre_ref) = refs[:-4], refs[-4:]
-    third = sgu_ref.shape[1] // 2
+def hidden_shared_kernel(count, *refs):
+    t_refs, g_refs, (sgu_ref, sd_ref, act_ref, pre_ref) = refs[:count], refs[count:-4], refs[-4:]
+    third = sd_ref.shape[1]
     for j in range(8):
         rows = slice(j * CHUNK, (j + 1) * CHUNK)
         both = matmul(pair(t_refs, j), sgu_ref[...])
         gate_pre, up = both[:, :third], both[:, third:]
-        d_act = da_ref[rows, :]
+        d_act = matmul(pair(g_refs, j), sd_ref[...])
         sigma = jax.nn.sigmoid(gate_pre)
         swish = gate_pre * sigma
         act_ref[rows, :] = low(swish * up)
@@ -497,25 +610,15 @@
     return whole_call(functools.partial(dispatch_kernel, slots // 8), args, outs, flops=flops)
 
 
-def shared_grad_in_kernel(*refs):
-    g_refs, (sd_ref, da_ref) = refs[:-2], refs[-2:]
-    for j in range(8):
-        da_ref[j * CHUNK : (j + 1) * CHUNK, :] = matmul(pair(g_refs, j), sd_ref[...])
-
-
 def hidden_shared(t_pieces, g_pieces, s_both, s_down):
     own, width = t_pieces[0].shape
     third = s_down.shape[1]
-    flops = 32 * own * width * third
-    d_act = whole_call(
-        shared_grad_in_kernel, list(g_pieces) + [s_down], [shaped((16 * own, third), F32)], flops=flops
-    )[0]
-    args = list(t_pieces) + [s_both, d_act]
+    args = list(t_pieces) + list(g_pieces) + [s_both, s_down]
     outs = [shaped((16 * own, third), BF), shaped((16 * own, 2 * third), BF)]
-    return whole_call(hidden_shared_kernel, args, outs, flops=2 * flops)
-
-
-def hidden_kernel(x0_ref, x1_ref, r0_ref, r1_ref, g0_ref, g1_ref, u0_ref, u1_ref, d0_ref, d1_ref, act_ref, dg_ref, du_ref):
+    return whole_call(functools.partial(hidden_shared_kernel, len(t_pieces)), args, outs, flops=96 * own * width * third)
+
+
+def hidden_kernel(x0_ref, x1_ref, r0_ref, r1_ref, g0_ref, g1_ref, u0_ref, u1_ref, d0_ref, d1_ref, act_ref, dg_ref, du_ref, away_ref):
     step = 256
     for j in range(x0_ref.shape[0] // step):
         rows = slice(j * step, (j + 1) * step)
@@ -528,6 +631,7 @@
         act_ref[rows, :] = low(swish * up)
         dg_ref[rows, :] = low(d_act * up * (sigma * (1.0 + gate * (1.0 - sigma))))
         du_ref[rows, :] = low(d_act * swish)
+    away_ref[...] = low(contract(act_ref[...], r1_ref[...]))
 
 
 def tiled_call(kernel, steps, args, specs, outs, out_specs, scratch=(), flops=0, aliases=None):
@@ -557,13 +661,14 @@
     by_row = pl.BlockSpec((tile, half), lambda i: (i, 0))
     args = list(rows_x) + list(rows_g) + [own[0], other[0], own[1], other[1], own[2], other[2]]
     specs = [whole_spec(value) for value in args[:4]] + [by_column] * 4 + [by_row] * 2
-    outs = [shaped((slots, hidden), BF)] * 3
-    out_specs = [pl.BlockSpec((slots, tile), lambda i: (0, i))] * 3
-    flops = 12 * slots * half * hidden
+    outs = [shaped((slots, hidden), BF)] * 3 + [shaped((hidden, half), BF)]
+    out_specs = [pl.BlockSpec((slots, tile), lambda i: (0, i))] * 3 + [by_row]
+    flops = 14 * slots * half * hidden
     return tiled_call(hidden_kernel, -(-hidden // tile), args, specs, outs, out_specs, flops=flops)
 
 
-def back_kernel(per, dg_ref, du_ref, g0_ref, g1_ref, u0_ref, u1_ref, target_ref, left_ref, right_ref, near_ref, far_ref, rows_ref):
+def back_kernel(per, dg_ref, du_ref, g0_ref, g1_ref, u0_ref, u1_ref, target_ref, left_ref, right_ref, *refs):
+    out_refs, rows_ref = refs[:4], refs[4]
     steps = pl.num_programs(0) // 2
     own = pl.program_id(0) < steps
 
@@ -579,7 +684,8 @@
     for j in range(8):
         hot = low(lax.broadcasted_iota(jnp.int32, (CHUNK, per), 1) == target_ref[j * CHUNK : (j + 1) * CHUNK, :])
         out = matmul(hot, rows_ref[j * per : (j + 1) * per, :])
-        put_half(near_ref, far_ref, j, 8, low(out + mat_trans(left_ref[j * CHUNK : (j + 1) * CHUNK, :], right)))
+        out = low(out + mat_trans(left_ref[j * CHUNK : (j + 1) * CHUNK, :], right))
+        out_refs[j // 2][(j % 2) * CHUNK : (j % 2 + 1) * CHUNK, :] = out
 
 
 def expert_back(d_gate, d_up, own, other, target, left, right):
@@ -593,8 +699,8 @@
     args = [d_gate, d_up, own[0], other[0], own[1], other[1], target, left, right]
     specs = [whole_spec(d_gate), whole_spec(d_up)] + [near, far] * 2
     specs += [whole_spec(target), whole_spec(left), pl.BlockSpec((tile, columns), lambda i: (i, 0))]
-    outs = [shaped((rows // 2, width), BF)] * 2
-    out_specs = [pl.BlockSpec((rows // 2, tile), lambda i: (0, i))] * 2
+    outs = [shaped((rows // 4, width), BF)] * 4
+    out_specs = [pl.BlockSpec((rows // 4, tile), lambda i: (0, i))] * 4
     flops = 4 * slots * width * hidden + 2 * rows * width * (columns + slots // 8)
     return tiled_call(
         functools.partial(back_kernel, slots // 8), 2 * steps, args, specs, outs, out_specs,
@@ -602,7 +708,8 @@
     )
 
 
-def out_kernel(per, index_ref, act_ref, share_ref, d0_ref, d1_ref, target_ref, left_ref, right_ref, out_ref, rows_ref):
+def out_kernel(per, act_ref, share_ref, d0_ref, d1_ref, target_ref, left_ref, right_ref, *refs):
+    out_refs, rows_ref = refs[:4], refs[4]
     steps = pl.num_programs(0) // 2
     own = pl.program_id(0) < steps
 
@@ -615,36 +722,33 @@
         rows_ref[...] = low(matmul(act_ref[...], d1_ref[...]) * share_ref[...])
 
     right = right_ref[...]
-    piece = CHUNK // 2
     for j in range(8):
         hot = low(lax.broadcasted_iota(jnp.int32, (CHUNK, per), 1) == target_ref[j * CHUNK : (j + 1) * CHUNK, :])
         out = matmul(hot, rows_ref[j * per : (j + 1) * per, :])
         out = low(out + mat_trans(left_ref[j * CHUNK : (j + 1) * CHUNK, :], right))
-        for k in range(2):
-            row = pl.multiple_of(index_ref[2 * j + k] * piece, piece)
-            out_ref[pl.ds(row, piece), :] = out[k * piece : (k + 1) * piece, :]
-
-
-def expert_out(act, share, own, other, target, left, right, index):
+        out_refs[j // 2][(j % 2) * CHUNK : (j % 2 + 1) * CHUNK, :] = out
+
+
+def expert_out(act, share, own, other, target, left, right):
     slots, hidden = act.shape
     rows, columns = left.shape
     width = right.shape[0]
     tile = 256
     steps = width // tile // 2
-    args = [index, act, share, own[2], other[2], target, left, right]
+    args = [act, share, own[2], other[2], target, left, right]
     specs = [
-        pl.BlockSpec(memory_space=pltpu.SMEM), whole_spec(act), whole_spec(share),
+        whole_spec(act), whole_spec(share),
         pl.BlockSpec((hidden, tile), lambda i: (0, jnp.minimum(i, steps - 1))),
         pl.BlockSpec((hidden, tile), lambda i: (0, jnp.maximum(i - steps, 0))),
         whole_spec(target), whole_spec(left), pl.BlockSpec((tile, columns), lambda i: (i, 0)),
     ]
-    outs = [shaped((rows, width), BF)]
-    out_specs = [pl.BlockSpec((rows, tile), lambda i: (0, i))]
+    outs = [shaped((rows // 4, width), BF)] * 4
+    out_specs = [pl.BlockSpec((rows // 4, tile), lambda i: (0, i))] * 4
     flops = 2 * slots * width * hidden + 2 * rows * width * (columns + slots // 8)
     return tiled_call(
         functools.partial(out_kernel, slots // 8), 2 * steps, args, specs, outs, out_specs,
         (pltpu.VMEM((slots, tile), BF),), flops=flops,
-    )[0]
+    )
 
 
 def shared_kernel(part, count, *refs):
@@ -696,7 +800,6 @@
     me = lax.axis_index("expert")
     dp = lax.axis_index("dp")
     core, x, z = me % 2, (me // 2) % 2, me // 4
-    scalars = jnp.stack([dp, z, x, core]).astype(jnp.int32)
 
     def turn(value):
         if not two:
@@ -750,10 +853,15 @@
     def as_row(value):
         return jnp.pad(value.reshape(1, -1), ((0, 0), (0, own_rows - value.size)))
 
-    small = [as_row(norm_in), as_row(norm_mid), as_row(latent_gain), as_row(low(lengths)), gate_high, gate_low]
-    small = jnp.concatenate(small, axis=0)
     small_rows = 48
-    small = jnp.pad(small, ((0, small_rows - small.shape[0]), (0, 0)))
+    lat_gain_rows = lax.dynamic_update_slice(jnp.zeros((LAT,), BF), latent_gain, ((dp * experts + me) * lat_rows,))
+    small = jnp.concatenate(
+        [
+            as_row(jnp.concatenate([norm_in, norm_mid])), lat_gain_rows.reshape(4, 128), as_row(low(lengths)),
+            jnp.zeros((10, own_rows), BF), gate_high, gate_low,
+        ],
+        axis=0,
+    )
 
     s_piece = jnp.concatenate(
         [
@@ -774,73 +882,74 @@
         lat = jnp.concatenate([wide_lat[:, :384], jnp.concatenate([wide_lat[:, 384:], low_rows], axis=1)], axis=0)
     else:
         lat = small
-    moved, _, _, _ = clock.slot((core_swap, away), (z_two, lat), (z_up, lat), (z_down, lat), (z_up, x0))
-    x1 = moved[4]
-    lats = jnp.stack([lat, moved[2], moved[1], moved[3]])
-    facts = lats[:, shard : shard + small_rows, 256:] if two else lats
+    s_kept, s_away = at(s_piece, core, 2), at(s_piece, 1 - core, 2)
+    clock.slot(feed=0.6)
+    moved, _, _, _ = clock.slot((core_swap, away), (core_swap, s_away), (z_up, x0), feed=0.55)
+    x1 = moved[2]
+    s_piece = jnp.stack([s_kept, moved[1]], axis=2)
     w_own = jnp.where(
         core == 0, jnp.concatenate([kept, moved[0]], axis=1), jnp.concatenate([moved[0], kept], axis=1)
     )
+    if two:
+        w_own = jnp.concatenate([w_own, jnp.broadcast_to(lat, (4,) + lat.shape)], axis=2)
+    s_kept, s_away = at(s_piece, x, 1), at(s_piece, 1 - x, 1)
     moved, _, _, _ = clock.slot(
         (z_two, at(w_own, (z + 2) % 4, 0)),
         (z_up, at(w_own, (z + 1) % 4, 0)),
         (z_down, at(w_own, (z + 3) % 4, 0)),
-        (core_swap, facts),
-        feed=0.75,
+        (x_swap, s_away),
+        feed=1.1,
     )
     w_own = jnp.stack([at(w_own, z, 0), moved[1], moved[0], moved[2]])
-    facts_few = jnp.concatenate([facts, moved[3]])
+    s_piece = jnp.stack([s_kept, moved[3]], axis=1)
     if two:
-        w_own = jnp.concatenate([w_own, lats], axis=2)
-    s_kept, s_away = at(s_piece, core, 2), at(s_piece, 1 - core, 2)
-
-    def tables_of(facts):
-        lengths_few = facts[:, 3, : lengths.size].astype(jnp.int32).reshape(8 * micro, lengths.shape[1])
-        position, doc = layout(lengths_few, rows)
-        freq = jnp.power(10000.0, -2.0 * jnp.arange(RD // 2, dtype=F32) / RD)
-        theta = position.reshape(-1, 1) * freq
-        cosine, sine = jnp.cos(theta), jnp.sin(theta)
-        cosine = jnp.concatenate([cosine] * 4, axis=1)
-        sine = jnp.concatenate([-sine, sine, -sine, sine], axis=1)
-        ids = doc + 4 * jnp.arange(8 * micro, dtype=jnp.int32)[:, None]
-        return cosine, sine, ids.reshape(-1, 1), ids.reshape(-1, 1, CHUNK)
-
-    moved, _, _, made = clock.slot(
-        (x_swap, w_own), (z_up, x1), (z_up, g0), *lane(w_own), (core_swap, x0), work=[(tables_of, facts_few)]
-    )
-    tables = made[0]
-    w_x, x2, g1 = moved[:3]
-    cx0 = moved[-1]
+        lats = w_own[..., W_COLS:]
+        facts = lats[:, shard : shard + small_rows, 256:]
+    else:
+        facts = jnp.stack([lat, z_up(lat), z_two(lat), z_down(lat)])
+
+    moved, _, _, _ = clock.slot(
+        (x_swap, w_own), *lane(w_own), (z_up, x1), (z_up, g0), (core_swap, lats if two else facts)
+    )
+    w_x, x2, g1, lat_other = moved[0], *moved[-3:]
+    facts_few = jnp.concatenate([facts, lat_other[:, shard : shard + small_rows, 256:] if two else lat_other])
+    lengths_few = facts_few[:, 5, : lengths.size].astype(jnp.int32).reshape(-1)
+    scalars = jnp.concatenate([jnp.stack([dp, z, x, core]).astype(jnp.int32), lengths_few])
+    table = jnp.asarray(angle_table(rows))
+    s_two, s_up, s_down = (at(s_piece, (z + k) % 4, 0) for k in (2, 1, 3))
     if two:
-        w_y = moved[3]
-        lat_near = jnp.concatenate([lats, w_x[..., W_COLS:], w_y[..., W_COLS:]])
+        w_y = moved[1]
         moved, _, _, _ = clock.slot(
-            (x_swap, w_y[:2]), (dp_swap, w_x[2:]), (z_up, x2), (core_swap, x1), (core_swap, lat_near)
+            (x_swap, w_y[:2]), (dp_swap, w_x[2:]), (z_up, x2),
+            (core_swap, jnp.concatenate([w_x[..., W_COLS:], w_y[..., W_COLS:]])),
+            (core_swap, jnp.concatenate([x0, x1])),
         )
-        w_far, x3, cx1, lat_other = moved[:2], *moved[2:]
+        w_far, x3, lat_other_xy, cx01 = moved[:2], *moved[2:]
         lat_far = jnp.concatenate([w_far[0][..., W_COLS:], w_far[1][..., W_COLS:]])
-        device = jnp.arange(devices, dtype=jnp.int32)
-        place = (device // 2 % 2 ^ x) + 2 * (device // 16 ^ dp)
-        place = (device % 2 ^ core) * 16 + place * 4 + (z + 4 - device // 4 % 4) % 4
-        moved, _, _, _ = clock.slot((core_swap, lat_far), (core_swap, x3), (core_swap, x2), feed=0.35)
-        cx3, cx2 = moved[1:]
+        moved, _, _, _ = clock.slot(
+            (core_swap, lat_far), (core_swap, jnp.concatenate([x2, x3])), (z_up, s_up), feed=0.35
+        )
+        cx23, s_up = moved[1:]
         weights = [w_own, w_x, w_y] + w_far
         layout_of = ((0, 0, 0), (1, 0, 0), (0, 1, 0), (1, 1, 0), (1, 1, 2))
-        w_lat = [lat_other, moved[0]]
-        every = [lat_near, lat_far, lat_other, moved[0]]
-        facts = reorder([jnp.concatenate([part[:, shard : shard + 16, 256:] for part in every])], place)[0]
-        gain_in = wide(facts[:, 0, :shard]).reshape(1, width)
-        gain_lat = wide(facts[:, 2, :lat_rows]).reshape(1, LAT)
-        w_exp = gain_lat
+        w_lat = [lat_other, lat_other_xy, moved[0]]
+        w_exp = gains = gain_lat = jnp.zeros((8, 128), F32)
+        route_from = [w_own, w_x, lat_other, lat_other_xy]
+        route_lanes = (W_COLS + 256, W_COLS + 256, 256, 256)
     else:
-        x3 = z_up(x2)
-        cx1, cx2, cx3 = core_swap(x1), core_swap(x2), core_swap(x3)
+        x3, s_up = z_up(x2), z_up(s_up)
+        cx01, cx23 = core_swap(jnp.concatenate([x0, x1])), core_swap(jnp.concatenate([x2, x3]))
         near, far = dp_gather(w_own[None], 0), dp_gather(w_x[None], 0)
         weights = [near[i] for i in range(ndp)] + [far[i] for i in range(ndp)]
         layout_of = tuple((side, j, 0) for side in range(2) for j in range(ndp))
         w_lat = lax.all_gather(w_latent, ("dp", "expert"), axis=0)
         w_lat = [w_lat[i][None] for i in range(devices)]
         facts = lax.all_gather(small, ("dp", "expert"), axis=0)
+        gains = wide(facts[:, 0, : 2 * shard]).reshape(devices, 2, shard).transpose(1, 0, 2).reshape(2, width)
+        gain_lat = wide(facts[:, 1:5]).sum(axis=0).reshape(1, LAT)
+        route_from = jnp.take(lax.dynamic_slice_in_dim(facts, dp * experts, experts, 0), row_index, axis=0)
+        route_from = [route_from[4 * i : 4 * i + 4] for i in range(4)]
+        route_lanes = (0, 0, 0, 0)
         w_exp = jnp.concatenate([value[..., Q_COLS + O_COLS :] for value in weights], axis=0)
         w_exp = w_exp.reshape(2, ndp, 4, 2 * shard, E_COLS).transpose(1, 2, 0, 3, 4)
         w_exp = w_exp.reshape(devices // 2, -1, E_COLS)
@@ -848,204 +957,208 @@
         chip_index = chips // 8 * 8 + ((z + 4 - chips // 2 % 4) % 4) * 2 + (chips % 2 ^ x)
         w_exp = reorder([w_exp], chip_index)[0]
         w_exp = w_exp.reshape(devices, groups, lat_rows, E_COLS).transpose(0, 2, 1, 3).reshape(LAT, groups * E_COLS)
-        gain_in = wide(facts[:, 0, :shard]).reshape(1, width)
-        gain_lat = wide(facts[:, 2, :lat_rows]).reshape(1, LAT)
-        every = None
-
-    def facts_of(facts, every):
-        if two:
-            facts = reorder([jnp.concatenate([part[:, shard : shard + small_rows, 256:] for part in every])], place)[0]
-        return facts, wide(facts[:, 1, :shard]).reshape(1, width)
-
-    def routing_of(facts):
-        group = wide(lax.dynamic_slice_in_dim(facts, dp * experts, experts, 0))
-        gate_all = group[:, 4 : 4 + 2 * experts].reshape(experts, 2, experts, own_rows)
-        gate_all = jnp.take(at(gate_all, me, 2).sum(axis=1), row_index, axis=0).reshape(blocks, rows)
-        routed = (gate_all > 0.0).astype(jnp.int32)
-        in_chunk = jnp.arange(blocks, dtype=jnp.int32)[:, None] % (CHUNK // rows)
-        target = jnp.where(routed > 0, in_chunk * cap + jnp.cumsum(routed, axis=1) - 1, -1)
-        return target.reshape(all_rows, 1), target.reshape(-1, 1, CHUNK), gate_all.reshape(-1, 1, CHUNK)
-
-    def small_facts(facts, every):
-        facts, gain_mid = facts_of(facts, every)
-        return routing_of(facts) + (gain_mid,)
-
-    x_pieces = [x0, x1, x2, x3, cx0, cx1, cx2, cx3]
+    slots = blocks * cap
+    route = functools.partial(routing, first=(shard if two else 0) + 16, lanes=route_lanes, slots=cap)
+
+    x_pieces = [x0, x1, x2, x3, cx01, cx23]
     moved, _, _, made = clock.slot(
-        (x_swap, g0), (z_up, g1), (core_swap, s_away),
-        feed=0.9,
+        (x_swap, g0), (z_up, g1), (z_down, g0),
+        feed=0.95,
         work=[
             (
                 lambda *a: attention_forward(*a[:3], layout_of, *a[3:], split=two),
-                scalars, x_pieces, weights, w_lat, w_exp, gain_in, gain_lat, tables,
+                scalars, x_pieces, weights, w_lat, w_exp, gains, gain_lat, table,
             )
         ],
     )
-    gx0, g2 = moved[:2]
-    s_piece = jnp.stack([s_kept, moved[2]], axis=2)
+    gx0, g2, g3 = moved
     (part_near, part_far), saved = made[0]
-
-    s_kept, s_away = at(s_piece, x, 1), at(s_piece, 1 - x, 1)
-    moved, _, _, _ = clock.slot((core_swap, part_far), (z_up, g2), (x_swap, g1), feed=0.6)
-    g3, gx1 = moved[1:]
+    gain_in, gain_mid, gain_lat = saved[-3:]
+
+    moved, _, _, _ = clock.slot((core_swap, part_far), (z_two, s_two), (z_down, s_down), feed=0.65)
+    s_two, s_down = moved[1:]
+    s_piece = jnp.stack([at(s_piece, z, 0), s_up, s_two, s_down]).reshape(experts, shard, 3 * ff_part)
     g_near = jnp.concatenate([g0, g1, g2, g3])
     terms = [wide(cut(part_near, k)) + wide(cut(moved[0], k)) for k in range(4)]
     moved, _, _, made = clock.slot(
-        (z_down, low(terms[3])), (x_swap, g2), work=[(small_facts, facts, every)], feed=0.67
-    )
-    gx2 = moved[1]
-    target_col, target_row, gate_row, gain_mid = made[0]
+        (z_down, low(terms[3])), (x_swap, g1), work=[(route, me.reshape(1), route_from)], feed=0.67
+    )
+    gx1 = moved[1]
+    target_row, gate_row, target_col = made[0]
     moved, _, _, _ = clock.slot(
-        (z_down, low(terms[2] + wide(moved[0]))), (x_swap, g3), (core_swap, g_near), feed=0.67
-    )
-    gx3, cg_near = moved[1:]
-    moved, _, _, _ = clock.slot((z_down, low(terms[1] + wide(moved[0]))), (x_swap, s_away), feed=0.67)
-    s_piece = jnp.stack([s_kept, moved[1]], axis=1)
+        (z_down, low(terms[2] + wide(moved[0]))), (x_swap, g2), (core_swap, g_near), feed=0.67
+    )
+    gx2, cg_near = moved[1:]
+    moved, _, _, _ = clock.slot((z_down, low(terms[1] + wide(moved[0]))), (x_swap, g3), feed=0.67)
+    gx3 = moved[1]
     xf = wide(tokens)
     mid = xf + terms[0] + wide(moved[0])
     scale_mid = rms_scale(mid)
     t0 = turn(low(mid * scale_mid * gain_mid))
 
-    slots = blocks * cap
     g_far = jnp.concatenate([gx0, gx1, gx2, gx3])
-    moved, _, _, _ = clock.slot((z_up, t0), (x_swap, t0), feed=0.67)
+    join = lambda *pieces: jnp.concatenate(pieces, axis=0)
+    moved, _, _, made = clock.slot(
+        (z_up, t0), (x_swap, t0), work=[(join, *fetched[0][2])] if two else [], feed=0.67
+    )
     t1, tx0 = moved
+    down_got = made
     moved, _, _, _ = clock.slot((z_up, t1), (x_swap, t1), (core_swap, g_far), feed=0.67)
     t2, tx1, cg_far = moved
     g_pieces = [g0, g1, g2, g3, gx0, gx1, gx2, gx3, cg_near, cg_far]
+    part = experts // 2
     moved, _, _, made = clock.slot(
-        (z_up, t2), (x_swap, t2),
-        feed=0.67,
+        (z_up, t2), (x_swap, t2), *lane(s_piece[:part]), (core_swap, tx0),
         work=[(functools.partial(enter_grad, slots=slots), g_pieces, target_row, gate_row)],
     )
-    t3, tx2 = moved
+    t3, tx2 = moved[:2]
+    s_got, ctx0 = moved[2:-1], moved[-1]
     *rows_g, share = made[0]
     t_near = jnp.concatenate([t0, t1, t2, t3])
-    moved, s_begun, _, _ = clock.slot(
-        (x_swap, t3), (core_swap, t_near), begin=[(z_two, at(s_piece, (z + 2) % 4, 0))], feed=0.67
-    )
-    tx3, ct_near = moved
-    t_far = jnp.concatenate([tx0, tx1, tx2, tx3])
-    moved, more, _, _ = clock.slot(
-        (core_swap, t_far),
-        begin=[(z_up, at(s_piece, (z + 1) % 4, 0)), (z_down, at(s_piece, (z + 3) % 4, 0))],
-        feed=0.67,
-    )
-    t_pieces = [t0, t1, t2, t3, tx0, tx1, tx2, tx3, ct_near, moved[0]]
-
-    _, _, ended, made = clock.slot(
-        end=more + s_begun, work=[(functools.partial(dispatch, slots=slots), t_pieces, target_row)], feed=2.0
-    )
-    rows_x = made[0]
-    s_piece = jnp.stack([at(s_piece, z, 0), ended[0], ended[2], ended[1]]).reshape(experts, shard, 3 * ff_part)
+    moved, _, _, made = clock.slot(
+        (x_swap, t3), (core_swap, t_near), *lane(s_piece[part:]), (core_swap, tx1),
+        work=[(join, *fetched[1][2])] if two else [],
+    )
+    tx3, ct_near = moved[:2]
+    s_got, ctx1 = s_got + moved[2:-1], moved[-1]
+    gate_got = made
     if two:
-        own, other = own_expert, [joined(fetched[i]) for i in (1, 2, 0)]
+        s_pieces = [s_piece, jnp.concatenate(s_got)]
+    else:
+        s_pieces = jnp.split(dp_gather(s_piece[None], 0), ndp)
+        s_pieces = [value.reshape(s_piece.shape) for value in s_pieces]
+    moved, _, _, made = clock.slot(
+        (core_swap, tx2), (core_swap, tx3), feed=0.4,
+        work=[(lambda *a: shared_weights(a, block_index, ff_pad), *s_pieces)],
+    )
+    s_both, s_down_w = made[0]
+    t_pieces = [t0, t1, t2, t3, tx0, tx1, tx2, tx3, ct_near, ctx0, ctx1, *moved]
+
+    _, _, _, made = clock.slot(
+        work=[
+            (functools.partial(dispatch, slots=slots), t_pieces, target_row),
+            (hidden_shared, t_pieces, g_pieces, s_both, s_down_w),
+        ],
+        feed=3.0,
+    )
+    rows_x, (s_act, d_s_pre) = made
+    if two:
+        assert all(entry[1] == entry[0].shape[0] for entry in fetched)
+        own, other = own_expert, [gate_got[0], join(*fetched[2][2]), down_got[0]]
     else:
         full = [dp_gather(own_expert[0], 0), dp_gather(own_expert[1], 0), dp_gather(own_expert[2], 1)]
         own = [full[0][:half], full[1][:half], full[2][:, :half]]
         other = [full[0][half:], full[1][half:], full[2][:, half:]]
-    s_got, _, _, made = clock.slot(*lane(s_piece), work=[(expert_hidden, rows_x, rows_g, own, other)])
-    e_act, d_gate, d_up = made[0]
-    s_pieces = [s_piece, s_got[0]] if two else jnp.split(dp_gather(s_piece[None], 0), ndp)
-    s_pieces = [value.reshape(s_piece.shape) for value in s_pieces]
-    _, _, _, made = clock.slot(work=[(contract, e_act, rows_g[1])])
+    _, _, _, made = clock.slot(work=[(expert_hidden, rows_x, rows_g, own, other)])
+    e_act, d_gate, d_up, d_down_away = made[0]
     if two:
-        sent = [clock.add(low(made[0]))]
+        sent = [clock.add(d_down_away)]
 
     _, _, _, made = clock.slot(
-        feed=0.2, work=[(lambda *a: shared_weights(a, block_index, ff_pad), *s_pieces)]
-    )
-    s_both, s_down = made[0]
-    _, _, _, made = clock.slot(work=[(hidden_shared, t_pieces, g_pieces, s_both, s_down)], feed=0.8)
-    s_act, d_s_pre = made[0]
-    _, _, _, made = clock.slot(
-        work=[(expert_back, d_gate, d_up, own, other, target_col, d_s_pre, s_both)], feed=1.3
-    )
-    near, far = made[0]
-    quads = 4 * own_rows
-    moved, _, _, made = clock.slot((core_swap, far[quads:]), work=[(contract, rows_x[1], d_gate)], feed=0.25)
+        work=[(expert_back, d_gate, d_up, own, other, target_col, d_s_pre, s_both)], feed=1.35
+    )
+    near, near_x, far, far_x = made[0]
+    moved, _, _, made = clock.slot((core_swap, far_x), work=[(contract, rows_x[1], d_gate)], feed=0.3)
     if two:
         sent.append(clock.add(low(made[0])))
-    away = [low(wide(cut(near[quads:], k)) + wide(cut(moved[0], k))) for k in range(4)]
+    away = [low(wide(cut(near_x, k)) + wide(cut(moved[0], k))) for k in range(4)]
     moved, _, _, made = clock.slot(
-        (x_swap, away[3]), (core_swap, far[:quads]), work=[(contract, rows_x[1], d_up)], feed=0.65
-    )
-    if two:
-        sent.append(clock.add(low(made[0])))
+        (x_swap, away[3]), (core_swap, far),
+        feed=0.72,
+        work=[(functools.partial(shared_gradient, part=ff_part), t_pieces, g_pieces, d_s_pre, s_act)],
+    )
+    d_shared = made[0].reshape(ndp, experts, shard, 3 * ff_part)
     home = [wide(cut(near, k)) + wide(cut(moved[1], k)) for k in range(4)]
     moved, _, _, made = clock.slot(
         (x_swap, away[2]), (z_down, low(home[3] + wide(moved[0]))),
-        feed=0.85,
-        work=[(expert_out, e_act, share, own, other, target_col, s_act, s_down, row_index)],
-    )
-    out_part = made[0]
+        feed=0.8,
+        work=[(expert_out, e_act, share, own, other, target_col, s_act, s_down_w)],
+    )
+    o_near, o_near_x, o_far, o_far_x = made[0]
+    s_away = d_shared[-1]
     moved, _, _, made = clock.slot(
-        (x_swap, away[1]), (z_down, low(home[2] + wide(moved[0]) + wide(moved[1]))),
-        work=[(contract, e_act, rows_g[0])], feed=0.65,
-    )
-    d_down_home = made[0]
+        (x_swap, away[1]), (z_down, low(home[2] + wide(moved[0]) + wide(moved[1]))), (core_swap, o_far_x),
+        *lane(s_away[:part]),
+        work=[(contract, rows_x[1], d_up), (contract, e_act, rows_g[0])],
+    )
+    d_down_home = made[1]
+    if two:
+        sent.append(clock.add(low(made[0])))
+    s_got = moved[3:]
+    o_away = [low(wide(cut(o_near_x, k)) + wide(cut(moved[2], k))) for k in range(4)]
     moved, _, _, made = clock.slot(
-        (x_swap, away[0]), (z_down, low(home[1] + wide(moved[0]) + wide(moved[1]))),
-        work=[(contract, rows_x[0], d_gate)], feed=0.65,
+        (x_swap, away[0]), (z_down, low(home[1] + wide(moved[0]) + wide(moved[1]))), (core_swap, o_far),
+        *lane(s_away[part:]),
+        work=[(contract, rows_x[0], d_gate)],
     )
     d_gate_home = made[0]
-    out_sum = lax.psum_scatter(clock.tie(out_part), "expert", scatter_dimension=0, tiled=True)
+    s_got += moved[3:]
+    o_home = [wide(cut(o_near, k)) + wide(cut(moved[2], k)) for k in range(4)]
+    if two:
+        d_shared = low(wide(d_shared[0]) + wide(jnp.concatenate(s_got)))
+    else:
+        d_shared = dp_scatter(d_shared)[0]
+    d_shared = d_shared.reshape(4, 2, 2, shard, 3 * ff_part)
     d_mid_normed = turn(home[0] + wide(moved[0]) + wide(moved[1]))
     d_mid_in, d_gain_mid = rms_back(d_mid_normed, mid, scale_mid, gain_mid)
     d_mid = cotangent + d_mid_in
 
     a0 = low(d_mid)
     moved, _, _, made = clock.slot(
-        (z_up, a0),
-        feed=0.7,
-        work=[(functools.partial(shared_gradient, part=ff_part), t_pieces, g_pieces, d_s_pre, s_act)],
-    )
-    a1 = moved[0]
-    d_shared = made[0].reshape(ndp, experts, shard, 3 * ff_part)
-    part = experts // 2
-    moved, _, _, made = clock.slot((z_up, a1), *lane(d_shared[1, :part]), work=[(contract, rows_x[0], d_up)])
-    a2, s_got = moved[0], moved[1:]
+        (z_up, a0), (x_swap, o_away[3]), feed=0.7, work=[(contract, rows_x[0], d_up)]
+    )
+    a1, ox = moved
     d_up_home = made[0]
-    moved, _, _, _ = clock.slot((z_up, a2), *lane(d_shared[1, part:]))
-    a3 = moved[0]
-    if two:
-        d_shared = low(wide(d_shared[0]) + wide(jnp.concatenate([s_got[0], moved[1]])))
-    else:
-        d_shared = dp_scatter(d_shared)[0]
-    d_shared = d_shared.reshape(4, 2, 2, shard, 3 * ff_part)
+    s_kept, s_away = at(d_shared, x, 1), at(d_shared, 1 - x, 1)
+    moved, _, _, _ = clock.slot(
+        (z_up, a1), (x_swap, o_away[2]), (z_down, low(o_home[3] + wide(ox))), (x_swap, o_away[0]), feed=0.9
+    )
+    a2, ox, o_sum, ox0 = moved
+    o_sum = low(o_home[2] + wide(ox) + wide(o_sum))
+    moved, _, _, _ = clock.slot((z_up, a2), (x_swap, o_away[1]), (z_down, o_sum), (x_swap, s_away), feed=0.95)
+    a3, ox, o_sum, s_got = moved
+    o_sum = low(o_home[1] + wide(ox) + wide(o_sum))
+    d_shared = jnp.stack([s_kept, s_got], axis=1)
     a_near = jnp.concatenate([a0, a1, a2, a3])
-    moved, _, _, _ = clock.slot((core_swap, a_near), feed=0.25)
+    moved, _, _, _ = clock.slot((core_swap, a_near), feed=0.35)
     a_pieces = [a0, a1, a2, a3, moved[0]]
+    backward = functools.partial(attention_backward, lat_rows=lat_rows)
     moved, _, _, made = clock.slot(
         (z_two, at(d_shared, (z + 2) % 4, 0)), (z_up, at(d_shared, (z + 1) % 4, 0)),
-        (z_down, at(d_shared, (z + 3) % 4, 0)),
-        feed=1.0,
-        work=[(attention_backward, scalars, x_pieces, a_pieces, saved, gain_in, gain_lat, tables)],
+        (z_down, at(d_shared, (z + 3) % 4, 0)), (z_down, o_sum),
+        feed=1.4,
+        work=[(backward, scalars, x_pieces, a_pieces, saved, d_gain_mid.reshape(1, width), table)],
     )
     d_shared = jnp.stack([at(d_shared, z, 0), moved[1], moved[0], moved[2]])
-    d_norm, d_head, d_wl, d_we, d_gain_in, d_gain_lat = made[0]
+    o_last = o_home[0] + wide(ox0) + wide(moved[3])
+    d_norm, d_head, d_wl = made[0]
     same_x = [[i for i in range(experts) if i // 2 % 2 == side] for side in range(2)]
     d_normed = lax.psum_scatter(d_norm, "expert", scatter_dimension=0, axis_index_groups=same_x, tiled=True)
 
-    d_we = d_we.reshape(devices, lat_rows, groups, E_COLS).transpose(0, 2, 1, 3).reshape(width, E_COLS)
-    d_head = jnp.concatenate([d_head, d_we], axis=1).reshape(ndp, 4, 2, 2 * shard, W_COLS)
-    gains = [d_gain_in.reshape(width, 1), d_gain_mid.reshape(width, 1)]
-    gains.append(jnp.pad(d_gain_lat.reshape(devices, lat_rows), ((0, 0), (0, shard - lat_rows))).reshape(width, 1))
-    d_wl = jnp.concatenate([d_wl[:, :lat_cols]] + [low(value) for value in gains], axis=1)
-    d_wl = jnp.pad(d_wl, ((0, 0), (0, -d_wl.shape[1] % 128))).reshape(ndp, 4, 2, 2, shard, -1)
-    s_kept, s_away = at(d_shared, x, 1), at(d_shared, 1 - x, 1)
+    if not two:
+        d_head = d_head.reshape(ndp, 4, 2, 2 * shard, W_COLS)
+        d_wl = d_wl.reshape(ndp, 4, 2, 2, shard, -1)
+    s_kept, s_away = at(d_shared, core, 2), at(d_shared, 1 - core, 2)
+
+    def add_received(home, *pieces):
+        return home + wide(jnp.concatenate(pieces))
+
     if two:
-        first, second = d_head[:, :2], d_head[:, 2:]
-        moved, _, _, _ = clock.slot(
-            (x_swap, at(first, 1 - x, 2)), (dp_swap, at(second, 1 - dp, 0)), (core_swap, at(d_wl, 1 - core, 3))
+        moved, _, _, made = clock.slot(
+            (x_swap, d_head[4:8]), (dp_swap, d_head[12:]), (core_swap, d_wl[1]), (core_swap, s_away),
+            work=[(add_received, d_down_home, *sent[0][2])],
         )
-        first = wide(at(first, x, 2)) + wide(moved[0])
-        second = wide(at(second, dp, 0)) + wide(moved[1])
-        d_wl = wide(at(d_wl, core, 3)) + wide(moved[2])
-        moved, _, _, _ = clock.slot(
+        d_down = made[0]
+        first = (wide(d_head[:4]) + wide(moved[0])).reshape(ndp, 2, 2 * shard, W_COLS)
+        second = (wide(d_head[8:12]) + wide(moved[1])).reshape(2, 2, 2 * shard, W_COLS)
+        d_wl = (wide(d_wl[0]) + wide(moved[2])).reshape(ndp, 4, 2, shard, -1)
+        d_shared = jnp.stack([s_kept, moved[3]], axis=2)
+        moved, _, _, made = clock.slot(
             (dp_swap, low(at(first, 1 - dp, 0))), (x_swap, low(at(second, 1 - x, 1))),
-            (x_swap, low(at(d_wl, 1 - x, 2))), feed=0.6,
+            (x_swap, low(at(d_wl, 1 - x, 2))), feed=0.65,
+            work=[(add_received, d_gate_home, *sent[1][2])],
         )
+        d_gate_all = made[0]
         first = at(first, dp, 0) + wide(moved[0])
         second = at(second, x, 1) + wide(moved[1])
         d_wl = at(d_wl, x, 2) + wide(moved[2])
@@ -1055,29 +1168,30 @@
         d_head = dp_scatter(low(d_head))[0]
         d_wl = wide(at(d_wl, core, 3)) + wide(core_swap(at(d_wl, 1 - core, 3)))
         d_wl = at(d_wl, x, 2) + wide(x_swap(low(at(d_wl, 1 - x, 2))))
-    moved, _, ended, _ = clock.slot(
+        d_shared = jnp.stack([s_kept, core_swap(s_away)], axis=2)
+        o_last = o_last + wide(z_down(o_sum))
+    d_shared = d_shared.reshape(experts, shard, 3 * ff_part)
+    moved, _, _, _ = clock.slot(
         (z_two, at(d_head, (z + 2) % 4, 0)), (z_down, at(d_head, (z + 3) % 4, 0)),
-        (z_up, at(d_head, (z + 1) % 4, 0)), (x_swap, s_away), *(lane(low(at(d_wl, 1 - dp, 0))) if two else []),
-        end=[out_sum], feed=2.0,
+        (z_up, at(d_head, (z + 1) % 4, 0)),
+        *(lane(low(at(d_wl, 1 - dp, 0))) if two else []), feed=3.0,
     )
     d_head = jnp.stack([at(d_head, z, 0), moved[1], moved[0], moved[2]]).reshape(4, 2, shard, W_COLS)
-    d_shared = jnp.stack([s_kept, moved[3]], axis=1)
-    d_wl = at(d_wl, dp, 0) + wide(moved[4]) if two else wide(dp_scatter(low(d_wl))[0])
-    out = low(mid + turn(wide(ended[0])))
-    s_kept, s_away = at(d_shared, core, 2), at(d_shared, 1 - core, 2)
-    moved, _, ended, _ = clock.slot(
+    d_wl = at(d_wl, dp, 0) + wide(moved[3]) if two else wide(dp_scatter(low(d_wl))[0])
+    out = low(mid + turn(o_last))
+    moved, _, ended, made = clock.slot(
         (core_swap, at(d_head, 1 - core, 1)), (z_two, low(at(d_wl, (z + 2) % 4, 0))),
-        (z_down, low(at(d_wl, (z + 3) % 4, 0))), (z_up, low(at(d_wl, (z + 1) % 4, 0))), (core_swap, s_away),
-        end=[d_normed],
-    )
+        (z_down, low(at(d_wl, (z + 3) % 4, 0))), (z_up, low(at(d_wl, (z + 1) % 4, 0))),
+        end=[d_normed], work=[(add_received, d_up_home, *sent[2][2])] if two else [],
+    )
+    d_up_all = made[0] if two else None
     d_head = jnp.stack([at(d_head, core, 1), moved[0]], axis=1).reshape(pairs, shard, W_COLS)
     d_wl = at(d_wl, z, 0) + wide(moved[1]) + wide(moved[2]) + wide(moved[3])
-    d_shared = jnp.stack([s_kept, moved[4]], axis=2).reshape(experts, shard, 3 * ff_part)
     d_normed = wide(ended[0])
 
     if two:
-        got = [wide(joined(entry)) for entry in sent]
-        d_expert = [d_gate_home + got[1], d_up_home + got[2], d_down_home + got[0]]
+        assert all(entry[1] == entry[0].shape[0] for entry in sent)
+        d_expert = [d_gate_all, d_up_all, d_down]
     else:
         d_expert = [
             wide(dp_scatter(low(jnp.concatenate([contract(value, d) for value in rows_x]))))

time: 866 us -> 802 us (0.926)
  local copies, waits for them, and re-layouts: 144 us -> 84.2 us
  starting transfers between devices: 112 us -> 148 us
  waiting for transfers between devices: 279 us -> 256 us
  other arithmetic: 86.8 us -> 76.9 us
    ppermute x75 -> x82, starting transfers between devices: 75.1 us -> 108 us  [move(): return lax.ppermute(value, 'expert', [(i, to(i)) for i in range(16)])]
    ppermute x75 -> x82, waiting for transfers between devices: 214 us -> 184 us  [move(): return lax.ppermute(value, 'expert', [(i, to(i)) for i in range(16)])]
    add x7, other arithmetic: 1.9 us -> 21.8 us  [the longest x3 18.4 us: add_received(): return home + wide(jnp.concatenate(pieces))]
    broadcast_in_dim x3 -> x0, other arithmetic: 17.5 us -> none  [the longest x1 7.93 us: local(): d_expert[2][None]]
    unnamed x297 -> x288, local copies, waits for them, and re-layouts: 39.5 us -> 27 us
    slice x10 -> x9, local copies, waits for them, and re-layouts: 9.39 us -> 0.37 us  [the longest x1 0.11 us: local(): s_away[part:]]
    dot_general x6 -> x5, matrix products: 35 us -> 27 us  [contract(): lax.dot_general(left, right, (((0,), (0,)), ((), ())), preferred_element_...]
    ppermute x37 -> x36, waiting for transfers between devices: 65.2 us -> 71.3 us  [dp_swap(): return lax.ppermute(value, 'dp', [(0, 1), (1, 0)])]
  transfers between devices with their start and end apart: 114 -> 119, of which waited for: 45 -> 50; matrix products, arithmetic and copies ran while one was open for 20% -> 16% of each run, Pallas kernels for 21% -> 19%
where the time goes in v3:
time: 802 us; the launch traced here: 792 us
  waiting for transfers between devices  256 us (32%)
  Pallas kernels  183 us (23%)
  starting transfers between devices  148 us (18%)
  local copies, waits for them, and re-layouts  84.2 us (10%)
  other arithmetic  76.9 us (10%)
  matrix products  27 us (3%)
  between operations  16.7 us (2%)
    ppermute x82, waiting for transfers between devices, move(): return lax.ppermute(value, 'expert', [(i, to(i)) for i in range(16)])  184 us
    ppermute x82, starting transfers between devices, move(): return lax.ppermute(value, 'expert', [(i, to(i)) for i in range(16)])  108 us
    pallas_call x10, Pallas kernels, whole_call(): pl.pallas_call(kernel, in_specs=specs, out_specs=[vmem] * len(outs), out_...  106 us
    pallas_call x3, Pallas kernels, tiled_call(): pl.pallas_call(kernel, grid=(steps,), in_specs=specs, out_specs=out_specs...  77.6 us
    ppermute x36, waiting for transfers between devices, dp_swap(): return lax.ppermute(value, 'dp', [(0, 1), (1, 0)])  71.3 us
    ppermute x36, starting transfers between devices, dp_swap(): return lax.ppermute(value, 'dp', [(0, 1), (1, 0)])  40.4 us
    slice x21, local copies, waits for them, and re-layouts, next_rows(): moves.append((self.go, array[start:stop]))  27.5 us
    dot_general x5, matrix products, contract(): lax.dot_general(left, right, (((0,), (0,)), ((), ())), preferred_element_...  27 us
  transfers between devices with their start and end apart: 119, of which 50 were waited for; matrix products, arithmetic and copies ran while one was open for 16% of the time, Pallas kernels for 19%

profile of v3, /device:TPU:0, one launch (start us, length us, event | category | flops | bytes accessed | tf_op | source)
XLA Modules:
  0.0 792.4 jit_solution(1853626767926473176)
XLA Ops:
  53.0 14.7 %collective-permute-done.6 = bf16[128,1152]{1,0:T(8,128)(2,1)S(1)} collective-permute-done((bf16[128,1152]{1,0:T(8,128)(2,1)}, bf16[128,1152]{1,0:T(8,128)(2,1)S(1)}, u32[]{:S(2)}, u32[]{:S(2)}) %collective-permute-start.6) | collective-permute-done | bytes 294944 | tf_op jit(solution)/shard_map/ppermute | solution.py:67
  79.9 10.1 %collective-permute-done.12.refs_2_ = bf16[128,2048]{1,0:T(8,128)(2,1)S(1)} collective-permute-done((bf16[128,2048]{1,0:T(8,128)(2,1)}, bf16[128,2048]{1,0:T(8,128)(2,1)S(1)}, u32[]{:S(2)}, u32[]{:S(2)}) %collective-permute-start.12) | collective-permute-done | bytes 524320 | tf_op jit(solution)/shard_map/ppermute | solution.py:67
  90.0 8.9 %collective-permute-done.13.refs_1_.refs_14_ = bf16[128,2048]{1,0:T(8,128)(2,1)S(1)} collective-permute-done((bf16[128,2048]{1,0:T(8,128)(2,1)S(1)}, bf16[128,2048]{1,0:T(8,128)(2,1)S(1)}, u32[]{:S(2)}, u32[]{:S(2)}) %collective-permute-start.13) | collective-permute-done | bytes 524320 | tf_op jit(solution)/shard_map/ppermute | solution.py:67
  140.8 19.1 %shard_map.298 = (bf16[512,2048]{1,0:T(8,128)(2,1)}, bf16[512,2048]{1,0:T(8,128)(2,1)}, bf16[1024,384]{1,0:T(8,128)(2,1)}, bf16[1024,128]{1,0:T(8,128)(2,1)}, f3...) custom-call(s32[68]{0:T(128)} %concatenate.127.place_ref, ...), custom_call_target="tpu_custom_call" | custom-call | flops 5368709120 | bytes 25294848 | tf_op jit(solution)/shard_map/pallas_call | solution.py:156
  164.5 15.1 %collective-permute-done.31 = bf16[2,2,64,528]{3,2,1,0:T(8,128)(2,1)S(1)} collective-permute-done((bf16[2,2,64,528]{3,2,1,0:T(8,128)(2,1)}, bf16[2,2,64,528]{3,2,1,0:T(8,128)(2,1)S(1)}, u32[]{:S(2)}, u32[]{:S(2)}) %collective-permute-start.31) | collective-permute-done | bytes 270368 | tf_op jit(solution)/shard_map/ppermute | solution.py:67
  186.2 8.2 %collective-permute-start.34 = (bf16[128,2048]{1,0:T(8,128)(2,1)}, bf16[128,2048]{1,0:T(8,128)(2,1)}, u32[]{:S(2)}, u32[]{:S(2)}) collective-permute-start(bf16[128,2048]{1,0:T(8,128)(2,1)} %add_convert_fusion.16), channel_id=1, source_target_pairs={{0,12},{1,13},{2,14},{3,15},{4,0},{5,1},{6,2},{7,3},{8,4},{9,5},{1... | collective-permute-start | bytes 1572872 | tf_op jit(solution)/shard_map/ppermute | solution.py:67
  215.9 7.6 collective-permute-done.37
  230.2 10.4 %collective-permute-start.42 = (bf16[128,2048]{1,0:T(8,128)(2,1)S(1)}, bf16[128,2048]{1,0:T(8,128)(2,1)S(1)}, u32[]{:S(2)}, u32[]{:S(2)}) collective-permute-start(bf16[128,2048]{1,0:T(8,128)(2,1)S(1)} %add_convert_fusion.14), channel_id=1, source_target_pairs={{0,12},{1,13},{2,14},{3,15},{4,0},{5,1},{6,2},{7,3},{8,4},{9,5},{1... | collective-permute-start | bytes 1572872 | tf_op jit(solution)/shard_map/ppermute | solution.py:67
  277.9 13.8 %collective-permute-done.48.refs_2_ = bf16[128,2048]{1,0:T(8,128)(2,1)} collective-permute-done((bf16[128,2048]{1,0:T(8,128)(2,1)S(1)}, bf16[128,2048]{1,0:T(8,128)(2,1)}, u32[]{:S(2)}, u32[]{:S(2)}) %collective-permute-start.48) | collective-permute-done | bytes 524320 | tf_op jit(solution)/shard_map/ppermute | solution.py:67
  320.2 9.7 %collective-permute-done.55.refs_7_ = bf16[128,2048]{1,0:T(8,128)(2,1)S(1)} collective-permute-done((bf16[128,2048]{1,0:T(8,128)(2,1)}, bf16[128,2048]{1,0:T(8,128)(2,1)S(1)}, u32[]{:S(2)}, u32[]{:S(2)}) %collective-permute-start.55) | collective-permute-done | bytes 524320 | tf_op jit(solution)/shard_map/ppermute | solution.py:67
  359.0 15.2 %shard_map.303 = (bf16[2048,256]{1,0:T(8,128)(2,1)}, bf16[2048,512]{1,0:T(8,128)(2,1)}) custom-call(bf16[128,2048]{1,0:T(8,128)(2,1)} %copy-done.9, bf16[128,2048]{1,0:T(8,128)(2,1)} %copy-done.42, bf16[128,2048]{1,0:T(8,128)(2,1)} %collective-permute-done.48.refs_2_, bf16[128,2048]{1,0:T(8,128)(2,1)} %collective-permute-done.51.refs_3_, ...), custom_call_target="tpu_custom_call" | custom-call | flops 6442450944 | bytes 23068672 | tf_op jit(solution)/shard_map/pallas_call | solution.py:156
  375.3 30.9 %shard_map.304 = (bf16[1024,1408]{1,0:T(8,128)(2,1)}, bf16[1024,1408]{1,0:T(8,128)(2,1)}, bf16[1024,1408]{1,0:T(8,128)(2,1)}, bf16[1408,1024]{1,0:T(8,128)(2,1)}) custom-call(bf16[1024,1024]{1,0:T(8,128)(2,1)} %get-tuple-element.911.x0_ref, bf16[1024,1024]{1,0:T(8,128)(2,1)} %get-tuple-element.887.x1_ref, bf16[1024,1024]{1,0:T(8,128)(2,1)} %get-tuple-element.890.r0_ref, ...), custom_call_target="tpu_custom_call" | custom-call | flops 20669530112 | bytes 37224448 | tf_op jit(solution)/shard_map/pallas_call | solution.py:639
  409.7 28.4 %shard_map.305 = (bf16[512,2048]{1,0:T(8,128)(2,1)}, bf16[512,2048]{1,0:T(8,128)(2,1)}, bf16[512,2048]{1,0:T(8,128)(2,1)}, bf16[512,2048]{1,0:T(8,128)(2,1)}) custom-call(bf16[1024,1408]{1,0:T(8,128)(2,1)} %get-tuple-element.902.dg_ref, bf16[1024,1408]{1,0:T(8,128)(2,1)} %get-tuple-element.912.du_ref, bf16[1024,1408]{1,0:T(8,128)(2,1)} %bitcast.226, ...), custom_call_target="tpu_custom_call" | custom-call | flops 17179869184 | bytes 29892608 | tf_op jit(solution)/shard_map/pallas_call | solution.py:639
  458.5 15.1 %shard_map.306 = bf16[2048,528]{1,0:T(8,128)(2,1)} custom-call(bf16[128,2048]{1,0:T(8,128)(2,1)} %copy-done.9, bf16[128,2048]{1,0:T(8,128)(2,1)} %copy-done.42, bf16[128,2048]{1,0:T(8,128)(2,1)} %collective-permute-done.48.refs_2_, bf16[128,2048]{1,0:T(8,128)(2,1)} %collective-permute-done.51.refs_3_, bf16[128,2048]{1,0:T(8,128)(2,1)} %collective-permute-done.46.refs_4_, ...), custom_call_target="tpu_custom_call" | custom-call | flops 6442450944 | bytes 22085632 | tf_op jit(solution)/shard_map/pallas_call | solution.py:156
  481.9 18.4 %shard_map.307 = (bf16[512,2048]{1,0:T(8,128)(2,1)}, bf16[512,2048]{1,0:T(8,128)(2,1)}, bf16[512,2048]{1,0:T(8,128)(2,1)}, bf16[512,2048]{1,0:T(8,128)(2,1)}) custom-call(bf16[1024,1408]{1,0:T(8,128)(2,1)} %get-tuple-element.889.act_ref, f32[1024,1]{1,0:T(8,128)} %get-tuple-element.865.share_ref, bf16[1408,1024]{1,0:T(8,128)(2,1)} %bitcast.230, ...), custom_call_target="tpu_custom_call" | custom-call | flops 9126805504 | bytes 19148800 | tf_op jit(solution)/shard_map/pallas_call | solution.py:639
  573.9 10.1 %collective-permute-done.85.refs_8_ = bf16[128,2048]{1,0:T(8,128)(2,1)S(1)} collective-permute-done((bf16[128,2048]{1,0:T(8,128)(2,1)S(1)}, bf16[128,2048]{1,0:T(8,128)(2,1)S(1)}, u32[]{:S(2)}, u32[]{:S(2)}) %collective-permute-start.85) | collective-permute-done | bytes 524320 | tf_op jit(solution)/shard_map/ppermute | solution.py:67
  583.9 7.5 collective-permute-done.87
  599.3 11.7 %collective-permute-done.90.refs_9_ = bf16[128,2048]{1,0:T(8,128)(2,1)S(1)} collective-permute-done((bf16[128,2048]{1,0:T(8,128)(2,1)S(1)}, bf16[128,2048]{1,0:T(8,128)(2,1)S(1)}, u32[]{:S(2)}, u32[]{:S(2)}) %collective-permute-start.90) | collective-permute-done | bytes 524320 | tf_op jit(solution)/shard_map/ppermute | solution.py:67
  611.0 10.0 %collective-permute-done.91 = bf16[128,2048]{1,0:T(8,128)(2,1)S(1)} collective-permute-done((bf16[128,2048]{1,0:T(8,128)(2,1)S(1)}, bf16[128,2048]{1,0:T(8,128)(2,1)S(1)}, u32[]{:S(2)}, u32[]{:S(2)}) %collective-permute-start.91) | collective-permute-done | bytes 524320 | tf_op jit(solution)/shard_map/ppermute | solution.py:67
  625.0 7.4 collective-permute-done.94
  639.1 30.5 %shard_map.308 = (bf16[1024,2048]{1,0:T(8,128)(2,1)}, bf16[16,128,768]{2,1,0:T(8,128)(2,1)}, bf16[2,16,64,640]{3,2,1,0:T(8,128)(2,1)}, bf16[16,128]{1,0:T(8,128)(2,1)}) custom-call(s32[68]{0:T(128)} %concatenate.127.place_ref, bf16[128,2048]{1,0:T(8,128)(2,1)} %refs_0_.1, bf16[128,2048]{1,0:T(8,128)(2,1)} %collective-permute-done.4.refs_1_, ...), custom_call_target="tpu_custom_call" | custom-call | flops 10737418240 | bytes 28964864 | tf_op jit(solution)/shard_map/pallas_call | solution.py:156
  684.7 11.1 %collective-permute-done.101 = bf16[4,128,768]{2,1,0:T(8,128)(2,1)S(1)} collective-permute-done((bf16[4,128,768]{2,1,0:T(8,128)(2,1)S(1)}, bf16[4,128,768]{2,1,0:T(8,128)(2,1)S(1)}, u32[]{:S(2)}, u32[]{:S(2)}) %collective-permute-start.101) | collective-permute-done | bytes 786464 | tf_op jit(solution)/shard_map/ppermute | solution.py:67
  710.1 11.2 %collective-permute-done.105 = bf16[224,1408]{1,0:T(8,128)(2,1)S(1)} collective-permute-done((bf16[224,1408]{1,0:T(8,128)(2,1)S(1)}, bf16[224,1408]{1,0:T(8,128)(2,1)S(1)}, u32[]{:S(2)}, u32[]{:S(2)}) %collective-permute-start.105) | collective-permute-done | bytes 630816 | tf_op jit(solution)/shard_map/ppermute | solution.py:811
  761.7 7.3 convert_add_fusion
  (692 shorter events, 443.6 us)
Async XLA Ops:
  7.2 761.8 %reduce-scatter.2.cloned.1.call-start = ((), (), s32[]{:S(2)}) async-start(), calls=%async_computation.1 | async-start | bytes 4718592 | tf_op jit(solution)/shard_map/reduce_scatter | solution.py:1136
  46.2 24.6 %collective-permute-start.5 = (bf16[544,1024]{1,0:T(8,128)(2,1)}, bf16[544,1024]{1,0:T(8,128)(2,1)}, u32[]{:S(2)}, u32[]{:S(2)}) collective-permute-start(bf16[544,1024]{1,0:T(8,128)(2,1)} %slice_bitcast_fusion.1), channel_id=1, source_target_pairs={{0,16},{16,0},{1,17},{17,1},{2,18},{18,2},{3,19},{19,3},{4,20},{20... | collective-permute-start | bytes 3342344 | tf_op jit(solution)/shard_map/ppermute | solution.py:811
  71.0 27.8 %collective-permute-start.10 = (bf16[4,128,1152]{2,1,0:T(8,128)(2,1)S(1)}, bf16[4,128,1152]{2,1,0:T(8,128)(2,1)S(1)}, u32[]{:S(2)}, u32[]{:S(2)}) collective-permute-start(bf16[4,128,1152]{2,1,0:T(8,128)(2,1)S(1)} %pad_maximum_fusion.10.refs_6_.refs_0_), channel_id=1, source_target_pairs={{0,2},{1,3},{2,0},{3,1},{4,6},{5,7},{6,4},{7,5},{8,10},{9,11},{10,... | collective-permute-start | bytes 3538952 | tf_op jit(solution)/shard_map/ppermute | solution.py:67
  72.6 26.3 %collective-permute-start.11 = (bf16[4,128,1152]{2,1,0:T(8,128)(2,1)S(1)}, bf16[4,128,1152]{2,1,0:T(8,128)(2,1)S(1)}, u32[]{:S(2)}, u32[]{:S(2)}) collective-permute-start(bf16[4,128,1152]{2,1,0:T(8,128)(2,1)S(1)} %pad_maximum_fusion.10.refs_6_.refs_0_), channel_id=1, source_target_pairs={{0,16},{16,0},{1,17},{17,1},{2,18},{18,2},{3,19},{19,3},{4,20},{20... | collective-permute-start | bytes 3538952 | tf_op jit(solution)/shard_map/ppermute | solution.py:811
  133.6 26.4 %collective-permute-start.25 = (bf16[224,1408]{1,0:T(8,128)(2,1)}, bf16[224,1408]{1,0:T(8,128)(2,1)S(1)}, u32[]{:S(2)}, u32[]{:S(2)}) collective-permute-start(bf16[224,1408]{1,0:T(8,128)(2,1)} %get-tuple-element.572), channel_id=1, source_target_pairs={{0,16},{16,0},{1,17},{17,1},{2,18},{18,2},{3,19},{19,3},{4,20},{20... | collective-permute-start | bytes 1892360 | tf_op jit(solution)/shard_map/ppermute | solution.py:811
  134.3 25.6 %collective-permute-start.26 = (bf16[128,2048]{1,0:T(8,128)(2,1)S(1)}, bf16[128,2048]{1,0:T(8,128)(2,1)S(1)}, u32[]{:S(2)}, u32[]{:S(2)}) collective-permute-start(bf16[128,2048]{1,0:T(8,128)(2,1)S(1)} %fusion.9.refs_0_.refs_13_), channel_id=1, source_target_pairs={{0,2},{1,3},{2,0},{3,1},{4,6},{5,7},{6,4},{7,5},{8,10},{9,11},{10,... | collective-permute-start | bytes 1572872 | tf_op jit(solution)/shard_map/ppermute | solution.py:67
  134.9 25.0 %collective-permute-start.27 = (bf16[128,2048]{1,0:T(8,128)(2,1)S(1)}, bf16[128,2048]{1,0:T(8,128)(2,1)S(1)}, u32[]{:S(2)}, u32[]{:S(2)}) collective-permute-start(bf16[128,2048]{1,0:T(8,128)(2,1)S(1)} %collective-permute-done.13.refs_1_.refs_14_), channel_id=1, source_target_pairs={{0,4},{1,5},{2,6},{3,7},{4,8},{5,9},{6,10},{7,11},{8,12},{9,13},{1... | collective-permute-start | bytes 1572872 | tf_op jit(solution)/shard_map/ppermute | solution.py:67
  136.0 23.9 %collective-permute-start.28 = (bf16[128,2048]{1,0:T(8,128)(2,1)S(1)}, bf16[128,2048]{1,0:T(8,128)(2,1)S(1)}, u32[]{:S(2)}, u32[]{:S(2)}) collective-permute-start(bf16[128,2048]{1,0:T(8,128)(2,1)S(1)} %fusion.9.refs_0_.refs_13_), channel_id=1, source_target_pairs={{0,12},{1,13},{2,14},{3,15},{4,0},{5,1},{6,2},{7,3},{8,4},{9,5},{1... | collective-permute-start | bytes 1572872 | tf_op jit(solution)/shard_map/ppermute | solution.py:67
  230.2 26.1 %collective-permute-start.42 = (bf16[128,2048]{1,0:T(8,128)(2,1)S(1)}, bf16[128,2048]{1,0:T(8,128)(2,1)S(1)}, u32[]{:S(2)}, u32[]{:S(2)}) collective-permute-start(bf16[128,2048]{1,0:T(8,128)(2,1)S(1)} %add_convert_fusion.14), channel_id=1, source_target_pairs={{0,12},{1,13},{2,14},{3,15},{4,0},{5,1},{6,2},{7,3},{8,4},{9,5},{1... | collective-permute-start | bytes 1572872 | tf_op jit(solution)/shard_map/ppermute | solution.py:67
  309.8 23.7 %collective-permute-start.56 = (bf16[512,2048]{1,0:T(8,128)(2,1)S(1)}, bf16[512,2048]{1,0:T(8,128)(2,1)S(1)}, u32[]{:S(2)}, u32[]{:S(2)}) collective-permute-start(bf16[512,2048]{1,0:T(8,128)(2,1)S(1)} %pad_maximum_fusion.2), channel_id=1, source_target_pairs={{0,1},{1,0},{2,3},{3,2},{4,5},{5,4},{6,7},{7,6},{8,9},{9,8},{10,11... | collective-permute-start | bytes 6291464 | tf_op jit(solution)/shard_map/ppermute | solution.py:67
  348.7 25.6 %collective-permute-start.62 = (bf16[352,1408]{1,0:T(8,128)(2,1)}, bf16[352,1408]{1,0:T(8,128)(2,1)S(1)}, u32[]{:S(2)}, u32[]{:S(2)}) collective-permute-start(bf16[352,1408]{1,0:T(8,128)(2,1)} %slice_bitcast_fusion.5), channel_id=1, source_target_pairs={{0,16},{16,0},{1,17},{17,1},{2,18},{18,2},{3,19},{19,3},{4,20},{20... | collective-permute-start | bytes 2973704 | tf_op jit(solution)/shard_map/ppermute | solution.py:811
  408.6 31.0 %collective-permute-start.63 = (bf16[672,1024]{1,0:T(8,128)(2,1)S(1)}, bf16[672,1024]{1,0:T(8,128)(2,1)S(1)}, u32[]{:S(2)}, u32[]{:S(2)}) collective-permute-start(bf16[672,1024]{1,0:T(8,128)(2,1)S(1)} %slice.455), channel_id=1, source_target_pairs={{0,16},{16,0},{1,17},{17,1},{2,18},{18,2},{3,19},{19,3},{4,20},{20... | collective-permute-start | bytes 4128776 | tf_op jit(solution)/shard_map/ppermute | solution.py:811
  476.7 23.7 %collective-permute-start.70 = (bf16[128,1408]{1,0:T(8,128)(2,1)}, bf16[128,1408]{1,0:T(8,128)(2,1)}, u32[]{:S(2)}, u32[]{:S(2)}) collective-permute-start(bf16[128,1408]{1,0:T(8,128)(2,1)} %slice.529), channel_id=1, source_target_pairs={{0,16},{16,0},{1,17},{17,1},{2,18},{18,2},{3,19},{19,3},{4,20},{20... | collective-permute-start | bytes 1081352 | tf_op jit(solution)/shard_map/ppermute | solution.py:811
  566.0 26.2 %collective-permute-start.84 = (bf16[320,1408]{1,0:T(8,128)(2,1)S(1)}, bf16[320,1408]{1,0:T(8,128)(2,1)S(1)}, u32[]{:S(2)}, u32[]{:S(2)}) collective-permute-start(bf16[320,1408]{1,0:T(8,128)(2,1)S(1)} %get-tuple-element.917), channel_id=1, source_target_pairs={{0,16},{16,0},{1,17},{17,1},{2,18},{18,2},{3,19},{19,3},{4,20},{20... | collective-permute-start | bytes 2703368 | tf_op jit(solution)/shard_map/ppermute | solution.py:811
  592.6 28.4 %collective-permute-start.89 = (bf16[320,1408]{1,0:T(8,128)(2,1)S(1)}, bf16[320,1408]{1,0:T(8,128)(2,1)S(1)}, u32[]{:S(2)}, u32[]{:S(2)}) collective-permute-start(bf16[320,1408]{1,0:T(8,128)(2,1)S(1)} %get-tuple-element.927), channel_id=1, source_target_pairs={{0,16},{16,0},{1,17},{17,1},{2,18},{18,2},{3,19},{19,3},{4,20},{20... | collective-permute-start | bytes 2703368 | tf_op jit(solution)/shard_map/ppermute | solution.py:811
  593.4 27.6 %collective-permute-start.93 = (bf16[4,2,64,528]{3,2,1,0:T(8,128)(2,1)S(1)}, bf16[4,2,64,528]{3,2,1,0:T(8,128)(2,1)S(1)}, u32[]{:S(2)}, u32[]{:S(2)}) collective-permute-start(bf16[4,2,64,528]{3,2,1,0:T(8,128)(2,1)S(1)} %get-tuple-element.931), channel_id=1, source_target_pairs={{0,2},{1,3},{2,0},{3,1},{4,6},{5,7},{6,4},{7,5},{8,10},{9,11},{10,... | collective-permute-start | bytes 1622024 | tf_op jit(solution)/shard_map/ppermute | solution.py:67
  594.9 26.1 %collective-permute-start.91 = (bf16[128,2048]{1,0:T(8,128)(2,1)S(1)}, bf16[128,2048]{1,0:T(8,128)(2,1)S(1)}, u32[]{:S(2)}, u32[]{:S(2)}) collective-permute-start(bf16[128,2048]{1,0:T(8,128)(2,1)S(1)} %get-tuple-element.929), channel_id=1, source_target_pairs={{0,2},{1,3},{2,0},{3,1},{4,6},{5,7},{6,4},{7,5},{8,10},{9,11},{10,... | collective-permute-start | bytes 1572872 | tf_op jit(solution)/shard_map/ppermute | solution.py:67
  596.0 25.0 %collective-permute-start.92 = (bf16[128,2048]{1,0:T(8,128)(2,1)S(1)}, bf16[128,2048]{1,0:T(8,128)(2,1)S(1)}, u32[]{:S(2)}, u32[]{:S(2)}) collective-permute-start(bf16[128,2048]{1,0:T(8,128)(2,1)S(1)} %add_convert_fusion.1), channel_id=1, source_target_pairs={{0,12},{1,13},{2,14},{3,15},{4,0},{5,1},{6,2},{7,3},{8,4},{9,5},{1... | collective-permute-start | bytes 1572872 | tf_op jit(solution)/shard_map/ppermute | solution.py:67
  632.4 37.2 %collective-permute-start.96 = (bf16[512,1408]{1,0:T(8,128)(2,1)S(1)}, bf16[512,1408]{1,0:T(8,128)(2,1)}, u32[]{:S(2)}, u32[]{:S(2)}) collective-permute-start(bf16[512,1408]{1,0:T(8,128)(2,1)S(1)} %slice.534), channel_id=1, source_target_pairs={{0,16},{16,0},{1,17},{17,1},{2,18},{18,2},{3,19},{19,3},{4,20},{20... | collective-permute-start | bytes 4325384 | tf_op jit(solution)/shard_map/ppermute | solution.py:811
  633.7 35.9 %collective-permute-start.97 = (bf16[2,2,64,528]{3,2,1,0:T(8,128)(2,1)}, bf16[2,2,64,528]{3,2,1,0:T(8,128)(2,1)S(1)}, u32[]{:S(2)}, u32[]{:S(2)}) collective-permute-start(bf16[2,2,64,528]{3,2,1,0:T(8,128)(2,1)} %get-tuple-element.942), channel_id=1, source_target_pairs={{0,8},{1,9},{2,10},{3,11},{4,12},{5,13},{6,14},{7,15},{8,0},{9,1},... | collective-permute-start | bytes 811016 | tf_op jit(solution)/shard_map/ppermute | solution.py:67
  633.9 35.7 %collective-permute-start.98 = (bf16[2,2,64,528]{3,2,1,0:T(8,128)(2,1)}, bf16[2,2,64,528]{3,2,1,0:T(8,128)(2,1)}, u32[]{:S(2)}, u32[]{:S(2)}) collective-permute-start(bf16[2,2,64,528]{3,2,1,0:T(8,128)(2,1)} %get-tuple-element.943), channel_id=1, source_target_pairs={{0,4},{1,5},{2,6},{3,7},{4,8},{5,9},{6,10},{7,11},{8,12},{9,13},{1... | collective-permute-start | bytes 811016 | tf_op jit(solution)/shard_map/ppermute | solution.py:67
  634.4 35.1 %collective-permute-start.99 = (bf16[2,2,64,528]{3,2,1,0:T(8,128)(2,1)}, bf16[2,2,64,528]{3,2,1,0:T(8,128)(2,1)}, u32[]{:S(2)}, u32[]{:S(2)}) collective-permute-start(bf16[2,2,64,528]{3,2,1,0:T(8,128)(2,1)} %get-tuple-element.944), channel_id=1, source_target_pairs={{0,12},{1,13},{2,14},{3,15},{4,0},{5,1},{6,2},{7,3},{8,4},{9,5},{1... | collective-permute-start | bytes 811016 | tf_op jit(solution)/shard_map/ppermute | solution.py:67
  637.7 31.9 %collective-permute-start.100 = (bf16[128,2048]{1,0:T(8,128)(2,1)}, bf16[128,2048]{1,0:T(8,128)(2,1)}, u32[]{:S(2)}, u32[]{:S(2)}) collective-permute-start(bf16[128,2048]{1,0:T(8,128)(2,1)} %add_convert_fusion), channel_id=1, source_target_pairs={{0,12},{1,13},{2,14},{3,15},{4,0},{5,1},{6,2},{7,3},{8,4},{9,5},{1... | collective-permute-start | bytes 1572872 | tf_op jit(solution)/shard_map/ppermute | solution.py:67
  725.5 28.3 %collective-permute-start.109 = (bf16[160,1408]{1,0:T(8,128)(2,1)}, bf16[160,1408]{1,0:T(8,128)(2,1)}, u32[]{:S(2)}, u32[]{:S(2)}) collective-permute-start(bf16[160,1408]{1,0:T(8,128)(2,1)} %slice.540), channel_id=1, source_target_pairs={{0,16},{16,0},{1,17},{17,1},{2,18},{18,2},{3,19},{19,3},{4,20},{20... | collective-permute-start | bytes 1351688 | tf_op jit(solution)/shard_map/ppermute | solution.py:811
  (234 other events, 3373.1 us)
Sparse Core Ops, SparseCore 0:
  669.7 53.7 reduce-scatter.1

commit v4 on v3

--- a/solution.py
+++ b/solution.py
@@ -114,7 +114,11 @@
             size -= (stop - start) * line
         return moves, entries
 
-    def slot(self, *moves, begin=(), end=(), work=(), feed=0):
+    def slot(self, *moves, begin=(), end=(), work=(), feed=0, lasting=0, fed_before=()):
+        later, later_entries = self.next_rows(lasting * 1e6)
+        begin = list(begin) + later
+        waited = [entry[2][place] for entry, place in fed_before]
+        end = waited + list(end)
         fed, entries = self.next_rows(feed * 1e6)
         moves = fed + list(moves)
         count, late = len(moves), len(moves) + len(begin)
@@ -130,6 +134,12 @@
         moved, ended = list(self.last[:count]), list(self.last[count : count + len(end)])
         for entry in entries:
             entry[2].append(moved.pop(0))
+        for entry, place in fed_before:
+            entry[2][place] = ended.pop(0)
+        self.lasting = []
+        for entry in later_entries:
+            self.lasting.append((entry, len(entry[2])))
+            entry[2].append(begun.pop(len(begun) - len(later_entries) + len(self.lasting) - 1))
         return moved, begun, ended, jax.tree.unflatten(tree, self.last[count + len(end) :])
 
 
@@ -210,6 +220,25 @@
     count = index.shape[0]
     outs = [shaped(a.shape[:2] + (a.shape[2] if not pad else parts * pad,), a.dtype) for a in arrays]
     return whole_call(functools.partial(reorder_kernel, count, parts), arrays, outs, scalars=index)
+
+
+def unpack_kernel(index_ref, in_ref, wq_ref, wo_ref, we_ref):
+    rows = we_ref.shape[0]
+    for a in range(in_ref.shape[0]):
+        value = wide(in_ref[index_ref[a]])
+        parts = [value[:, :HD], value[:, 2 * HD : 2 * HD + RD], value[:, HD : 2 * HD], value[:, 2 * HD + RD : Q_COLS]]
+        wq_ref[:, a * Q_COLS : (a + 1) * Q_COLS] = jnp.concatenate(parts, axis=1)
+        wo_ref[:, a * O_COLS : (a + 1) * O_COLS] = value[:, Q_COLS : Q_COLS + O_COLS]
+        for g in range(4):
+            we_ref[:, (4 * a + g) * E_COLS : (4 * a + g + 1) * E_COLS] = value[g * rows : (g + 1) * rows, Q_COLS + O_COLS :]
+
+
+def unpack(blocks, index, rows):
+    pairs, shard, _ = blocks.shape
+    outs = [
+        shaped((shard, pairs * Q_COLS), F32), shaped((shard, pairs * O_COLS), F32), shaped((rows, 4 * pairs * E_COLS), F32)
+    ]
+    return whole_call(unpack_kernel, [blocks], outs, scalars=index)
 
 
 def swap_halves(values):
@@ -883,8 +912,8 @@
     else:
         lat = small
     s_kept, s_away = at(s_piece, core, 2), at(s_piece, 1 - core, 2)
-    clock.slot(feed=0.6)
-    moved, _, _, _ = clock.slot((core_swap, away), (core_swap, s_away), (z_up, x0), feed=0.55)
+    clock.slot(feed=0.65)
+    moved, _, _, _ = clock.slot((core_swap, away), (core_swap, s_away), (z_up, x0), feed=0.59)
     x1 = moved[2]
     s_piece = jnp.stack([s_kept, moved[1]], axis=2)
     w_own = jnp.where(
@@ -898,7 +927,7 @@
         (z_up, at(w_own, (z + 1) % 4, 0)),
         (z_down, at(w_own, (z + 3) % 4, 0)),
         (x_swap, s_away),
-        feed=1.1,
+        feed=1.17,
     )
     w_own = jnp.stack([at(w_own, z, 0), moved[1], moved[0], moved[2]])
     s_piece = jnp.stack([s_kept, moved[3]], axis=1)
@@ -927,7 +956,7 @@
         w_far, x3, lat_other_xy, cx01 = moved[:2], *moved[2:]
         lat_far = jnp.concatenate([w_far[0][..., W_COLS:], w_far[1][..., W_COLS:]])
         moved, _, _, _ = clock.slot(
-            (core_swap, lat_far), (core_swap, jnp.concatenate([x2, x3])), (z_up, s_up), feed=0.35
+            (core_swap, lat_far), (core_swap, jnp.concatenate([x2, x3])), (z_up, s_up), feed=0.5
         )
         cx23, s_up = moved[1:]
         weights = [w_own, w_x, w_y] + w_far
@@ -963,7 +992,7 @@
     x_pieces = [x0, x1, x2, x3, cx01, cx23]
     moved, _, _, made = clock.slot(
         (x_swap, g0), (z_up, g1), (z_down, g0),
-        feed=0.95,
+        feed=1.0,
         work=[
             (
                 lambda *a: attention_forward(*a[:3], layout_of, *a[3:], split=two),
@@ -1055,23 +1084,23 @@
         sent = [clock.add(d_down_away)]
 
     _, _, _, made = clock.slot(
-        work=[(expert_back, d_gate, d_up, own, other, target_col, d_s_pre, s_both)], feed=1.35
+        work=[(expert_back, d_gate, d_up, own, other, target_col, d_s_pre, s_both)], feed=1.42
     )
     near, near_x, far, far_x = made[0]
-    moved, _, _, made = clock.slot((core_swap, far_x), work=[(contract, rows_x[1], d_gate)], feed=0.3)
+    moved, _, _, made = clock.slot((core_swap, far_x), work=[(contract, rows_x[1], d_gate)], feed=0.35)
     if two:
         sent.append(clock.add(low(made[0])))
     away = [low(wide(cut(near_x, k)) + wide(cut(moved[0], k))) for k in range(4)]
     moved, _, _, made = clock.slot(
         (x_swap, away[3]), (core_swap, far),
-        feed=0.72,
+        feed=0.75,
         work=[(functools.partial(shared_gradient, part=ff_part), t_pieces, g_pieces, d_s_pre, s_act)],
     )
     d_shared = made[0].reshape(ndp, experts, shard, 3 * ff_part)
     home = [wide(cut(near, k)) + wide(cut(moved[1], k)) for k in range(4)]
     moved, _, _, made = clock.slot(
         (x_swap, away[2]), (z_down, low(home[3] + wide(moved[0]))),
-        feed=0.8,
+        feed=0.9,
         work=[(expert_out, e_act, share, own, other, target_col, s_act, s_down_w)],
     )
     o_near, o_near_x, o_far, o_far_x = made[0]
@@ -1104,33 +1133,35 @@
     d_mid = cotangent + d_mid_in
 
     a0 = low(d_mid)
+    s_kept, s_away = at(d_shared, x, 1), at(d_shared, 1 - x, 1)
     moved, _, _, made = clock.slot(
-        (z_up, a0), (x_swap, o_away[3]), feed=0.7, work=[(contract, rows_x[0], d_up)]
-    )
-    a1, ox = moved
+        (z_up, a0), (x_swap, o_away[3]), lasting=1.65, work=[(contract, rows_x[0], d_up)]
+    )
+    a1, ox3 = moved
     d_up_home = made[0]
-    s_kept, s_away = at(d_shared, x, 1), at(d_shared, 1 - x, 1)
     moved, _, _, _ = clock.slot(
-        (z_up, a1), (x_swap, o_away[2]), (z_down, low(o_home[3] + wide(ox))), (x_swap, o_away[0]), feed=0.9
-    )
-    a2, ox, o_sum, ox0 = moved
-    o_sum = low(o_home[2] + wide(ox) + wide(o_sum))
-    moved, _, _, _ = clock.slot((z_up, a2), (x_swap, o_away[1]), (z_down, o_sum), (x_swap, s_away), feed=0.95)
-    a3, ox, o_sum, s_got = moved
-    o_sum = low(o_home[1] + wide(ox) + wide(o_sum))
-    d_shared = jnp.stack([s_kept, s_got], axis=1)
-    a_near = jnp.concatenate([a0, a1, a2, a3])
-    moved, _, _, _ = clock.slot((core_swap, a_near), feed=0.35)
+        (z_up, a1), (x_swap, o_away[2]), (z_down, low(o_home[3] + wide(ox3))), fed_before=clock.lasting
+    )
+    a2, ox2, o_sum = moved
+    o_sum = low(o_home[2] + wide(ox2) + wide(o_sum))
+    moved, _, _, _ = clock.slot((z_up, a2), (x_swap, o_away[1]), feed=0.67)
+    a3, ox1 = moved
+    moved, _, _, _ = clock.slot(
+        (core_swap, jnp.concatenate([a0, a1, a2, a3])), (x_swap, s_away),
+        (z_down, o_sum), feed=0.6,
+    )
     a_pieces = [a0, a1, a2, a3, moved[0]]
+    d_shared = jnp.stack([s_kept, moved[1]], axis=1)
+    o_sum = low(o_home[1] + wide(ox1) + wide(moved[2]))
     backward = functools.partial(attention_backward, lat_rows=lat_rows)
     moved, _, _, made = clock.slot(
         (z_two, at(d_shared, (z + 2) % 4, 0)), (z_up, at(d_shared, (z + 1) % 4, 0)),
         (z_down, at(d_shared, (z + 3) % 4, 0)), (z_down, o_sum),
-        feed=1.4,
+        feed=1.6,
         work=[(backward, scalars, x_pieces, a_pieces, saved, d_gain_mid.reshape(1, width), table)],
     )
     d_shared = jnp.stack([at(d_shared, z, 0), moved[1], moved[0], moved[2]])
-    o_last = o_home[0] + wide(ox0) + wide(moved[3])
+    o_last = o_home[0] + wide(moved[3])
     d_norm, d_head, d_wl = made[0]
     same_x = [[i for i in range(experts) if i // 2 % 2 == side] for side in range(2)]
     d_normed = lax.psum_scatter(d_norm, "expert", scatter_dimension=0, axis_index_groups=same_x, tiled=True)
@@ -1152,13 +1183,13 @@
         first = (wide(d_head[:4]) + wide(moved[0])).reshape(ndp, 2, 2 * shard, W_COLS)
         second = (wide(d_head[8:12]) + wide(moved[1])).reshape(2, 2, 2 * shard, W_COLS)
         d_wl = (wide(d_wl[0]) + wide(moved[2])).reshape(ndp, 4, 2, shard, -1)
-        d_shared = jnp.stack([s_kept, moved[3]], axis=2)
+        d_shared = jnp.stack([s_kept, moved[3]], axis=2).reshape(experts, shard, 3 * ff_part)
         moved, _, _, made = clock.slot(
             (dp_swap, low(at(first, 1 - dp, 0))), (x_swap, low(at(second, 1 - x, 1))),
-            (x_swap, low(at(d_wl, 1 - x, 2))), feed=0.65,
-            work=[(add_received, d_gate_home, *sent[1][2])],
+            (x_swap, low(at(d_wl, 1 - x, 2))), feed=0.45,
+            work=[(add_received, d_gate_home, *sent[1][2]), (lambda a: reorder([a], block_index)[0], d_shared)],
         )
-        d_gate_all = made[0]
+        d_gate_all, d_shared = made
         first = at(first, dp, 0) + wide(moved[0])
         second = at(second, x, 1) + wide(moved[1])
         d_wl = at(d_wl, x, 2) + wide(moved[2])
@@ -1168,9 +1199,8 @@
         d_head = dp_scatter(low(d_head))[0]
         d_wl = wide(at(d_wl, core, 3)) + wide(core_swap(at(d_wl, 1 - core, 3)))
         d_wl = at(d_wl, x, 2) + wide(x_swap(low(at(d_wl, 1 - x, 2))))
-        d_shared = jnp.stack([s_kept, core_swap(s_away)], axis=2)
-        o_last = o_last + wide(z_down(o_sum))
-    d_shared = d_shared.reshape(experts, shard, 3 * ff_part)
+        d_shared = jnp.stack([s_kept, core_swap(s_away)], axis=2).reshape(experts, shard, 3 * ff_part)
+        d_shared = reorder([d_shared], block_index)[0]
     moved, _, _, _ = clock.slot(
         (z_two, at(d_head, (z + 2) % 4, 0)), (z_down, at(d_head, (z + 3) % 4, 0)),
         (z_up, at(d_head, (z + 1) % 4, 0)),
@@ -1178,13 +1208,13 @@
     )
     d_head = jnp.stack([at(d_head, z, 0), moved[1], moved[0], moved[2]]).reshape(4, 2, shard, W_COLS)
     d_wl = at(d_wl, dp, 0) + wide(moved[3]) if two else wide(dp_scatter(low(d_wl))[0])
-    out = low(mid + turn(o_last))
     moved, _, ended, made = clock.slot(
         (core_swap, at(d_head, 1 - core, 1)), (z_two, low(at(d_wl, (z + 2) % 4, 0))),
-        (z_down, low(at(d_wl, (z + 3) % 4, 0))), (z_up, low(at(d_wl, (z + 1) % 4, 0))),
+        (z_down, low(at(d_wl, (z + 3) % 4, 0))), (z_up, low(at(d_wl, (z + 1) % 4, 0))), (x_swap, o_away[0]),
         end=[d_normed], work=[(add_received, d_up_home, *sent[2][2])] if two else [],
     )
     d_up_all = made[0] if two else None
+    out = low(mid + turn(o_last + wide(moved[4])))
     d_head = jnp.stack([at(d_head, core, 1), moved[0]], axis=1).reshape(pairs, shard, W_COLS)
     d_wl = at(d_wl, z, 0) + wide(moved[1]) + wide(moved[2]) + wide(moved[3])
     d_normed = wide(ended[0])
@@ -1200,25 +1230,29 @@
         d_expert.append(wide(dp_scatter(low(jnp.concatenate([contract(e_act, value) for value in rows_g], axis=1)), 1)))
     d_in, _ = rms_back(d_normed, xf, rms_scale(xf), gain_in)
     d_tokens = d_mid + d_in
-    d_shared = wide(reorder([d_shared], block_index)[0])
+    d_shared = wide(d_shared)
     grad_sg, grad_su = (
         d_shared[:, :, i * ff_part : (i + 1) * ff_part].transpose(1, 0, 2).reshape(shard, ff_s) for i in range(2)
     )
     grad_sd = d_shared[:, :, 2 * ff_part :].transpose(0, 2, 1).reshape(ff_s, shard)
     pair_number = jnp.arange(pairs, dtype=jnp.int32)
     pair_index = ((pair_number // 2 + 4 - z) % 4) * 2 + (pair_number % 2 ^ core)
-    d_head = wide(reorder([d_head], pair_index)[0])
-    grad_wq = jnp.concatenate(
-        [
-            d_head[..., : 2 * HD].reshape(pairs, shard, 2, HD),
-            d_head[..., 2 * HD : Q_COLS].reshape(pairs, shard, 2, RD),
-        ],
-        axis=3,
-    )
-    grad_wq = grad_wq.transpose(1, 0, 2, 3).reshape(shard, HEADS * (HD + RD))
-    grad_wo = d_head[..., Q_COLS : Q_COLS + O_COLS].transpose(0, 2, 1).reshape(HEADS * VD, shard)
-    grad_we = d_head[..., Q_COLS + O_COLS :].reshape(pairs, groups, lat_rows, E_COLS).transpose(2, 0, 1, 3)
-    grad_we = grad_we.reshape(lat_rows, HEADS * (HD + VD))
+    if two:
+        grad_wq, grad_wo, grad_we = unpack(d_head, pair_index, lat_rows)
+        grad_wo = grad_wo.T
+    else:
+        d_head = wide(reorder([d_head], pair_index)[0])
+        grad_wq = jnp.concatenate(
+            [
+                d_head[..., : 2 * HD].reshape(pairs, shard, 2, HD),
+                d_head[..., 2 * HD : Q_COLS].reshape(pairs, shard, 2, RD),
+            ],
+            axis=3,
+        )
+        grad_wq = grad_wq.transpose(1, 0, 2, 3).reshape(shard, HEADS * (HD + RD))
+        grad_wo = d_head[..., Q_COLS : Q_COLS + O_COLS].transpose(0, 2, 1).reshape(HEADS * VD, shard)
+        grad_we = d_head[..., Q_COLS + O_COLS :].reshape(pairs, groups, lat_rows, E_COLS).transpose(2, 0, 1, 3)
+        grad_we = grad_we.reshape(lat_rows, HEADS * (HD + VD))
     return (
         out,
         d_tokens,

time: 802 us -> 794 us (0.990)
  other arithmetic: 76.9 us -> 89.9 us
  local copies, waits for them, and re-layouts: 84.2 us -> 76.1 us
    ppermute x36 -> x33, waiting for transfers between devices: 71.3 us -> 39.8 us  [dp_swap(): return lax.ppermute(value, 'dp', [(0, 1), (1, 0)])]
    ppermute x82, waiting for transfers between devices: 184 us -> 210 us  [move(): return lax.ppermute(value, 'expert', [(i, to(i)) for i in range(16)])]
    concatenate x1 -> x3, other arithmetic: 0.24 us -> 9.97 us  [the longest x2 9.82 us: local(): join = lambda *pieces: jnp.concatenate(pieces, axis=0)]
    unnamed x288 -> x277, local copies, waits for them, and re-layouts: 27 us -> 18.7 us
    ppermute x36 -> x33, starting transfers between devices: 40.4 us -> 38 us  [dp_swap(): return lax.ppermute(value, 'dp', [(0, 1), (1, 0)])]
    slice x21 -> x19, local copies, waits for them, and re-layouts: 27.5 us -> 28.8 us  [next_rows(): moves.append((self.go, array[start:stop]))]
  transfers between devices with their start and end apart: 119 -> 116, of which waited for: 50 -> 51; matrix products, arithmetic and copies ran while one was open for 16% -> 17% of each run, Pallas kernels for 19% -> 19%
where the time goes in v4:
time: 794 us; the launch traced here: 789 us
  waiting for transfers between devices  250 us (31%)
  Pallas kernels  184 us (23%)
  starting transfers between devices  146 us (18%)
  other arithmetic  89.9 us (11%)
  local copies, waits for them, and re-layouts  76.1 us (10%)
  matrix products  27 us (3%)
  between operations  16.3 us (2%)
    ppermute x82, waiting for transfers between devices, move(): return lax.ppermute(value, 'expert', [(i, to(i)) for i in range(16)])  210 us
    ppermute x82, starting transfers between devices, move(): return lax.ppermute(value, 'expert', [(i, to(i)) for i in range(16)])  108 us
    pallas_call x10, Pallas kernels, whole_call(): pl.pallas_call(kernel, in_specs=specs, out_specs=[vmem] * len(outs), out_...  106 us
    pallas_call x3, Pallas kernels, tiled_call(): pl.pallas_call(kernel, grid=(steps,), in_specs=specs, out_specs=out_specs...  77.8 us
    ppermute x33, waiting for transfers between devices, dp_swap(): return lax.ppermute(value, 'dp', [(0, 1), (1, 0)])  39.8 us
    ppermute x33, starting transfers between devices, dp_swap(): return lax.ppermute(value, 'dp', [(0, 1), (1, 0)])  38 us
    slice x19, local copies, waits for them, and re-layouts, next_rows(): moves.append((self.go, array[start:stop]))  28.8 us
    dot_general x5, matrix products, contract(): lax.dot_general(left, right, (((0,), (0,)), ((), ())), preferred_element_...  27 us
  transfers between devices with their start and end apart: 116, of which 51 were waited for; matrix products, arithmetic and copies ran while one was open for 17% of the time, Pallas kernels for 19%

profile of v4, /device:TPU:0, one launch (start us, length us, event | category | flops | bytes accessed | tf_op | source)
XLA Modules:
  0.0 789.4 jit_solution(16963193075921470717)
XLA Ops:
  34.2 7.9 %collective-permute-done.4.refs_1_ = bf16[128,2048]{1,0:T(8,128)(2,1)S(1)} collective-permute-done((bf16[128,2048]{1,0:T(8,128)(2,1)S(1)}, bf16[128,2048]{1,0:T(8,128)(2,1)S(1)}, u32[]{:S(2)}, u32[]{:S(2)}) %collective-permute-start.4) | collective-permute-done | bytes 524320 | tf_op jit(solution)/shard_map/ppermute | solution.py:67
  56.5 14.5 %collective-permute-done.6 = bf16[128,1152]{1,0:T(8,128)(2,1)S(1)} collective-permute-done((bf16[128,1152]{1,0:T(8,128)(2,1)}, bf16[128,1152]{1,0:T(8,128)(2,1)S(1)}, u32[]{:S(2)}, u32[]{:S(2)}) %collective-permute-start.6) | collective-permute-done | bytes 294944 | tf_op jit(solution)/shard_map/ppermute | solution.py:67
  81.6 11.2 %collective-permute-done.12.refs_2_ = bf16[128,2048]{1,0:T(8,128)(2,1)S(1)} collective-permute-done((bf16[128,2048]{1,0:T(8,128)(2,1)S(1)}, bf16[128,2048]{1,0:T(8,128)(2,1)S(1)}, u32[]{:S(2)}, u32[]{:S(2)}) %collective-permute-start.12) | collective-permute-done | bytes 524320 | tf_op jit(solution)/shard_map/ppermute | solution.py:67
  111.6 7.4 collective-permute-done.17.refs_3_
  146.4 19.2 %shard_map.298 = (bf16[512,2048]{1,0:T(8,128)(2,1)}, bf16[512,2048]{1,0:T(8,128)(2,1)}, bf16[1024,384]{1,0:T(8,128)(2,1)}, bf16[1024,128]{1,0:T(8,128)(2,1)}, f3...) custom-call(s32[68]{0:T(128)} %concatenate.124.place_ref, ...), custom_call_target="tpu_custom_call" | custom-call | flops 5368709120 | bytes 25294848 | tf_op jit(solution)/shard_map/pallas_call | solution.py:166
  168.9 15.1 %collective-permute-done.30 = bf16[2,2,64,528]{3,2,1,0:T(8,128)(2,1)S(1)} collective-permute-done((bf16[2,2,64,528]{3,2,1,0:T(8,128)(2,1)}, bf16[2,2,64,528]{3,2,1,0:T(8,128)(2,1)S(1)}, u32[]{:S(2)}, u32[]{:S(2)}) %collective-permute-start.30) | collective-permute-done | bytes 270368 | tf_op jit(solution)/shard_map/ppermute | solution.py:67
  190.6 8.0 %collective-permute-start.33 = (bf16[128,2048]{1,0:T(8,128)(2,1)}, bf16[128,2048]{1,0:T(8,128)(2,1)}, u32[]{:S(2)}, u32[]{:S(2)}) collective-permute-start(bf16[128,2048]{1,0:T(8,128)(2,1)} %add_convert_fusion.16), channel_id=1, source_target_pairs={{0,12},{1,13},{2,14},{3,15},{4,0},{5,1},{6,2},{7,3},{8,4},{9,5},{1... | collective-permute-start | bytes 1572872 | tf_op jit(solution)/shard_map/ppermute | solution.py:67
  214.1 13.6 %collective-permute-start.36 = (bf16[128,2048]{1,0:T(8,128)(2,1)S(1)}, bf16[128,2048]{1,0:T(8,128)(2,1)S(1)}, u32[]{:S(2)}, u32[]{:S(2)}) collective-permute-start(bf16[128,2048]{1,0:T(8,128)(2,1)S(1)} %add_convert_fusion.15), channel_id=1, source_target_pairs={{0,12},{1,13},{2,14},{3,15},{4,0},{5,1},{6,2},{7,3},{8,4},{9,5},{1... | collective-permute-start | bytes 1572872 | tf_op jit(solution)/shard_map/ppermute | solution.py:67
  231.7 7.7 collective-permute-done.36
  246.0 9.3 %collective-permute-done.40 = bf16[128,2048]{1,0:T(8,128)(2,1)S(1)} collective-permute-done((bf16[128,2048]{1,0:T(8,128)(2,1)S(1)}, bf16[128,2048]{1,0:T(8,128)(2,1)S(1)}, u32[]{:S(2)}, u32[]{:S(2)}) %collective-permute-start.40) | collective-permute-done | bytes 524320 | tf_op jit(solution)/shard_map/ppermute | solution.py:67
  277.0 13.8 %collective-permute-done.46.refs_2_ = bf16[128,2048]{1,0:T(8,128)(2,1)} collective-permute-done((bf16[128,2048]{1,0:T(8,128)(2,1)S(1)}, bf16[128,2048]{1,0:T(8,128)(2,1)}, u32[]{:S(2)}, u32[]{:S(2)}) %collective-permute-start.46) | collective-permute-done | bytes 524320 | tf_op jit(solution)/shard_map/ppermute | solution.py:67
  353.0 15.1 %shard_map.303 = (bf16[2048,256]{1,0:T(8,128)(2,1)}, bf16[2048,512]{1,0:T(8,128)(2,1)}) custom-call(bf16[128,2048]{1,0:T(8,128)(2,1)} %copy-done.12, bf16[128,2048]{1,0:T(8,128)(2,1)} %copy-done.48, bf16[128,2048]{1,0:T(8,128)(2,1)} %collective-permute-done.46.refs_2_, bf16[128,2048]{1,0:T(8,128)(2,1)} %collective-permute-done.49.refs_3_, ...), custom_call_target="tpu_custom_call" | custom-call | flops 6442450944 | bytes 23068672 | tf_op jit(solution)/shard_map/pallas_call | solution.py:166
  369.0 30.7 %shard_map.304 = (bf16[1024,1408]{1,0:T(8,128)(2,1)}, bf16[1024,1408]{1,0:T(8,128)(2,1)}, bf16[1024,1408]{1,0:T(8,128)(2,1)}, bf16[1408,1024]{1,0:T(8,128)(2,1)}) custom-call(bf16[1024,1024]{1,0:T(8,128)(2,1)} %get-tuple-element.900.x0_ref, bf16[1024,1024]{1,0:T(8,128)(2,1)} %get-tuple-element.877.x1_ref, bf16[1024,1024]{1,0:T(8,128)(2,1)} %get-tuple-element.880.r0_ref, ...), custom_call_target="tpu_custom_call" | custom-call | flops 20669530112 | bytes 37224448 | tf_op jit(solution)/shard_map/pallas_call | solution.py:668
  403.9 28.8 %shard_map.305 = (bf16[512,2048]{1,0:T(8,128)(2,1)}, bf16[512,2048]{1,0:T(8,128)(2,1)}, bf16[512,2048]{1,0:T(8,128)(2,1)}, bf16[512,2048]{1,0:T(8,128)(2,1)}) custom-call(bf16[1024,1408]{1,0:T(8,128)(2,1)} %get-tuple-element.892.dg_ref, bf16[1024,1408]{1,0:T(8,128)(2,1)} %get-tuple-element.901.du_ref, bf16[1024,1408]{1,0:T(8,128)(2,1)} %bitcast.216, ...), custom_call_target="tpu_custom_call" | custom-call | flops 17179869184 | bytes 29892608 | tf_op jit(solution)/shard_map/pallas_call | solution.py:668
  454.4 15.1 %shard_map.306 = bf16[2048,528]{1,0:T(8,128)(2,1)} custom-call(bf16[128,2048]{1,0:T(8,128)(2,1)} %copy-done.12, bf16[128,2048]{1,0:T(8,128)(2,1)} %copy-done.48, bf16[128,2048]{1,0:T(8,128)(2,1)} %collective-permute-done.46.refs_2_, bf16[128,2048]{1,0:T(8,128)(2,1)} %collective-permute-done.49.refs_3_, bf16[128,2048]{1,0:T(8,128)(2,1)} %collective-permute-done.44.refs_4_, ...), custom_call_target="tpu_custom_call" | custom-call | flops 6442450944 | bytes 22085632 | tf_op jit(solution)/shard_map/pallas_call | solution.py:166
  478.8 18.3 %shard_map.307 = (bf16[512,2048]{1,0:T(8,128)(2,1)}, bf16[512,2048]{1,0:T(8,128)(2,1)}, bf16[512,2048]{1,0:T(8,128)(2,1)}, bf16[512,2048]{1,0:T(8,128)(2,1)}) custom-call(bf16[1024,1408]{1,0:T(8,128)(2,1)} %get-tuple-element.879.act_ref, f32[1024,1]{1,0:T(8,128)} %get-tuple-element.855.share_ref, bf16[1408,1024]{1,0:T(8,128)(2,1)} %bitcast.214, ...), custom_call_target="tpu_custom_call" | custom-call | flops 9126805504 | bytes 19148800 | tf_op jit(solution)/shard_map/pallas_call | solution.py:668
  562.2 11.3 %collective-permute-done.81.refs_8_ = bf16[128,2048]{1,0:T(8,128)(2,1)S(1)} collective-permute-done((bf16[128,2048]{1,0:T(8,128)(2,1)S(1)}, bf16[128,2048]{1,0:T(8,128)(2,1)S(1)}, u32[]{:S(2)}, u32[]{:S(2)}) %collective-permute-start.81) | collective-permute-done | bytes 524320 | tf_op jit(solution)/shard_map/ppermute | solution.py:67
  573.5 7.0 collective-permute-done.83
  584.9 12.3 %collective-permute-done.86.refs_9_ = bf16[128,2048]{1,0:T(8,128)(2,1)S(1)} collective-permute-done((bf16[128,2048]{1,0:T(8,128)(2,1)S(1)}, bf16[128,2048]{1,0:T(8,128)(2,1)S(1)}, u32[]{:S(2)}, u32[]{:S(2)}) %collective-permute-start.86) | collective-permute-done | bytes 524320 | tf_op jit(solution)/shard_map/ppermute | solution.py:67
  601.1 12.7 %collective-permute-done.91 = bf16[128,2048]{1,0:T(8,128)(2,1)S(1)} collective-permute-done((bf16[128,2048]{1,0:T(8,128)(2,1)S(1)}, bf16[128,2048]{1,0:T(8,128)(2,1)S(1)}, u32[]{:S(2)}, u32[]{:S(2)}) %collective-permute-start.91) | collective-permute-done | bytes 524320 | tf_op jit(solution)/shard_map/ppermute | solution.py:67
  624.4 30.6 %shard_map.308 = (bf16[1024,2048]{1,0:T(8,128)(2,1)}, bf16[16,128,768]{2,1,0:T(8,128)(2,1)}, bf16[2,16,64,640]{3,2,1,0:T(8,128)(2,1)}, bf16[16,128]{1,0:T(8,128)(2,1)}) custom-call(s32[68]{0:T(128)} %concatenate.124.place_ref, bf16[128,2048]{1,0:T(8,128)(2,1)} %refs_0_.1, bf16[128,2048]{1,0:T(8,128)(2,1)} %copy-done.91, bf16[128,2048]{1,0:T(8,128)(2,1)} %copy-done.92, ...), custom_call_target="tpu_custom_call" | custom-call | flops 10737418240 | bytes 28964864 | tf_op jit(solution)/shard_map/pallas_call | solution.py:166
  667.8 7.1 convert_add_fusion.2
  674.8 10.6 %collective-permute-done.97 = bf16[4,128,768]{2,1,0:T(8,128)(2,1)S(1)} collective-permute-done((bf16[4,128,768]{2,1,0:T(8,128)(2,1)S(1)}, bf16[4,128,768]{2,1,0:T(8,128)(2,1)S(1)}, u32[]{:S(2)}, u32[]{:S(2)}) %collective-permute-start.97) | collective-permute-done | bytes 786464 | tf_op jit(solution)/shard_map/ppermute | solution.py:67
  755.8 7.1 convert_add_fusion
  (661 shorter events, 438.6 us)
Async XLA Ops:
  7.2 761.8 %reduce-scatter.2.cloned.1.call-start = ((), (), s32[]{:S(2)}) async-start(), calls=%async_computation.1 | async-start | bytes 4718592 | tf_op jit(solution)/shard_map/reduce_scatter | solution.py:1167
  46.8 26.2 %collective-permute-start.5 = (bf16[576,1024]{1,0:T(8,128)(2,1)}, bf16[576,1024]{1,0:T(8,128)(2,1)}, u32[]{:S(2)}, u32[]{:S(2)}) collective-permute-start(bf16[576,1024]{1,0:T(8,128)(2,1)} %slice_bitcast_fusion.1), channel_id=1, source_target_pairs={{0,16},{16,0},{1,17},{17,1},{2,18},{18,2},{3,19},{19,3},{4,20},{20... | collective-permute-start | bytes 3538952 | tf_op jit(solution)/shard_map/ppermute | solution.py:840
  48.3 22.7 %collective-permute-start.9 = (bf16[4,2,64,528]{3,2,1,0:T(8,128)(2,1)}, bf16[4,2,64,528]{3,2,1,0:T(8,128)(2,1)}, u32[]{:S(2)}, u32[]{:S(2)}) collective-permute-start(bf16[4,2,64,528]{3,2,1,0:T(8,128)(2,1)} %get-tuple-element.533), channel_id=1, source_target_pairs={{0,2},{1,3},{2,0},{3,1},{4,6},{5,7},{6,4},{7,5},{8,10},{9,11},{10,... | collective-permute-start | bytes 1622024 | tf_op jit(solution)/shard_map/ppermute | solution.py:67
  73.3 26.4 %collective-permute-start.10 = (bf16[4,128,1152]{2,1,0:T(8,128)(2,1)S(1)}, bf16[4,128,1152]{2,1,0:T(8,128)(2,1)S(1)}, u32[]{:S(2)}, u32[]{:S(2)}) collective-permute-start(bf16[4,128,1152]{2,1,0:T(8,128)(2,1)S(1)} %pad_maximum_fusion.12.refs_6_.refs_0_), channel_id=1, source_target_pairs={{0,2},{1,3},{2,0},{3,1},{4,6},{5,7},{6,4},{7,5},{8,10},{9,11},{10,... | collective-permute-start | bytes 3538952 | tf_op jit(solution)/shard_map/ppermute | solution.py:67
  74.6 25.1 %collective-permute-start.11 = (bf16[4,128,1152]{2,1,0:T(8,128)(2,1)S(1)}, bf16[4,128,1152]{2,1,0:T(8,128)(2,1)S(1)}, u32[]{:S(2)}, u32[]{:S(2)}) collective-permute-start(bf16[4,128,1152]{2,1,0:T(8,128)(2,1)S(1)} %pad_maximum_fusion.12.refs_6_.refs_0_), channel_id=1, source_target_pairs={{0,16},{16,0},{1,17},{17,1},{2,18},{18,2},{3,19},{19,3},{4,20},{20... | collective-permute-start | bytes 3538952 | tf_op jit(solution)/shard_map/ppermute | solution.py:840
  137.4 28.3 %collective-permute-start.25 = (bf16[128,2048]{1,0:T(8,128)(2,1)S(1)}, bf16[128,2048]{1,0:T(8,128)(2,1)S(1)}, u32[]{:S(2)}, u32[]{:S(2)}) collective-permute-start(bf16[128,2048]{1,0:T(8,128)(2,1)S(1)} %fusion.9.refs_0_.refs_13_), channel_id=1, source_target_pairs={{0,2},{1,3},{2,0},{3,1},{4,6},{5,7},{6,4},{7,5},{8,10},{9,11},{10,... | collective-permute-start | bytes 1572872 | tf_op jit(solution)/shard_map/ppermute | solution.py:67
  138.2 27.5 %collective-permute-start.26 = (bf16[128,2048]{1,0:T(8,128)(2,1)S(1)}, bf16[128,2048]{1,0:T(8,128)(2,1)S(1)}, u32[]{:S(2)}, u32[]{:S(2)}) collective-permute-start(bf16[128,2048]{1,0:T(8,128)(2,1)S(1)} %collective-permute-done.13.refs_1_.refs_14_), channel_id=1, source_target_pairs={{0,4},{1,5},{2,6},{3,7},{4,8},{5,9},{6,10},{7,11},{8,12},{9,13},{1... | collective-permute-start | bytes 1572872 | tf_op jit(solution)/shard_map/ppermute | solution.py:67
  139.5 26.2 %collective-permute-start.27 = (bf16[128,2048]{1,0:T(8,128)(2,1)S(1)}, bf16[128,2048]{1,0:T(8,128)(2,1)S(1)}, u32[]{:S(2)}, u32[]{:S(2)}) collective-permute-start(bf16[128,2048]{1,0:T(8,128)(2,1)S(1)} %fusion.9.refs_0_.refs_13_), channel_id=1, source_target_pairs={{0,12},{1,13},{2,14},{3,15},{4,0},{5,1},{6,2},{7,3},{8,4},{9,5},{1... | collective-permute-start | bytes 1572872 | tf_op jit(solution)/shard_map/ppermute | solution.py:67
  142.2 23.5 %collective-permute-start.24 = (bf16[352,1408]{1,0:T(8,128)(2,1)}, bf16[352,1408]{1,0:T(8,128)(2,1)}, u32[]{:S(2)}, u32[]{:S(2)}) collective-permute-start(bf16[352,1408]{1,0:T(8,128)(2,1)} %slice_bitcast_fusion.5), channel_id=1, source_target_pairs={{0,16},{16,0},{1,17},{17,1},{2,18},{18,2},{3,19},{19,3},{4,20},{20... | collective-permute-start | bytes 2973704 | tf_op jit(solution)/shard_map/ppermute | solution.py:840
  212.9 28.5 %collective-permute-start.38 = (bf16[512,2048]{1,0:T(8,128)(2,1)S(1)}, bf16[512,2048]{1,0:T(8,128)(2,1)S(1)}, u32[]{:S(2)}, u32[]{:S(2)}) collective-permute-start(bf16[512,2048]{1,0:T(8,128)(2,1)S(1)} %copy-done.33), channel_id=1, source_target_pairs={{0,1},{1,0},{2,3},{3,2},{4,5},{5,4},{6,7},{7,6},{8,9},{9,8},{10,11... | collective-permute-start | bytes 6291464 | tf_op jit(solution)/shard_map/ppermute | solution.py:67
  213.0 28.4 %collective-permute-start.35 = (bf16[224,1408]{1,0:T(8,128)(2,1)S(1)}, bf16[224,1408]{1,0:T(8,128)(2,1)S(1)}, u32[]{:S(2)}, u32[]{:S(2)}) collective-permute-start(bf16[224,1408]{1,0:T(8,128)(2,1)S(1)} %copy-done.78), channel_id=1, source_target_pairs={{0,16},{16,0},{1,17},{17,1},{2,18},{18,2},{3,19},{19,3},{4,20},{20... | collective-permute-start | bytes 1892360 | tf_op jit(solution)/shard_map/ppermute | solution.py:840
  214.1 25.3 %collective-permute-start.36 = (bf16[128,2048]{1,0:T(8,128)(2,1)S(1)}, bf16[128,2048]{1,0:T(8,128)(2,1)S(1)}, u32[]{:S(2)}, u32[]{:S(2)}) collective-permute-start(bf16[128,2048]{1,0:T(8,128)(2,1)S(1)} %add_convert_fusion.15), channel_id=1, source_target_pairs={{0,12},{1,13},{2,14},{3,15},{4,0},{5,1},{6,2},{7,3},{8,4},{9,5},{1... | collective-permute-start | bytes 1572872 | tf_op jit(solution)/shard_map/ppermute | solution.py:67
  345.4 22.7 %collective-permute-start.60 = (bf16[224,1408]{1,0:T(8,128)(2,1)S(1)}, bf16[224,1408]{1,0:T(8,128)(2,1)S(1)}, u32[]{:S(2)}, u32[]{:S(2)}) collective-permute-start(bf16[224,1408]{1,0:T(8,128)(2,1)S(1)} %copy-done.71), channel_id=1, source_target_pairs={{0,16},{16,0},{1,17},{17,1},{2,18},{18,2},{3,19},{19,3},{4,20},{20... | collective-permute-start | bytes 1892360 | tf_op jit(solution)/shard_map/ppermute | solution.py:840
  402.9 32.4 %collective-permute-start.61 = (bf16[704,1024]{1,0:T(8,128)(2,1)S(1)}, bf16[704,1024]{1,0:T(8,128)(2,1)S(1)}, u32[]{:S(2)}, u32[]{:S(2)}) collective-permute-start(bf16[704,1024]{1,0:T(8,128)(2,1)S(1)} %slice.424), channel_id=1, source_target_pairs={{0,16},{16,0},{1,17},{17,1},{2,18},{18,2},{3,19},{19,3},{4,20},{20... | collective-permute-start | bytes 4325384 | tf_op jit(solution)/shard_map/ppermute | solution.py:840
  472.7 24.6 %collective-permute-start.67 = (bf16[192,1024]{1,0:T(8,128)(2,1)}, bf16[192,1024]{1,0:T(8,128)(2,1)S(1)}, u32[]{:S(2)}, u32[]{:S(2)}) collective-permute-start(bf16[192,1024]{1,0:T(8,128)(2,1)} %slice.422), channel_id=1, source_target_pairs={{0,16},{16,0},{1,17},{17,1},{2,18},{18,2},{3,19},{19,3},{4,20},{20... | collective-permute-start | bytes 1179656 | tf_op jit(solution)/shard_map/ppermute | solution.py:840
  473.8 23.5 %collective-permute-start.69 = (bf16[128,2048]{1,0:T(8,128)(2,1)}, bf16[128,2048]{1,0:T(8,128)(2,1)}, u32[]{:S(2)}, u32[]{:S(2)}) collective-permute-start(bf16[128,2048]{1,0:T(8,128)(2,1)} %get-tuple-element.852), channel_id=1, source_target_pairs={{0,2},{1,3},{2,0},{3,1},{4,6},{5,7},{6,4},{7,5},{8,10},{9,11},{10,... | collective-permute-start | bytes 1572872 | tf_op jit(solution)/shard_map/ppermute | solution.py:67
  474.5 22.8 %collective-permute-start.70 = (bf16[128,2048]{1,0:T(8,128)(2,1)}, bf16[128,2048]{1,0:T(8,128)(2,1)}, u32[]{:S(2)}, u32[]{:S(2)}) collective-permute-start(bf16[128,2048]{1,0:T(8,128)(2,1)} %add_convert_fusion.11), channel_id=1, source_target_pairs={{0,12},{1,13},{2,14},{3,15},{4,0},{5,1},{6,2},{7,3},{8,4},{9,5},{1... | collective-permute-start | bytes 1572872 | tf_op jit(solution)/shard_map/ppermute | solution.py:67
  545.7 35.0 %collective-permute-start.84 = (bf16[576,1408]{1,0:T(8,128)(2,1)S(1)}, bf16[576,1408]{1,0:T(8,128)(2,1)S(1)}, u32[]{:S(2)}, u32[]{:S(2)}) collective-permute-start(bf16[576,1408]{1,0:T(8,128)(2,1)S(1)} %slice.498), channel_id=1, source_target_pairs={{0,16},{16,0},{1,17},{17,1},{2,18},{18,2},{3,19},{19,3},{4,20},{20... | collective-permute-start | bytes 4866056 | tf_op jit(solution)/shard_map/ppermute | solution.py:840
  618.5 36.8 %collective-permute-start.92 = (bf16[576,1408]{1,0:T(8,128)(2,1)S(1)}, bf16[576,1408]{1,0:T(8,128)(2,1)}, u32[]{:S(2)}, u32[]{:S(2)}) collective-permute-start(bf16[576,1408]{1,0:T(8,128)(2,1)S(1)} %slice.494), channel_id=1, source_target_pairs={{0,16},{16,0},{1,17},{17,1},{2,18},{18,2},{3,19},{19,3},{4,20},{20... | collective-permute-start | bytes 4866056 | tf_op jit(solution)/shard_map/ppermute | solution.py:840
  619.0 36.0 %collective-permute-start.93 = (bf16[2,2,64,528]{3,2,1,0:T(8,128)(2,1)}, bf16[2,2,64,528]{3,2,1,0:T(8,128)(2,1)}, u32[]{:S(2)}, u32[]{:S(2)}) collective-permute-start(bf16[2,2,64,528]{3,2,1,0:T(8,128)(2,1)} %get-tuple-element.928), channel_id=1, source_target_pairs={{0,8},{1,9},{2,10},{3,11},{4,12},{5,13},{6,14},{7,15},{8,0},{9,1},... | collective-permute-start | bytes 811016 | tf_op jit(solution)/shard_map/ppermute | solution.py:67
  619.0 36.0 %collective-permute-start.94 = (bf16[2,2,64,528]{3,2,1,0:T(8,128)(2,1)}, bf16[2,2,64,528]{3,2,1,0:T(8,128)(2,1)}, u32[]{:S(2)}, u32[]{:S(2)}) collective-permute-start(bf16[2,2,64,528]{3,2,1,0:T(8,128)(2,1)} %get-tuple-element.929), channel_id=1, source_target_pairs={{0,4},{1,5},{2,6},{3,7},{4,8},{5,9},{6,10},{7,11},{8,12},{9,13},{1... | collective-permute-start | bytes 811016 | tf_op jit(solution)/shard_map/ppermute | solution.py:67
  620.5 34.5 %collective-permute-start.95 = (bf16[2,2,64,528]{3,2,1,0:T(8,128)(2,1)}, bf16[2,2,64,528]{3,2,1,0:T(8,128)(2,1)}, u32[]{:S(2)}, u32[]{:S(2)}) collective-permute-start(bf16[2,2,64,528]{3,2,1,0:T(8,128)(2,1)} %get-tuple-element.930), channel_id=1, source_target_pairs={{0,12},{1,13},{2,14},{3,15},{4,0},{5,1},{6,2},{7,3},{8,4},{9,5},{1... | collective-permute-start | bytes 811016 | tf_op jit(solution)/shard_map/ppermute | solution.py:67
  622.8 32.2 %collective-permute-start.96 = (bf16[128,2048]{1,0:T(8,128)(2,1)S(1)}, bf16[128,2048]{1,0:T(8,128)(2,1)S(1)}, u32[]{:S(2)}, u32[]{:S(2)}) collective-permute-start(bf16[128,2048]{1,0:T(8,128)(2,1)S(1)} %add_convert_fusion.1), channel_id=1, source_target_pairs={{0,12},{1,13},{2,14},{3,15},{4,0},{5,1},{6,2},{7,3},{8,4},{9,5},{1... | collective-permute-start | bytes 1572872 | tf_op jit(solution)/shard_map/ppermute | solution.py:67
  661.3 24.3 %collective-permute-start.99 = (bf16[16,64,640]{2,1,0:T(8,128)(2,1)}, bf16[16,64,640]{2,1,0:T(8,128)(2,1)}, u32[]{:S(2)}, u32[]{:S(2)}) collective-permute-start(bf16[16,64,640]{2,1,0:T(8,128)(2,1)} %slice_bitcast_fusion), channel_id=1, source_target_pairs={{0,1},{1,0},{2,3},{3,2},{4,5},{5,4},{6,7},{7,6},{8,9},{9,8},{10,11... | collective-permute-start | bytes 3932168 | tf_op jit(solution)/shard_map/ppermute | solution.py:67
  (230 other events, 3246.5 us)
Sparse Core Ops, SparseCore 0:
  655.4 53.1 reduce-scatter.1

commit v5 on v4

--- a/solution.py
+++ b/solution.py
@@ -1135,24 +1135,21 @@
     a0 = low(d_mid)
     s_kept, s_away = at(d_shared, x, 1), at(d_shared, 1 - x, 1)
     moved, _, _, made = clock.slot(
-        (z_up, a0), (x_swap, o_away[3]), lasting=1.65, work=[(contract, rows_x[0], d_up)]
+        (z_up, a0), (x_swap, o_away[3]), lasting=1.45, work=[(contract, rows_x[0], d_up)]
     )
     a1, ox3 = moved
     d_up_home = made[0]
-    moved, _, _, _ = clock.slot(
-        (z_up, a1), (x_swap, o_away[2]), (z_down, low(o_home[3] + wide(ox3))), fed_before=clock.lasting
-    )
-    a2, ox2, o_sum = moved
-    o_sum = low(o_home[2] + wide(ox2) + wide(o_sum))
+    moved, _, _, _ = clock.slot((z_up, a1), (x_swap, o_away[2]), fed_before=clock.lasting)
+    a2, ox2 = moved
     moved, _, _, _ = clock.slot((z_up, a2), (x_swap, o_away[1]), feed=0.67)
     a3, ox1 = moved
     moved, _, _, _ = clock.slot(
         (core_swap, jnp.concatenate([a0, a1, a2, a3])), (x_swap, s_away),
-        (z_down, o_sum), feed=0.6,
+        (z_down, low(o_home[3] + wide(ox3))), feed=0.6,
     )
     a_pieces = [a0, a1, a2, a3, moved[0]]
     d_shared = jnp.stack([s_kept, moved[1]], axis=1)
-    o_sum = low(o_home[1] + wide(ox1) + wide(moved[2]))
+    o_sum = low(o_home[2] + wide(ox2) + wide(moved[2]))
     backward = functools.partial(attention_backward, lat_rows=lat_rows)
     moved, _, _, made = clock.slot(
         (z_two, at(d_shared, (z + 2) % 4, 0)), (z_up, at(d_shared, (z + 1) % 4, 0)),
@@ -1161,7 +1158,7 @@
         work=[(backward, scalars, x_pieces, a_pieces, saved, d_gain_mid.reshape(1, width), table)],
     )
     d_shared = jnp.stack([at(d_shared, z, 0), moved[1], moved[0], moved[2]])
-    o_last = o_home[0] + wide(moved[3])
+    o_sum = low(o_home[1] + wide(ox1) + wide(moved[3]))
     d_norm, d_head, d_wl = made[0]
     same_x = [[i for i in range(experts) if i // 2 % 2 == side] for side in range(2)]
     d_normed = lax.psum_scatter(d_norm, "expert", scatter_dimension=0, axis_index_groups=same_x, tiled=True)
@@ -1183,13 +1180,14 @@
         first = (wide(d_head[:4]) + wide(moved[0])).reshape(ndp, 2, 2 * shard, W_COLS)
         second = (wide(d_head[8:12]) + wide(moved[1])).reshape(2, 2, 2 * shard, W_COLS)
         d_wl = (wide(d_wl[0]) + wide(moved[2])).reshape(ndp, 4, 2, shard, -1)
-        d_shared = jnp.stack([s_kept, moved[3]], axis=2).reshape(experts, shard, 3 * ff_part)
+        d_shared = jnp.stack([s_kept, moved[3]], axis=2)
         moved, _, _, made = clock.slot(
             (dp_swap, low(at(first, 1 - dp, 0))), (x_swap, low(at(second, 1 - x, 1))),
-            (x_swap, low(at(d_wl, 1 - x, 2))), feed=0.45,
-            work=[(add_received, d_gate_home, *sent[1][2]), (lambda a: reorder([a], block_index)[0], d_shared)],
+            (x_swap, low(at(d_wl, 1 - x, 2))), (z_down, o_sum), feed=0.45,
+            work=[(add_received, d_gate_home, *sent[1][2])],
         )
-        d_gate_all, d_shared = made
+        d_gate_all = made[0]
+        o_last = o_home[0] + wide(moved[3])
         first = at(first, dp, 0) + wide(moved[0])
         second = at(second, x, 1) + wide(moved[1])
         d_wl = at(d_wl, x, 2) + wide(moved[2])
@@ -1199,8 +1197,9 @@
         d_head = dp_scatter(low(d_head))[0]
         d_wl = wide(at(d_wl, core, 3)) + wide(core_swap(at(d_wl, 1 - core, 3)))
         d_wl = at(d_wl, x, 2) + wide(x_swap(low(at(d_wl, 1 - x, 2))))
-        d_shared = jnp.stack([s_kept, core_swap(s_away)], axis=2).reshape(experts, shard, 3 * ff_part)
-        d_shared = reorder([d_shared], block_index)[0]
+        d_shared = jnp.stack([s_kept, core_swap(s_away)], axis=2)
+        o_last = o_home[0] + wide(z_down(o_sum))
+    d_shared = d_shared.reshape(experts, shard, 3 * ff_part)
     moved, _, _, _ = clock.slot(
         (z_two, at(d_head, (z + 2) % 4, 0)), (z_down, at(d_head, (z + 3) % 4, 0)),
         (z_up, at(d_head, (z + 1) % 4, 0)),
@@ -1230,7 +1229,7 @@
         d_expert.append(wide(dp_scatter(low(jnp.concatenate([contract(e_act, value) for value in rows_g], axis=1)), 1)))
     d_in, _ = rms_back(d_normed, xf, rms_scale(xf), gain_in)
     d_tokens = d_mid + d_in
-    d_shared = wide(d_shared)
+    d_shared = wide(reorder([d_shared], block_index)[0])
     grad_sg, grad_su = (
         d_shared[:, :, i * ff_part : (i + 1) * ff_part].transpose(1, 0, 2).reshape(shard, ff_s) for i in range(2)
     )

time: 794 us -> 777 us (0.979)
  starting transfers between devices: 146 us -> 131 us
    ppermute x82, waiting for transfers between devices: 210 us -> 190 us  [move(): return lax.ppermute(value, 'expert', [(i, to(i)) for i in range(16)])]
    ppermute x33 -> x34, waiting for transfers between devices: 39.8 us -> 57.2 us  [dp_swap(): return lax.ppermute(value, 'dp', [(0, 1), (1, 0)])]
    ppermute x82, starting transfers between devices: 108 us -> 92.2 us  [move(): return lax.ppermute(value, 'expert', [(i, to(i)) for i in range(16)])]
    convert_element_type x17 -> x18, other arithmetic: 17.7 us -> 19.6 us  [low(): return value.astype(BF)]
    unnamed x277 -> x291, local copies, waits for them, and re-layouts: 18.7 us -> 16.8 us
    ppermute x33 -> x34, starting transfers between devices: 38 us -> 38.3 us  [dp_swap(): return lax.ppermute(value, 'dp', [(0, 1), (1, 0)])]
  transfers between devices with their start and end apart: 116 -> 117, of which waited for: 51 -> 48; matrix products, arithmetic and copies ran while one was open for 17% -> 17% of each run, Pallas kernels for 19% -> 20%
where the time goes in v5:
time: 777 us; the launch traced here: 768 us
  waiting for transfers between devices  247 us (32%)
  Pallas kernels  184 us (24%)
  starting transfers between devices  131 us (17%)
  other arithmetic  90.5 us (12%)
  local copies, waits for them, and re-layouts  72.2 us (9%)
  matrix products  27 us (3%)
  between operations  16.4 us (2%)
    ppermute x82, waiting for transfers between devices, move(): return lax.ppermute(value, 'expert', [(i, to(i)) for i in range(16)])  190 us
    pallas_call x10, Pallas kernels, whole_call(): pl.pallas_call(kernel, in_specs=specs, out_specs=[vmem] * len(outs), out_...  106 us
    ppermute x82, starting transfers between devices, move(): return lax.ppermute(value, 'expert', [(i, to(i)) for i in range(16)])  92.2 us
    pallas_call x3, Pallas kernels, tiled_call(): pl.pallas_call(kernel, grid=(steps,), in_specs=specs, out_specs=out_specs...  77.8 us
    ppermute x34, waiting for transfers between devices, dp_swap(): return lax.ppermute(value, 'dp', [(0, 1), (1, 0)])  57.2 us
    ppermute x34, starting transfers between devices, dp_swap(): return lax.ppermute(value, 'dp', [(0, 1), (1, 0)])  38.3 us
    slice x19, local copies, waits for them, and re-layouts, next_rows(): moves.append((self.go, array[start:stop]))  28.7 us
    dot_general x5, matrix products, contract(): lax.dot_general(left, right, (((0,), (0,)), ((), ())), preferred_element_...  27 us
  transfers between devices with their start and end apart: 117, of which 48 were waited for; matrix products, arithmetic and copies ran while one was open for 17% of the time, Pallas kernels for 20%

profile of v5, /device:TPU:0, one launch (start us, length us, event | category | flops | bytes accessed | tf_op | source)
XLA Modules:
  0.0 767.9 jit_solution(1979563671522443043)
XLA Ops:
  34.2 7.9 %collective-permute-done.4.refs_1_ = bf16[128,2048]{1,0:T(8,128)(2,1)S(1)} collective-permute-done((bf16[128,2048]{1,0:T(8,128)(2,1)S(1)}, bf16[128,2048]{1,0:T(8,128)(2,1)S(1)}, u32[]{:S(2)}, u32[]{:S(2)}) %collective-permute-start.4) | collective-permute-done | bytes 524320 | tf_op jit(solution)/shard_map/ppermute | solution.py:67
  56.5 14.5 %collective-permute-done.6 = bf16[128,1152]{1,0:T(8,128)(2,1)S(1)} collective-permute-done((bf16[128,1152]{1,0:T(8,128)(2,1)}, bf16[128,1152]{1,0:T(8,128)(2,1)S(1)}, u32[]{:S(2)}, u32[]{:S(2)}) %collective-permute-start.6) | collective-permute-done | bytes 294944 | tf_op jit(solution)/shard_map/ppermute | solution.py:67
  81.6 11.2 %collective-permute-done.12.refs_2_ = bf16[128,2048]{1,0:T(8,128)(2,1)S(1)} collective-permute-done((bf16[128,2048]{1,0:T(8,128)(2,1)S(1)}, bf16[128,2048]{1,0:T(8,128)(2,1)S(1)}, u32[]{:S(2)}, u32[]{:S(2)}) %collective-permute-start.12) | collective-permute-done | bytes 524320 | tf_op jit(solution)/shard_map/ppermute | solution.py:67
  92.7 6.9 collective-permute-done.13.refs_1_.refs_14_
  111.7 7.4 collective-permute-done.17.refs_3_
  146.7 19.2 %shard_map.298 = (bf16[512,2048]{1,0:T(8,128)(2,1)}, bf16[512,2048]{1,0:T(8,128)(2,1)}, bf16[1024,384]{1,0:T(8,128)(2,1)}, bf16[1024,128]{1,0:T(8,128)(2,1)}, f3...) custom-call(s32[68]{0:T(128)} %concatenate.124.place_ref, ...), custom_call_target="tpu_custom_call" | custom-call | flops 5368709120 | bytes 25294848 | tf_op jit(solution)/shard_map/pallas_call | solution.py:166
  169.1 15.1 %collective-permute-done.30 = bf16[2,2,64,528]{3,2,1,0:T(8,128)(2,1)S(1)} collective-permute-done((bf16[2,2,64,528]{3,2,1,0:T(8,128)(2,1)}, bf16[2,2,64,528]{3,2,1,0:T(8,128)(2,1)S(1)}, u32[]{:S(2)}, u32[]{:S(2)}) %collective-permute-start.30) | collective-permute-done | bytes 270368 | tf_op jit(solution)/shard_map/ppermute | solution.py:67
  190.8 8.0 %collective-permute-start.33 = (bf16[128,2048]{1,0:T(8,128)(2,1)}, bf16[128,2048]{1,0:T(8,128)(2,1)}, u32[]{:S(2)}, u32[]{:S(2)}) collective-permute-start(bf16[128,2048]{1,0:T(8,128)(2,1)} %add_convert_fusion.16), channel_id=1, source_target_pairs={{0,12},{1,13},{2,14},{3,15},{4,0},{5,1},{6,2},{7,3},{8,4},{9,5},{1... | collective-permute-start | bytes 1572872 | tf_op jit(solution)/shard_map/ppermute | solution.py:67
  220.8 7.7 %collective-permute-done.36 = bf16[128,2048]{1,0:T(8,128)(2,1)S(1)} collective-permute-done((bf16[128,2048]{1,0:T(8,128)(2,1)S(1)}, bf16[128,2048]{1,0:T(8,128)(2,1)S(1)}, u32[]{:S(2)}, u32[]{:S(2)}) %collective-permute-start.36) | collective-permute-done | bytes 524320 | tf_op jit(solution)/shard_map/ppermute | solution.py:67
  235.0 9.4 %collective-permute-done.40 = bf16[128,2048]{1,0:T(8,128)(2,1)S(1)} collective-permute-done((bf16[128,2048]{1,0:T(8,128)(2,1)S(1)}, bf16[128,2048]{1,0:T(8,128)(2,1)S(1)}, u32[]{:S(2)}, u32[]{:S(2)}) %collective-permute-start.40) | collective-permute-done | bytes 524320 | tf_op jit(solution)/shard_map/ppermute | solution.py:67
  267.3 13.6 %collective-permute-done.46.refs_2_ = bf16[128,2048]{1,0:T(8,128)(2,1)} collective-permute-done((bf16[128,2048]{1,0:T(8,128)(2,1)S(1)}, bf16[128,2048]{1,0:T(8,128)(2,1)}, u32[]{:S(2)}, u32[]{:S(2)}) %collective-permute-start.46) | collective-permute-done | bytes 524320 | tf_op jit(solution)/shard_map/ppermute | solution.py:67
  284.1 6.9 shard_map.300
  343.4 15.1 %shard_map.303 = (bf16[2048,256]{1,0:T(8,128)(2,1)}, bf16[2048,512]{1,0:T(8,128)(2,1)}) custom-call(bf16[128,2048]{1,0:T(8,128)(2,1)} %copy-done.8, bf16[128,2048]{1,0:T(8,128)(2,1)} %copy-done.42, bf16[128,2048]{1,0:T(8,128)(2,1)} %collective-permute-done.46.refs_2_, bf16[128,2048]{1,0:T(8,128)(2,1)} %collective-permute-done.49.refs_3_, ...), custom_call_target="tpu_custom_call" | custom-call | flops 6442450944 | bytes 23068672 | tf_op jit(solution)/shard_map/pallas_call | solution.py:166
  359.4 30.7 %shard_map.304 = (bf16[1024,1408]{1,0:T(8,128)(2,1)}, bf16[1024,1408]{1,0:T(8,128)(2,1)}, bf16[1024,1408]{1,0:T(8,128)(2,1)}, bf16[1408,1024]{1,0:T(8,128)(2,1)}) custom-call(bf16[1024,1024]{1,0:T(8,128)(2,1)} %get-tuple-element.901.x0_ref, bf16[1024,1024]{1,0:T(8,128)(2,1)} %get-tuple-element.878.x1_ref, bf16[1024,1024]{1,0:T(8,128)(2,1)} %get-tuple-element.881.r0_ref, ...), custom_call_target="tpu_custom_call" | custom-call | flops 20669530112 | bytes 37224448 | tf_op jit(solution)/shard_map/pallas_call | solution.py:668
  394.4 28.8 %shard_map.305 = (bf16[512,2048]{1,0:T(8,128)(2,1)}, bf16[512,2048]{1,0:T(8,128)(2,1)}, bf16[512,2048]{1,0:T(8,128)(2,1)}, bf16[512,2048]{1,0:T(8,128)(2,1)}) custom-call(bf16[1024,1408]{1,0:T(8,128)(2,1)} %get-tuple-element.893.dg_ref, bf16[1024,1408]{1,0:T(8,128)(2,1)} %get-tuple-element.902.du_ref, bf16[1024,1408]{1,0:T(8,128)(2,1)} %bitcast.218, ...), custom_call_target="tpu_custom_call" | custom-call | flops 17179869184 | bytes 29892608 | tf_op jit(solution)/shard_map/pallas_call | solution.py:668
  444.9 15.1 %shard_map.306 = bf16[2048,528]{1,0:T(8,128)(2,1)} custom-call(bf16[128,2048]{1,0:T(8,128)(2,1)} %copy-done.8, bf16[128,2048]{1,0:T(8,128)(2,1)} %copy-done.42, bf16[128,2048]{1,0:T(8,128)(2,1)} %collective-permute-done.46.refs_2_, bf16[128,2048]{1,0:T(8,128)(2,1)} %collective-permute-done.49.refs_3_, bf16[128,2048]{1,0:T(8,128)(2,1)} %collective-permute-done.44.refs_4_, ...), custom_call_target="tpu_custom_call" | custom-call | flops 6442450944 | bytes 22085632 | tf_op jit(solution)/shard_map/pallas_call | solution.py:166
  467.8 18.3 %shard_map.307 = (bf16[512,2048]{1,0:T(8,128)(2,1)}, bf16[512,2048]{1,0:T(8,128)(2,1)}, bf16[512,2048]{1,0:T(8,128)(2,1)}, bf16[512,2048]{1,0:T(8,128)(2,1)}) custom-call(bf16[1024,1408]{1,0:T(8,128)(2,1)} %get-tuple-element.880.act_ref, f32[1024,1]{1,0:T(8,128)} %get-tuple-element.856.share_ref, bf16[1408,1024]{1,0:T(8,128)(2,1)} %bitcast.216, ...), custom_call_target="tpu_custom_call" | custom-call | flops 9126805504 | bytes 19148800 | tf_op jit(solution)/shard_map/pallas_call | solution.py:668
  547.4 10.1 %collective-permute-done.81.refs_8_ = bf16[128,2048]{1,0:T(8,128)(2,1)S(1)} collective-permute-done((bf16[128,2048]{1,0:T(8,128)(2,1)S(1)}, bf16[128,2048]{1,0:T(8,128)(2,1)S(1)}, u32[]{:S(2)}, u32[]{:S(2)}) %collective-permute-start.81) | collective-permute-done | bytes 524320 | tf_op jit(solution)/shard_map/ppermute | solution.py:67
  566.5 9.5 %collective-permute-done.85.refs_9_ = bf16[128,2048]{1,0:T(8,128)(2,1)S(1)} collective-permute-done((bf16[128,2048]{1,0:T(8,128)(2,1)S(1)}, bf16[128,2048]{1,0:T(8,128)(2,1)S(1)}, u32[]{:S(2)}, u32[]{:S(2)}) %collective-permute-start.85) | collective-permute-done | bytes 524320 | tf_op jit(solution)/shard_map/ppermute | solution.py:67
  583.3 12.7 %collective-permute-done.87 = bf16[96,1408]{1,0:T(8,128)(2,1)S(1)} collective-permute-done((bf16[96,1408]{1,0:T(8,128)(2,1)S(1)}, bf16[96,1408]{1,0:T(8,128)(2,1)S(1)}, u32[]{:S(2)}, u32[]{:S(2)}) %collective-permute-start.87) | collective-permute-done | bytes 270368 | tf_op jit(solution)/shard_map/ppermute | solution.py:840
  604.1 30.8 %shard_map.308 = (bf16[1024,2048]{1,0:T(8,128)(2,1)}, bf16[16,128,768]{2,1,0:T(8,128)(2,1)}, bf16[2,16,64,640]{3,2,1,0:T(8,128)(2,1)}, bf16[16,128]{1,0:T(8,128)(2,1)}) custom-call(s32[68]{0:T(128)} %concatenate.124.place_ref, bf16[128,2048]{1,0:T(8,128)(2,1)} %refs_0_.1, bf16[128,2048]{1,0:T(8,128)(2,1)} %copy-done.89, bf16[128,2048]{1,0:T(8,128)(2,1)} %copy-done.90, ...), custom_call_target="tpu_custom_call" | custom-call | flops 10737418240 | bytes 28964864 | tf_op jit(solution)/shard_map/pallas_call | solution.py:166
  653.2 8.7 %collective-permute-done.97 = bf16[4,128,768]{2,1,0:T(8,128)(2,1)S(1)} collective-permute-done((bf16[4,128,768]{2,1,0:T(8,128)(2,1)S(1)}, bf16[4,128,768]{2,1,0:T(8,128)(2,1)S(1)}, u32[]{:S(2)}, u32[]{:S(2)}) %collective-permute-start.97) | collective-permute-done | bytes 786464 | tf_op jit(solution)/shard_map/ppermute | solution.py:67
  676.5 7.0 collective-permute-done.101
  683.5 12.8 %collective-permute-done.105 = bf16[128,2048]{1,0:T(8,128)(2,1)S(1)} collective-permute-done((bf16[128,2048]{1,0:T(8,128)(2,1)}, bf16[128,2048]{1,0:T(8,128)(2,1)S(1)}, u32[]{:S(2)}, u32[]{:S(2)}) %collective-permute-start.105) | collective-permute-done | bytes 524320 | tf_op jit(solution)/shard_map/ppermute | solution.py:67
  (678 shorter events, 423.9 us)
Async XLA Ops:
  7.2 740.2 %reduce-scatter.2.cloned.1.call-start = ((), (), s32[]{:S(2)}) async-start(), calls=%async_computation.1 | async-start | bytes 4718592 | tf_op jit(solution)/shard_map/reduce_scatter | solution.py:1164
  46.8 26.2 %collective-permute-start.5 = (bf16[576,1024]{1,0:T(8,128)(2,1)}, bf16[576,1024]{1,0:T(8,128)(2,1)}, u32[]{:S(2)}, u32[]{:S(2)}) collective-permute-start(bf16[576,1024]{1,0:T(8,128)(2,1)} %slice_bitcast_fusion.1), channel_id=1, source_target_pairs={{0,16},{16,0},{1,17},{17,1},{2,18},{18,2},{3,19},{19,3},{4,20},{20... | collective-permute-start | bytes 3538952 | tf_op jit(solution)/shard_map/ppermute | solution.py:840
  48.3 22.7 %collective-permute-start.9 = (bf16[4,2,64,528]{3,2,1,0:T(8,128)(2,1)}, bf16[4,2,64,528]{3,2,1,0:T(8,128)(2,1)}, u32[]{:S(2)}, u32[]{:S(2)}) collective-permute-start(bf16[4,2,64,528]{3,2,1,0:T(8,128)(2,1)} %get-tuple-element.534), channel_id=1, source_target_pairs={{0,2},{1,3},{2,0},{3,1},{4,6},{5,7},{6,4},{7,5},{8,10},{9,11},{10,... | collective-permute-start | bytes 1622024 | tf_op jit(solution)/shard_map/ppermute | solution.py:67
  73.3 26.4 %collective-permute-start.10 = (bf16[4,128,1152]{2,1,0:T(8,128)(2,1)S(1)}, bf16[4,128,1152]{2,1,0:T(8,128)(2,1)S(1)}, u32[]{:S(2)}, u32[]{:S(2)}) collective-permute-start(bf16[4,128,1152]{2,1,0:T(8,128)(2,1)S(1)} %pad_maximum_fusion.12.refs_6_.refs_0_), channel_id=1, source_target_pairs={{0,2},{1,3},{2,0},{3,1},{4,6},{5,7},{6,4},{7,5},{8,10},{9,11},{10,... | collective-permute-start | bytes 3538952 | tf_op jit(solution)/shard_map/ppermute | solution.py:67
  74.6 25.1 %collective-permute-start.11 = (bf16[4,128,1152]{2,1,0:T(8,128)(2,1)S(1)}, bf16[4,128,1152]{2,1,0:T(8,128)(2,1)S(1)}, u32[]{:S(2)}, u32[]{:S(2)}) collective-permute-start(bf16[4,128,1152]{2,1,0:T(8,128)(2,1)S(1)} %pad_maximum_fusion.12.refs_6_.refs_0_), channel_id=1, source_target_pairs={{0,16},{16,0},{1,17},{17,1},{2,18},{18,2},{3,19},{19,3},{4,20},{20... | collective-permute-start | bytes 3538952 | tf_op jit(solution)/shard_map/ppermute | solution.py:840
  137.4 28.4 %collective-permute-start.25 = (bf16[128,2048]{1,0:T(8,128)(2,1)S(1)}, bf16[128,2048]{1,0:T(8,128)(2,1)S(1)}, u32[]{:S(2)}, u32[]{:S(2)}) collective-permute-start(bf16[128,2048]{1,0:T(8,128)(2,1)S(1)} %fusion.9.refs_0_.refs_13_), channel_id=1, source_target_pairs={{0,2},{1,3},{2,0},{3,1},{4,6},{5,7},{6,4},{7,5},{8,10},{9,11},{10,... | collective-permute-start | bytes 1572872 | tf_op jit(solution)/shard_map/ppermute | solution.py:67
  138.2 27.7 %collective-permute-start.26 = (bf16[128,2048]{1,0:T(8,128)(2,1)S(1)}, bf16[128,2048]{1,0:T(8,128)(2,1)S(1)}, u32[]{:S(2)}, u32[]{:S(2)}) collective-permute-start(bf16[128,2048]{1,0:T(8,128)(2,1)S(1)} %collective-permute-done.13.refs_1_.refs_14_), channel_id=1, source_target_pairs={{0,4},{1,5},{2,6},{3,7},{4,8},{5,9},{6,10},{7,11},{8,12},{9,13},{1... | collective-permute-start | bytes 1572872 | tf_op jit(solution)/shard_map/ppermute | solution.py:67
  139.6 26.3 %collective-permute-start.27 = (bf16[128,2048]{1,0:T(8,128)(2,1)S(1)}, bf16[128,2048]{1,0:T(8,128)(2,1)S(1)}, u32[]{:S(2)}, u32[]{:S(2)}) collective-permute-start(bf16[128,2048]{1,0:T(8,128)(2,1)S(1)} %fusion.9.refs_0_.refs_13_), channel_id=1, source_target_pairs={{0,12},{1,13},{2,14},{3,15},{4,0},{5,1},{6,2},{7,3},{8,4},{9,5},{1... | collective-permute-start | bytes 1572872 | tf_op jit(solution)/shard_map/ppermute | solution.py:67
  142.5 23.4 %collective-permute-start.24 = (bf16[352,1408]{1,0:T(8,128)(2,1)}, bf16[352,1408]{1,0:T(8,128)(2,1)}, u32[]{:S(2)}, u32[]{:S(2)}) collective-permute-start(bf16[352,1408]{1,0:T(8,128)(2,1)} %slice_bitcast_fusion.5), channel_id=1, source_target_pairs={{0,16},{16,0},{1,17},{17,1},{2,18},{18,2},{3,19},{19,3},{4,20},{20... | collective-permute-start | bytes 2973704 | tf_op jit(solution)/shard_map/ppermute | solution.py:840
  189.8 21.7 %collective-permute-start.32 = (bf16[224,1408]{1,0:T(8,128)(2,1)}, bf16[224,1408]{1,0:T(8,128)(2,1)}, u32[]{:S(2)}, u32[]{:S(2)}) collective-permute-start(bf16[224,1408]{1,0:T(8,128)(2,1)} %get-tuple-element.629), channel_id=1, source_target_pairs={{0,16},{16,0},{1,17},{17,1},{2,18},{18,2},{3,19},{19,3},{4,20},{20... | collective-permute-start | bytes 1892360 | tf_op jit(solution)/shard_map/ppermute | solution.py:840
  335.9 22.6 %collective-permute-start.60 = (bf16[224,1408]{1,0:T(8,128)(2,1)S(1)}, bf16[224,1408]{1,0:T(8,128)(2,1)S(1)}, u32[]{:S(2)}, u32[]{:S(2)}) collective-permute-start(bf16[224,1408]{1,0:T(8,128)(2,1)S(1)} %copy-done.67), channel_id=1, source_target_pairs={{0,16},{16,0},{1,17},{17,1},{2,18},{18,2},{3,19},{19,3},{4,20},{20... | collective-permute-start | bytes 1892360 | tf_op jit(solution)/shard_map/ppermute | solution.py:840
  393.3 32.4 %collective-permute-start.61 = (bf16[704,1024]{1,0:T(8,128)(2,1)S(1)}, bf16[704,1024]{1,0:T(8,128)(2,1)S(1)}, u32[]{:S(2)}, u32[]{:S(2)}) collective-permute-start(bf16[704,1024]{1,0:T(8,128)(2,1)S(1)} %slice.427), channel_id=1, source_target_pairs={{0,16},{16,0},{1,17},{17,1},{2,18},{18,2},{3,19},{19,3},{4,20},{20... | collective-permute-start | bytes 4325384 | tf_op jit(solution)/shard_map/ppermute | solution.py:840
  463.1 23.2 %collective-permute-start.67 = (bf16[192,1024]{1,0:T(8,128)(2,1)}, bf16[192,1024]{1,0:T(8,128)(2,1)S(1)}, u32[]{:S(2)}, u32[]{:S(2)}) collective-permute-start(bf16[192,1024]{1,0:T(8,128)(2,1)} %slice.425), channel_id=1, source_target_pairs={{0,16},{16,0},{1,17},{17,1},{2,18},{18,2},{3,19},{19,3},{4,20},{20... | collective-permute-start | bytes 1179656 | tf_op jit(solution)/shard_map/ppermute | solution.py:840
  464.2 22.1 %collective-permute-start.69 = (bf16[128,2048]{1,0:T(8,128)(2,1)}, bf16[128,2048]{1,0:T(8,128)(2,1)}, u32[]{:S(2)}, u32[]{:S(2)}) collective-permute-start(bf16[128,2048]{1,0:T(8,128)(2,1)} %get-tuple-element.853), channel_id=1, source_target_pairs={{0,2},{1,3},{2,0},{3,1},{4,6},{5,7},{6,4},{7,5},{8,10},{9,11},{10,... | collective-permute-start | bytes 1572872 | tf_op jit(solution)/shard_map/ppermute | solution.py:67
  464.9 21.4 %collective-permute-start.70 = (bf16[128,2048]{1,0:T(8,128)(2,1)}, bf16[128,2048]{1,0:T(8,128)(2,1)}, u32[]{:S(2)}, u32[]{:S(2)}) collective-permute-start(bf16[128,2048]{1,0:T(8,128)(2,1)} %add_convert_fusion.11), channel_id=1, source_target_pairs={{0,12},{1,13},{2,14},{3,15},{4,0},{5,1},{6,2},{7,3},{8,4},{9,5},{1... | collective-permute-start | bytes 1572872 | tf_op jit(solution)/shard_map/ppermute | solution.py:67
  530.1 31.8 %collective-permute-start.83 = (bf16[512,1408]{1,0:T(8,128)(2,1)S(1)}, bf16[512,1408]{1,0:T(8,128)(2,1)S(1)}, u32[]{:S(2)}, u32[]{:S(2)}) collective-permute-start(bf16[512,1408]{1,0:T(8,128)(2,1)S(1)} %slice.504), channel_id=1, source_target_pairs={{0,16},{16,0},{1,17},{17,1},{2,18},{18,2},{3,19},{19,3},{4,20},{20... | collective-permute-start | bytes 4325384 | tf_op jit(solution)/shard_map/ppermute | solution.py:840
  597.8 37.2 %collective-permute-start.92 = (bf16[576,1408]{1,0:T(8,128)(2,1)}, bf16[576,1408]{1,0:T(8,128)(2,1)}, u32[]{:S(2)}, u32[]{:S(2)}) collective-permute-start(bf16[576,1408]{1,0:T(8,128)(2,1)} %slice.499), channel_id=1, source_target_pairs={{0,16},{16,0},{1,17},{17,1},{2,18},{18,2},{3,19},{19,3},{4,20},{20... | collective-permute-start | bytes 4866056 | tf_op jit(solution)/shard_map/ppermute | solution.py:840
  599.3 35.7 %collective-permute-start.93 = (bf16[2,2,64,528]{3,2,1,0:T(8,128)(2,1)}, bf16[2,2,64,528]{3,2,1,0:T(8,128)(2,1)}, u32[]{:S(2)}, u32[]{:S(2)}) collective-permute-start(bf16[2,2,64,528]{3,2,1,0:T(8,128)(2,1)} %get-tuple-element.929), channel_id=1, source_target_pairs={{0,8},{1,9},{2,10},{3,11},{4,12},{5,13},{6,14},{7,15},{8,0},{9,1},... | collective-permute-start | bytes 811016 | tf_op jit(solution)/shard_map/ppermute | solution.py:67
  599.7 35.2 %collective-permute-start.94 = (bf16[2,2,64,528]{3,2,1,0:T(8,128)(2,1)}, bf16[2,2,64,528]{3,2,1,0:T(8,128)(2,1)}, u32[]{:S(2)}, u32[]{:S(2)}) collective-permute-start(bf16[2,2,64,528]{3,2,1,0:T(8,128)(2,1)} %get-tuple-element.930), channel_id=1, source_target_pairs={{0,4},{1,5},{2,6},{3,7},{4,8},{5,9},{6,10},{7,11},{8,12},{9,13},{1... | collective-permute-start | bytes 811016 | tf_op jit(solution)/shard_map/ppermute | solution.py:67
  600.4 34.6 %collective-permute-start.95 = (bf16[2,2,64,528]{3,2,1,0:T(8,128)(2,1)}, bf16[2,2,64,528]{3,2,1,0:T(8,128)(2,1)}, u32[]{:S(2)}, u32[]{:S(2)}) collective-permute-start(bf16[2,2,64,528]{3,2,1,0:T(8,128)(2,1)} %get-tuple-element.931), channel_id=1, source_target_pairs={{0,12},{1,13},{2,14},{3,15},{4,0},{5,1},{6,2},{7,3},{8,4},{9,5},{1... | collective-permute-start | bytes 811016 | tf_op jit(solution)/shard_map/ppermute | solution.py:67
  603.6 31.4 %collective-permute-start.96 = (bf16[128,2048]{1,0:T(8,128)(2,1)S(1)}, bf16[128,2048]{1,0:T(8,128)(2,1)}, u32[]{:S(2)}, u32[]{:S(2)}) collective-permute-start(bf16[128,2048]{1,0:T(8,128)(2,1)S(1)} %add_convert_fusion.2), channel_id=1, source_target_pairs={{0,12},{1,13},{2,14},{3,15},{4,0},{5,1},{6,2},{7,3},{8,4},{9,5},{1... | collective-permute-start | bytes 1572872 | tf_op jit(solution)/shard_map/ppermute | solution.py:67
  666.7 29.6 %collective-permute-start.105 = (bf16[128,2048]{1,0:T(8,128)(2,1)}, bf16[128,2048]{1,0:T(8,128)(2,1)S(1)}, u32[]{:S(2)}, u32[]{:S(2)}) collective-permute-start(bf16[128,2048]{1,0:T(8,128)(2,1)} %add_convert_fusion.1), channel_id=1, source_target_pairs={{0,12},{1,13},{2,14},{3,15},{4,0},{5,1},{6,2},{7,3},{8,4},{9,5},{1... | collective-permute-start | bytes 1572872 | tf_op jit(solution)/shard_map/ppermute | solution.py:67
  668.4 27.9 %collective-permute-start.104 = (bf16[2,4,64,640]{3,2,1,0:T(8,128)(2,1)S(1)}, bf16[2,4,64,640]{3,2,1,0:T(8,128)(2,1)S(1)}, u32[]{:S(2)}, u32[]{:S(2)}) collective-permute-start(bf16[2,4,64,640]{3,2,1,0:T(8,128)(2,1)S(1)} %fusion.14), channel_id=1, source_target_pairs={{0,2},{1,3},{2,0},{3,1},{4,6},{5,7},{6,4},{7,5},{8,10},{9,11},{10,... | collective-permute-start | bytes 1966088 | tf_op jit(solution)/shard_map/ppermute | solution.py:67
  700.9 22.5 %collective-permute-start.106 = (bf16[160,1408]{1,0:T(8,128)(2,1)}, bf16[160,1408]{1,0:T(8,128)(2,1)}, u32[]{:S(2)}, u32[]{:S(2)}) collective-permute-start(bf16[160,1408]{1,0:T(8,128)(2,1)} %get-tuple-element.999), channel_id=1, source_target_pairs={{0,16},{16,0},{1,17},{17,1},{2,18},{18,2},{3,19},{19,3},{4,20},{20... | collective-permute-start | bytes 1351688 | tf_op jit(solution)/shard_map/ppermute | solution.py:840
  (238 other events, 3217.4 us)
Sparse Core Ops, SparseCore 0:
  635.2 64.0 reduce-scatter.1

commit v6 on v5

--- a/solution.py
+++ b/solution.py
@@ -912,9 +912,8 @@
     else:
         lat = small
     s_kept, s_away = at(s_piece, core, 2), at(s_piece, 1 - core, 2)
-    clock.slot(feed=0.65)
-    moved, _, _, _ = clock.slot((core_swap, away), (core_swap, s_away), (z_up, x0), feed=0.59)
-    x1 = moved[2]
+    x1 = clock.slot((z_up, x0), feed=0.65)[0][0]
+    moved, _, _, _ = clock.slot((core_swap, away), (core_swap, s_away), feed=0.15)
     s_piece = jnp.stack([s_kept, moved[1]], axis=2)
     w_own = jnp.where(
         core == 0, jnp.concatenate([kept, moved[0]], axis=1), jnp.concatenate([moved[0], kept], axis=1)
@@ -956,9 +955,9 @@
         w_far, x3, lat_other_xy, cx01 = moved[:2], *moved[2:]
         lat_far = jnp.concatenate([w_far[0][..., W_COLS:], w_far[1][..., W_COLS:]])
         moved, _, _, _ = clock.slot(
-            (core_swap, lat_far), (core_swap, jnp.concatenate([x2, x3])), (z_up, s_up), feed=0.5
+            (core_swap, lat_far), (core_swap, jnp.concatenate([x2, x3])), (z_up, s_up), (z_down, s_down), feed=0.55
         )
-        cx23, s_up = moved[1:]
+        cx23, s_up, s_down = moved[1:]
         weights = [w_own, w_x, w_y] + w_far
         layout_of = ((0, 0, 0), (1, 0, 0), (0, 1, 0), (1, 1, 0), (1, 1, 2))
         w_lat = [lat_other, lat_other_xy, moved[0]]
@@ -966,7 +965,7 @@
         route_from = [w_own, w_x, lat_other, lat_other_xy]
         route_lanes = (W_COLS + 256, W_COLS + 256, 256, 256)
     else:
-        x3, s_up = z_up(x2), z_up(s_up)
+        x3, s_up, s_down = z_up(x2), z_up(s_up), z_down(s_down)
         cx01, cx23 = core_swap(jnp.concatenate([x0, x1])), core_swap(jnp.concatenate([x2, x3]))
         near, far = dp_gather(w_own[None], 0), dp_gather(w_x[None], 0)
         weights = [near[i] for i in range(ndp)] + [far[i] for i in range(ndp)]
@@ -1004,8 +1003,8 @@
     (part_near, part_far), saved = made[0]
     gain_in, gain_mid, gain_lat = saved[-3:]
 
-    moved, _, _, _ = clock.slot((core_swap, part_far), (z_two, s_two), (z_down, s_down), feed=0.65)
-    s_two, s_down = moved[1:]
+    moved, _, _, _ = clock.slot((core_swap, part_far), (z_two, s_two), feed=0.55)
+    s_two = moved[1]
     s_piece = jnp.stack([at(s_piece, z, 0), s_up, s_two, s_down]).reshape(experts, shard, 3 * ff_part)
     g_near = jnp.concatenate([g0, g1, g2, g3])
     terms = [wide(cut(part_near, k)) + wide(cut(moved[0], k)) for k in range(4)]
@@ -1018,7 +1017,7 @@
         (z_down, low(terms[2] + wide(moved[0]))), (x_swap, g2), (core_swap, g_near), feed=0.67
     )
     gx2, cg_near = moved[1:]
-    moved, _, _, _ = clock.slot((z_down, low(terms[1] + wide(moved[0]))), (x_swap, g3), feed=0.67)
+    moved, _, _, _ = clock.slot((z_down, low(terms[1] + wide(moved[0]))), (x_swap, g3), feed=0.45)
     gx3 = moved[1]
     xf = wide(tokens)
     mid = xf + terms[0] + wide(moved[0])
@@ -1057,7 +1056,7 @@
         s_pieces = jnp.split(dp_gather(s_piece[None], 0), ndp)
         s_pieces = [value.reshape(s_piece.shape) for value in s_pieces]
     moved, _, _, made = clock.slot(
-        (core_swap, tx2), (core_swap, tx3), feed=0.4,
+        (core_swap, tx2), (core_swap, tx3), feed=0.55,
         work=[(lambda *a: shared_weights(a, block_index, ff_pad), *s_pieces)],
     )
     s_both, s_down_w = made[0]

time: 777 us -> 775 us (level)
  local copies, waits for them, and re-layouts: 72.2 us -> 83.7 us
  other arithmetic: 90.5 us -> 80 us
    unnamed x291 -> x294, local copies, waits for them, and re-layouts: 16.8 us -> 29.9 us
    ppermute x34 -> x35, waiting for transfers between devices: 57.2 us -> 68 us  [dp_swap(): return lax.ppermute(value, 'dp', [(0, 1), (1, 0)])]
    concatenate x2 -> x0, other arithmetic: 9.82 us -> none  [local(): join = lambda *pieces: jnp.concatenate(pieces, axis=0)]
    ppermute x82, waiting for transfers between devices: 190 us -> 181 us  [move(): return lax.ppermute(value, 'expert', [(i, to(i)) for i in range(16)])]
    ppermute x34 -> x35, starting transfers between devices: 38.3 us -> 36.9 us  [dp_swap(): return lax.ppermute(value, 'dp', [(0, 1), (1, 0)])]
    slice x19 -> x22, local copies, waits for them, and re-layouts: 28.7 us -> 27.6 us  [next_rows(): moves.append((self.go, array[start:stop]))]
  transfers between devices with their start and end apart: 117 -> 118, of which waited for: 48 -> 51; matrix products, arithmetic and copies ran while one was open for 17% -> 17% of each run, Pallas kernels for 20% -> 20%
where the time goes in v6:
time: 775 us; the launch traced here: 765 us
  waiting for transfers between devices  249 us (32%)
  Pallas kernels  184 us (24%)
  starting transfers between devices  125 us (16%)
  local copies, waits for them, and re-layouts  83.7 us (11%)
  other arithmetic  80 us (10%)
  matrix products  27 us (3%)
  between operations  16.4 us (2%)
    ppermute x82, waiting for transfers between devices, move(): return lax.ppermute(value, 'expert', [(i, to(i)) for i in range(16)])  181 us
    pallas_call x10, Pallas kernels, whole_call(): pl.pallas_call(kernel, in_specs=specs, out_specs=[vmem] * len(outs), out_...  106 us
    ppermute x82, starting transfers between devices, move(): return lax.ppermute(value, 'expert', [(i, to(i)) for i in range(16)])  88.3 us
    pallas_call x3, Pallas kernels, tiled_call(): pl.pallas_call(kernel, grid=(steps,), in_specs=specs, out_specs=out_specs...  77.6 us
    ppermute x35, waiting for transfers between devices, dp_swap(): return lax.ppermute(value, 'dp', [(0, 1), (1, 0)])  68 us
    ppermute x35, starting transfers between devices, dp_swap(): return lax.ppermute(value, 'dp', [(0, 1), (1, 0)])  36.9 us
    unnamed x294, local copies, waits for them, and re-layouts  29.9 us
    slice x22, local copies, waits for them, and re-layouts, next_rows(): moves.append((self.go, array[start:stop]))  27.6 us
  transfers between devices with their start and end apart: 118, of which 51 were waited for; matrix products, arithmetic and copies ran while one was open for 17% of the time, Pallas kernels for 20%

profile of v6, /device:TPU:0, one launch (start us, length us, event | category | flops | bytes accessed | tf_op | source)
XLA Modules:
  0.0 765.0 jit_solution(15853871356531670092)
XLA Ops:
  48.6 15.0 %collective-permute-done.6 = bf16[128,1152]{1,0:T(8,128)(2,1)S(1)} collective-permute-done((bf16[128,1152]{1,0:T(8,128)(2,1)}, bf16[128,1152]{1,0:T(8,128)(2,1)S(1)}, u32[]{:S(2)}, u32[]{:S(2)}) %collective-permute-start.6) | collective-permute-done | bytes 294944 | tf_op jit(solution)/shard_map/ppermute | solution.py:67
  74.6 11.0 %collective-permute-done.12.refs_2_ = bf16[128,2048]{1,0:T(8,128)(2,1)S(1)} collective-permute-done((bf16[128,2048]{1,0:T(8,128)(2,1)}, bf16[128,2048]{1,0:T(8,128)(2,1)S(1)}, u32[]{:S(2)}, u32[]{:S(2)}) %collective-permute-start.12) | collective-permute-done | bytes 524320 | tf_op jit(solution)/shard_map/ppermute | solution.py:67
  85.6 7.9 %collective-permute-done.13.refs_1_.refs_14_ = bf16[128,2048]{1,0:T(8,128)(2,1)S(1)} collective-permute-done((bf16[128,2048]{1,0:T(8,128)(2,1)S(1)}, bf16[128,2048]{1,0:T(8,128)(2,1)S(1)}, u32[]{:S(2)}, u32[]{:S(2)}) %collective-permute-start.13) | collective-permute-done | bytes 524320 | tf_op jit(solution)/shard_map/ppermute | solution.py:67
  105.2 7.6 collective-permute-done.17.refs_3_
  144.2 19.1 %shard_map.298 = (bf16[512,2048]{1,0:T(8,128)(2,1)}, bf16[512,2048]{1,0:T(8,128)(2,1)}, bf16[1024,384]{1,0:T(8,128)(2,1)}, bf16[1024,128]{1,0:T(8,128)(2,1)}, f3...) custom-call(s32[68]{0:T(128)} %concatenate.124.place_ref, ...), custom_call_target="tpu_custom_call" | custom-call | flops 5368709120 | bytes 25294848 | tf_op jit(solution)/shard_map/pallas_call | solution.py:166
  165.0 16.1 %collective-permute-done.32 = bf16[2,2,64,528]{3,2,1,0:T(8,128)(2,1)S(1)} collective-permute-done((bf16[2,2,64,528]{3,2,1,0:T(8,128)(2,1)}, bf16[2,2,64,528]{3,2,1,0:T(8,128)(2,1)S(1)}, u32[]{:S(2)}, u32[]{:S(2)}) %collective-permute-start.32) | collective-permute-done | bytes 270368 | tf_op jit(solution)/shard_map/ppermute | solution.py:67
  208.0 9.6 %collective-permute-done.37 = bf16[128,2048]{1,0:T(8,128)(2,1)S(1)} collective-permute-done((bf16[128,2048]{1,0:T(8,128)(2,1)S(1)}, bf16[128,2048]{1,0:T(8,128)(2,1)S(1)}, u32[]{:S(2)}, u32[]{:S(2)}) %collective-permute-start.37) | collective-permute-done | bytes 524320 | tf_op jit(solution)/shard_map/ppermute | solution.py:67
  227.4 8.8 %collective-permute-done.40 = bf16[160,1408]{1,0:T(8,128)(2,1)S(1)} collective-permute-done((bf16[160,1408]{1,0:T(8,128)(2,1)S(1)}, bf16[160,1408]{1,0:T(8,128)(2,1)S(1)}, u32[]{:S(2)}, u32[]{:S(2)}) %collective-permute-start.40) | collective-permute-done | bytes 450592 | tf_op jit(solution)/shard_map/ppermute | solution.py:840
  257.0 14.1 %collective-permute-done.47.refs_2_ = bf16[128,2048]{1,0:T(8,128)(2,1)S(1)} collective-permute-done((bf16[128,2048]{1,0:T(8,128)(2,1)S(1)}, bf16[128,2048]{1,0:T(8,128)(2,1)S(1)}, u32[]{:S(2)}, u32[]{:S(2)}) %collective-permute-start.47) | collective-permute-done | bytes 524320 | tf_op jit(solution)/shard_map/ppermute | solution.py:67
  276.9 7.0 shard_map.300
  320.9 7.8 %collective-permute-done.58 = bf16[192,1408]{1,0:T(8,128)(2,1)S(1)} collective-permute-done((bf16[192,1408]{1,0:T(8,128)(2,1)}, bf16[192,1408]{1,0:T(8,128)(2,1)S(1)}, u32[]{:S(2)}, u32[]{:S(2)}) %collective-permute-start.58) | collective-permute-done | bytes 540704 | tf_op jit(solution)/shard_map/ppermute | solution.py:840
  338.9 15.2 %shard_map.303 = (bf16[2048,256]{1,0:T(8,128)(2,1)}, bf16[2048,512]{1,0:T(8,128)(2,1)}) custom-call(bf16[128,2048]{1,0:T(8,128)(2,1)} %copy-done.8, bf16[128,2048]{1,0:T(8,128)(2,1)} %copy-done.40, bf16[128,2048]{1,0:T(8,128)(2,1)} %copy-done.42, bf16[128,2048]{1,0:T(8,128)(2,1)} %copy-done.43, bf16[128,2048]{1,0:T(8,128)(2,1)} %collective-permute-done.45.refs_4_, ...), custom_call_target="tpu_custom_call" | custom-call | flops 6442450944 | bytes 23068672 | tf_op jit(solution)/shard_map/pallas_call | solution.py:166
  355.5 30.9 %shard_map.304 = (bf16[1024,1408]{1,0:T(8,128)(2,1)}, bf16[1024,1408]{1,0:T(8,128)(2,1)}, bf16[1024,1408]{1,0:T(8,128)(2,1)}, bf16[1408,1024]{1,0:T(8,128)(2,1)}) custom-call(bf16[1024,1024]{1,0:T(8,128)(2,1)} %get-tuple-element.913.x0_ref, bf16[1024,1024]{1,0:T(8,128)(2,1)} %get-tuple-element.890.x1_ref, bf16[1024,1024]{1,0:T(8,128)(2,1)} %get-tuple-element.893.r0_ref, ...), custom_call_target="tpu_custom_call" | custom-call | flops 20669530112 | bytes 37224448 | tf_op jit(solution)/shard_map/pallas_call | solution.py:668
  390.6 28.4 %shard_map.305 = (bf16[512,2048]{1,0:T(8,128)(2,1)}, bf16[512,2048]{1,0:T(8,128)(2,1)}, bf16[512,2048]{1,0:T(8,128)(2,1)}, bf16[512,2048]{1,0:T(8,128)(2,1)}) custom-call(bf16[1024,1408]{1,0:T(8,128)(2,1)} %get-tuple-element.905.dg_ref, bf16[1024,1408]{1,0:T(8,128)(2,1)} %get-tuple-element.914.du_ref, bf16[1024,1408]{1,0:T(8,128)(2,1)} %bitcast.220, ...), custom_call_target="tpu_custom_call" | custom-call | flops 17179869184 | bytes 29892608 | tf_op jit(solution)/shard_map/pallas_call | solution.py:668
  440.9 15.2 %shard_map.306 = bf16[2048,528]{1,0:T(8,128)(2,1)} custom-call(bf16[128,2048]{1,0:T(8,128)(2,1)} %copy-done.8, bf16[128,2048]{1,0:T(8,128)(2,1)} %copy-done.40, bf16[128,2048]{1,0:T(8,128)(2,1)} %copy-done.42, bf16[128,2048]{1,0:T(8,128)(2,1)} %copy-done.43, bf16[128,2048]{1,0:T(8,128)(2,1)} %collective-permute-done.45.refs_4_, ...), custom_call_target="tpu_custom_call" | custom-call | flops 6442450944 | bytes 22085632 | tf_op jit(solution)/shard_map/pallas_call | solution.py:166
  465.5 18.3 %shard_map.307 = (bf16[512,2048]{1,0:T(8,128)(2,1)}, bf16[512,2048]{1,0:T(8,128)(2,1)}, bf16[512,2048]{1,0:T(8,128)(2,1)}, bf16[512,2048]{1,0:T(8,128)(2,1)}) custom-call(bf16[1024,1408]{1,0:T(8,128)(2,1)} %get-tuple-element.892.act_ref, f32[1024,1]{1,0:T(8,128)} %get-tuple-element.868.share_ref, bf16[1408,1024]{1,0:T(8,128)(2,1)} %bitcast.218, ...), custom_call_target="tpu_custom_call" | custom-call | flops 9126805504 | bytes 19148800 | tf_op jit(solution)/shard_map/pallas_call | solution.py:668
  544.5 9.8 %collective-permute-done.82.refs_8_ = bf16[128,2048]{1,0:T(8,128)(2,1)S(1)} collective-permute-done((bf16[128,2048]{1,0:T(8,128)(2,1)S(1)}, bf16[128,2048]{1,0:T(8,128)(2,1)S(1)}, u32[]{:S(2)}, u32[]{:S(2)}) %collective-permute-start.82) | collective-permute-done | bytes 524320 | tf_op jit(solution)/shard_map/ppermute | solution.py:67
  563.6 9.3 %collective-permute-done.86.refs_9_ = bf16[128,2048]{1,0:T(8,128)(2,1)S(1)} collective-permute-done((bf16[128,2048]{1,0:T(8,128)(2,1)S(1)}, bf16[128,2048]{1,0:T(8,128)(2,1)S(1)}, u32[]{:S(2)}, u32[]{:S(2)}) %collective-permute-start.86) | collective-permute-done | bytes 524320 | tf_op jit(solution)/shard_map/ppermute | solution.py:67
  580.5 12.7 %collective-permute-done.88 = bf16[96,1408]{1,0:T(8,128)(2,1)S(1)} collective-permute-done((bf16[96,1408]{1,0:T(8,128)(2,1)S(1)}, bf16[96,1408]{1,0:T(8,128)(2,1)S(1)}, u32[]{:S(2)}, u32[]{:S(2)}) %collective-permute-start.88) | collective-permute-done | bytes 270368 | tf_op jit(solution)/shard_map/ppermute | solution.py:840
  601.4 30.7 %shard_map.308 = (bf16[1024,2048]{1,0:T(8,128)(2,1)}, bf16[16,128,768]{2,1,0:T(8,128)(2,1)}, bf16[2,16,64,640]{3,2,1,0:T(8,128)(2,1)}, bf16[16,128]{1,0:T(8,128)(2,1)}) custom-call(s32[68]{0:T(128)} %concatenate.124.place_ref, bf16[128,2048]{1,0:T(8,128)(2,1)} %refs_0_.1, bf16[128,2048]{1,0:T(8,128)(2,1)} %collective-permute-done.1.refs_1_, ...), custom_call_target="tpu_custom_call" | custom-call | flops 10737418240 | bytes 28964864 | tf_op jit(solution)/shard_map/pallas_call | solution.py:166
  641.1 6.9 convert_add_fusion.2
  650.5 8.6 %collective-permute-done.98 = bf16[4,128,768]{2,1,0:T(8,128)(2,1)S(1)} collective-permute-done((bf16[4,128,768]{2,1,0:T(8,128)(2,1)S(1)}, bf16[4,128,768]{2,1,0:T(8,128)(2,1)S(1)}, u32[]{:S(2)}, u32[]{:S(2)}) %collective-permute-start.98) | collective-permute-done | bytes 786464 | tf_op jit(solution)/shard_map/ppermute | solution.py:67
  673.7 6.9 collective-permute-done.102
  680.6 12.7 %collective-permute-done.106 = bf16[128,2048]{1,0:T(8,128)(2,1)S(1)} collective-permute-done((bf16[128,2048]{1,0:T(8,128)(2,1)}, bf16[128,2048]{1,0:T(8,128)(2,1)S(1)}, u32[]{:S(2)}, u32[]{:S(2)}) %collective-permute-start.106) | collective-permute-done | bytes 524320 | tf_op jit(solution)/shard_map/ppermute | solution.py:67
  (686 shorter events, 419.0 us)
Async XLA Ops:
  7.2 737.4 %reduce-scatter.2.cloned.1.call-start = ((), (), s32[]{:S(2)}) async-start(), calls=%async_computation.1 | async-start | bytes 4718592 | tf_op jit(solution)/shard_map/reduce_scatter | solution.py:1163
  37.3 27.2 %collective-permute-start.5 = (bf16[576,1024]{1,0:T(8,128)(2,1)}, bf16[576,1024]{1,0:T(8,128)(2,1)S(1)}, u32[]{:S(2)}, u32[]{:S(2)}) collective-permute-start(bf16[576,1024]{1,0:T(8,128)(2,1)} %slice_bitcast_fusion.1), channel_id=1, source_target_pairs={{0,16},{16,0},{1,17},{17,1},{2,18},{18,2},{3,19},{19,3},{4,20},{20... | collective-permute-start | bytes 3538952 | tf_op jit(solution)/shard_map/ppermute | solution.py:840
  38.9 24.8 %collective-permute-start.9 = (bf16[4,2,64,528]{3,2,1,0:T(8,128)(2,1)}, bf16[4,2,64,528]{3,2,1,0:T(8,128)(2,1)}, u32[]{:S(2)}, u32[]{:S(2)}) collective-permute-start(bf16[4,2,64,528]{3,2,1,0:T(8,128)(2,1)} %get-tuple-element.542), channel_id=1, source_target_pairs={{0,2},{1,3},{2,0},{3,1},{4,6},{5,7},{6,4},{7,5},{8,10},{9,11},{10,... | collective-permute-start | bytes 1622024 | tf_op jit(solution)/shard_map/ppermute | solution.py:67
  41.1 22.5 %collective-permute-start.6 = (bf16[128,1152]{1,0:T(8,128)(2,1)}, bf16[128,1152]{1,0:T(8,128)(2,1)S(1)}, u32[]{:S(2)}, u32[]{:S(2)}) collective-permute-start(bf16[128,1152]{1,0:T(8,128)(2,1)} %get-tuple-element.539), channel_id=1, source_target_pairs={{0,8},{1,9},{2,10},{3,11},{4,12},{5,13},{6,14},{7,15},{8,0},{9,1},... | collective-permute-start | bytes 884744 | tf_op jit(solution)/shard_map/ppermute | solution.py:67
  65.7 27.8 %collective-permute-start.10 = (bf16[4,128,1152]{2,1,0:T(8,128)(2,1)S(1)}, bf16[4,128,1152]{2,1,0:T(8,128)(2,1)S(1)}, u32[]{:S(2)}, u32[]{:S(2)}) collective-permute-start(bf16[4,128,1152]{2,1,0:T(8,128)(2,1)S(1)} %pad_maximum_fusion.10.refs_6_.refs_0_), channel_id=1, source_target_pairs={{0,2},{1,3},{2,0},{3,1},{4,6},{5,7},{6,4},{7,5},{8,10},{9,11},{10,... | collective-permute-start | bytes 3538952 | tf_op jit(solution)/shard_map/ppermute | solution.py:67
  67.2 26.3 %collective-permute-start.11 = (bf16[4,128,1152]{2,1,0:T(8,128)(2,1)S(1)}, bf16[4,128,1152]{2,1,0:T(8,128)(2,1)S(1)}, u32[]{:S(2)}, u32[]{:S(2)}) collective-permute-start(bf16[4,128,1152]{2,1,0:T(8,128)(2,1)S(1)} %pad_maximum_fusion.10.refs_6_.refs_0_), channel_id=1, source_target_pairs={{0,16},{16,0},{1,17},{17,1},{2,18},{18,2},{3,19},{19,3},{4,20},{20... | collective-permute-start | bytes 3538952 | tf_op jit(solution)/shard_map/ppermute | solution.py:840
  134.8 28.9 %collective-permute-start.27 = (bf16[128,2048]{1,0:T(8,128)(2,1)S(1)}, bf16[128,2048]{1,0:T(8,128)(2,1)S(1)}, u32[]{:S(2)}, u32[]{:S(2)}) collective-permute-start(bf16[128,2048]{1,0:T(8,128)(2,1)S(1)} %fusion.9.refs_0_.refs_13_), channel_id=1, source_target_pairs={{0,2},{1,3},{2,0},{3,1},{4,6},{5,7},{6,4},{7,5},{8,10},{9,11},{10,... | collective-permute-start | bytes 1572872 | tf_op jit(solution)/shard_map/ppermute | solution.py:67
  135.4 28.2 %collective-permute-start.28 = (bf16[128,2048]{1,0:T(8,128)(2,1)S(1)}, bf16[128,2048]{1,0:T(8,128)(2,1)S(1)}, u32[]{:S(2)}, u32[]{:S(2)}) collective-permute-start(bf16[128,2048]{1,0:T(8,128)(2,1)S(1)} %collective-permute-done.13.refs_1_.refs_14_), channel_id=1, source_target_pairs={{0,4},{1,5},{2,6},{3,7},{4,8},{5,9},{6,10},{7,11},{8,12},{9,13},{1... | collective-permute-start | bytes 1572872 | tf_op jit(solution)/shard_map/ppermute | solution.py:67
  136.0 27.7 %collective-permute-start.29 = (bf16[128,2048]{1,0:T(8,128)(2,1)S(1)}, bf16[128,2048]{1,0:T(8,128)(2,1)S(1)}, u32[]{:S(2)}, u32[]{:S(2)}) collective-permute-start(bf16[128,2048]{1,0:T(8,128)(2,1)S(1)} %fusion.9.refs_0_.refs_13_), channel_id=1, source_target_pairs={{0,12},{1,13},{2,14},{3,15},{4,0},{5,1},{6,2},{7,3},{8,4},{9,5},{1... | collective-permute-start | bytes 1572872 | tf_op jit(solution)/shard_map/ppermute | solution.py:67
  139.7 24.0 %collective-permute-start.26 = (bf16[224,1408]{1,0:T(8,128)(2,1)}, bf16[224,1408]{1,0:T(8,128)(2,1)}, u32[]{:S(2)}, u32[]{:S(2)}) collective-permute-start(bf16[224,1408]{1,0:T(8,128)(2,1)} %get-tuple-element.579), channel_id=1, source_target_pairs={{0,16},{16,0},{1,17},{17,1},{2,18},{18,2},{3,19},{19,3},{4,20},{20... | collective-permute-start | bytes 1892360 | tf_op jit(solution)/shard_map/ppermute | solution.py:840
  329.5 24.9 %collective-permute-start.61 = (bf16[384,1408]{1,0:T(8,128)(2,1)S(1)}, bf16[384,1408]{1,0:T(8,128)(2,1)S(1)}, u32[]{:S(2)}, u32[]{:S(2)}) collective-permute-start(bf16[384,1408]{1,0:T(8,128)(2,1)S(1)} %slice_bitcast_fusion.2), channel_id=1, source_target_pairs={{0,16},{16,0},{1,17},{17,1},{2,18},{18,2},{3,19},{19,3},{4,20},{20... | collective-permute-start | bytes 3244040 | tf_op jit(solution)/shard_map/ppermute | solution.py:840
  389.6 32.2 %collective-permute-start.62 = (bf16[704,1024]{1,0:T(8,128)(2,1)S(1)}, bf16[704,1024]{1,0:T(8,128)(2,1)S(1)}, u32[]{:S(2)}, u32[]{:S(2)}) collective-permute-start(bf16[704,1024]{1,0:T(8,128)(2,1)S(1)} %slice.435), channel_id=1, source_target_pairs={{0,16},{16,0},{1,17},{17,1},{2,18},{18,2},{3,19},{19,3},{4,20},{20... | collective-permute-start | bytes 4325384 | tf_op jit(solution)/shard_map/ppermute | solution.py:840
  459.2 24.8 %collective-permute-start.68 = (bf16[192,1024]{1,0:T(8,128)(2,1)}, bf16[192,1024]{1,0:T(8,128)(2,1)S(1)}, u32[]{:S(2)}, u32[]{:S(2)}) collective-permute-start(bf16[192,1024]{1,0:T(8,128)(2,1)} %slice.433), channel_id=1, source_target_pairs={{0,16},{16,0},{1,17},{17,1},{2,18},{18,2},{3,19},{19,3},{4,20},{20... | collective-permute-start | bytes 1179656 | tf_op jit(solution)/shard_map/ppermute | solution.py:840
  460.2 23.8 %collective-permute-start.70 = (bf16[128,2048]{1,0:T(8,128)(2,1)}, bf16[128,2048]{1,0:T(8,128)(2,1)}, u32[]{:S(2)}, u32[]{:S(2)}) collective-permute-start(bf16[128,2048]{1,0:T(8,128)(2,1)} %get-tuple-element.865), channel_id=1, source_target_pairs={{0,2},{1,3},{2,0},{3,1},{4,6},{5,7},{6,4},{7,5},{8,10},{9,11},{10,... | collective-permute-start | bytes 1572872 | tf_op jit(solution)/shard_map/ppermute | solution.py:67
  461.0 23.0 %collective-permute-start.71 = (bf16[128,2048]{1,0:T(8,128)(2,1)}, bf16[128,2048]{1,0:T(8,128)(2,1)}, u32[]{:S(2)}, u32[]{:S(2)}) collective-permute-start(bf16[128,2048]{1,0:T(8,128)(2,1)} %add_convert_fusion.11), channel_id=1, source_target_pairs={{0,12},{1,13},{2,14},{3,15},{4,0},{5,1},{6,2},{7,3},{8,4},{9,5},{1... | collective-permute-start | bytes 1572872 | tf_op jit(solution)/shard_map/ppermute | solution.py:67
  527.4 31.8 %collective-permute-start.84 = (bf16[512,1408]{1,0:T(8,128)(2,1)S(1)}, bf16[512,1408]{1,0:T(8,128)(2,1)S(1)}, u32[]{:S(2)}, u32[]{:S(2)}) collective-permute-start(bf16[512,1408]{1,0:T(8,128)(2,1)S(1)} %slice.512), channel_id=1, source_target_pairs={{0,16},{16,0},{1,17},{17,1},{2,18},{18,2},{3,19},{19,3},{4,20},{20... | collective-permute-start | bytes 4325384 | tf_op jit(solution)/shard_map/ppermute | solution.py:840
  595.0 37.1 %collective-permute-start.93 = (bf16[576,1408]{1,0:T(8,128)(2,1)}, bf16[576,1408]{1,0:T(8,128)(2,1)}, u32[]{:S(2)}, u32[]{:S(2)}) collective-permute-start(bf16[576,1408]{1,0:T(8,128)(2,1)} %slice.507), channel_id=1, source_target_pairs={{0,16},{16,0},{1,17},{17,1},{2,18},{18,2},{3,19},{19,3},{4,20},{20... | collective-permute-start | bytes 4866056 | tf_op jit(solution)/shard_map/ppermute | solution.py:840
  596.5 35.6 %collective-permute-start.94 = (bf16[2,2,64,528]{3,2,1,0:T(8,128)(2,1)}, bf16[2,2,64,528]{3,2,1,0:T(8,128)(2,1)}, u32[]{:S(2)}, u32[]{:S(2)}) collective-permute-start(bf16[2,2,64,528]{3,2,1,0:T(8,128)(2,1)} %get-tuple-element.941), channel_id=1, source_target_pairs={{0,8},{1,9},{2,10},{3,11},{4,12},{5,13},{6,14},{7,15},{8,0},{9,1},... | collective-permute-start | bytes 811016 | tf_op jit(solution)/shard_map/ppermute | solution.py:67
  597.3 34.8 %collective-permute-start.95 = (bf16[2,2,64,528]{3,2,1,0:T(8,128)(2,1)}, bf16[2,2,64,528]{3,2,1,0:T(8,128)(2,1)}, u32[]{:S(2)}, u32[]{:S(2)}) collective-permute-start(bf16[2,2,64,528]{3,2,1,0:T(8,128)(2,1)} %get-tuple-element.942), channel_id=1, source_target_pairs={{0,4},{1,5},{2,6},{3,7},{4,8},{5,9},{6,10},{7,11},{8,12},{9,13},{1... | collective-permute-start | bytes 811016 | tf_op jit(solution)/shard_map/ppermute | solution.py:67
  597.7 34.4 %collective-permute-start.96 = (bf16[2,2,64,528]{3,2,1,0:T(8,128)(2,1)}, bf16[2,2,64,528]{3,2,1,0:T(8,128)(2,1)}, u32[]{:S(2)}, u32[]{:S(2)}) collective-permute-start(bf16[2,2,64,528]{3,2,1,0:T(8,128)(2,1)} %get-tuple-element.943), channel_id=1, source_target_pairs={{0,12},{1,13},{2,14},{3,15},{4,0},{5,1},{6,2},{7,3},{8,4},{9,5},{1... | collective-permute-start | bytes 811016 | tf_op jit(solution)/shard_map/ppermute | solution.py:67
  601.1 31.0 %collective-permute-start.97 = (bf16[128,2048]{1,0:T(8,128)(2,1)S(1)}, bf16[128,2048]{1,0:T(8,128)(2,1)}, u32[]{:S(2)}, u32[]{:S(2)}) collective-permute-start(bf16[128,2048]{1,0:T(8,128)(2,1)S(1)} %add_convert_fusion.2), channel_id=1, source_target_pairs={{0,12},{1,13},{2,14},{3,15},{4,0},{5,1},{6,2},{7,3},{8,4},{9,5},{1... | collective-permute-start | bytes 1572872 | tf_op jit(solution)/shard_map/ppermute | solution.py:67
  663.8 29.6 %collective-permute-start.106 = (bf16[128,2048]{1,0:T(8,128)(2,1)}, bf16[128,2048]{1,0:T(8,128)(2,1)S(1)}, u32[]{:S(2)}, u32[]{:S(2)}) collective-permute-start(bf16[128,2048]{1,0:T(8,128)(2,1)} %add_convert_fusion.1), channel_id=1, source_target_pairs={{0,12},{1,13},{2,14},{3,15},{4,0},{5,1},{6,2},{7,3},{8,4},{9,5},{1... | collective-permute-start | bytes 1572872 | tf_op jit(solution)/shard_map/ppermute | solution.py:67
  665.5 27.9 %collective-permute-start.105 = (bf16[2,4,64,640]{3,2,1,0:T(8,128)(2,1)S(1)}, bf16[2,4,64,640]{3,2,1,0:T(8,128)(2,1)S(1)}, u32[]{:S(2)}, u32[]{:S(2)}) collective-permute-start(bf16[2,4,64,640]{3,2,1,0:T(8,128)(2,1)S(1)} %fusion.14), channel_id=1, source_target_pairs={{0,2},{1,3},{2,0},{3,1},{4,6},{5,7},{6,4},{7,5},{8,10},{9,11},{10,... | collective-permute-start | bytes 1966088 | tf_op jit(solution)/shard_map/ppermute | solution.py:67
  698.0 22.6 %collective-permute-start.107 = (bf16[160,1408]{1,0:T(8,128)(2,1)}, bf16[160,1408]{1,0:T(8,128)(2,1)}, u32[]{:S(2)}, u32[]{:S(2)}) collective-permute-start(bf16[160,1408]{1,0:T(8,128)(2,1)} %get-tuple-element.1011), channel_id=1, source_target_pairs={{0,16},{16,0},{1,17},{17,1},{2,18},{18,2},{3,19},{19,3},{4,20},{20... | collective-permute-start | bytes 1351688 | tf_op jit(solution)/shard_map/ppermute | solution.py:840
  (237 other events, 3283.7 us)
Sparse Core Ops, SparseCore 0:
  632.3 63.9 reduce-scatter.1
